TPU v7x, 32 devices: a whole 2x2x4 slice. The times are simulated.
32 devices in a mesh: dp: 2 (over y), expert: 16 (over z, x, core).
Axes of the slice: x: 2, y: 2, z: 4, core: 2. Of those that a mesh axis runs over, the one named last changes fastest.
Arguments:
- tokens: bfloat16 [12288, 1280], P(('dp', 'expert')), may hold values from -6 to 6
- lengths: int32 [32, 4], P(('dp', 'expert')), may hold values from 1 to 288, 384 in all within a row
- routes: int32 [12288, 6], P(('dp', 'expert')), may hold values from 0 to 15, all different within a row; in each aligned block of 384 rows (0 to 383, 384 to 767, ...) at most 184 rows name the same one
- cotangent: bfloat16 [12288, 1280], P(('dp', 'expert')), may hold values from -6 to 6
- norm_gains: float32 [2, 1280], P(None, ('dp', 'expert')), may hold values from 0.5 to 1.5
- gains_m: float32 [2, 1280], P(None, ('dp', 'expert')), as said below
- gains_v: float32 [2, 1280], P(None, ('dp', 'expert')), as said below
- w_qkv: float32 [1280, 3840], P(('dp', 'expert')), may hold values from -0.15625 to 0.15625
- m_qkv: float32 [1280, 3840], P(('dp', 'expert')), as said below
- v_qkv: float32 [1280, 3840], P(('dp', 'expert')), as said below
- w_out: float32 [1280, 1280], P(('dp', 'expert')), may hold values from -1.25 to 1.25
- m_out: float32 [1280, 1280], P(('dp', 'expert')), as said below
- v_out: float32 [1280, 1280], P(('dp', 'expert')), as said below
- w_shared_in: float32 [1280, 1792], P(('dp', 'expert')), may hold values from -0.15625 to 0.15625
- m_shared_in: float32 [1280, 1792], P(('dp', 'expert')), as said below
- v_shared_in: float32 [1280, 1792], P(('dp', 'expert')), as said below
- w_shared_down: float32 [896, 1280], P(('dp', 'expert')), may hold values from -0.1875 to 0.1875
- m_shared_down: float32 [896, 1280], P(('dp', 'expert')), as said below
- v_shared_down: float32 [896, 1280], P(('dp', 'expert')), as said below
- w_router: float32 [1280, 16], P(('dp', 'expert')), may hold values from -0.078125 to 0.078125
- m_router: float32 [1280, 16], P(('dp', 'expert')), as said below
- v_router: float32 [1280, 16], P(('dp', 'expert')), as said below
- w_expert_in: float32 [16, 1280, 1792], P('expert', 'dp'), may hold values from -0.15625 to 0.15625
- m_expert_in: float32 [16, 1280, 1792], P('expert', 'dp'), as said below
- v_expert_in: float32 [16, 1280, 1792], P('expert', 'dp'), as said below
- w_expert_down: float32 [16, 896, 1280], P('expert', 'dp'), may hold values from -1.5 to 1.5
- m_expert_down: float32 [16, 896, 1280], P('expert', 'dp'), as said below
- v_expert_down: float32 [16, 896, 1280], P('expert', 'dp'), as said below
Outputs:
- mixed: bfloat16 [12288, 1280], P(('dp', 'expert'))
- input_grad: float32 [12288, 1280], P(('dp', 'expert'))
- gains_new: float32 [2, 1280], P(None, ('dp', 'expert'))
- gains_m_new: float32 [2, 1280], P(None, ('dp', 'expert'))
- gains_v_new: float32 [2, 1280], P(None, ('dp', 'expert'))
- w_qkv_new: float32 [1280, 3840], P(('dp', 'expert'))
- m_qkv_new: float32 [1280, 3840], P(('dp', 'expert'))
- v_qkv_new: float32 [1280, 3840], P(('dp', 'expert'))
- w_out_new: float32 [1280, 1280], P(('dp', 'expert'))
- m_out_new: float32 [1280, 1280], P(('dp', 'expert'))
- v_out_new: float32 [1280, 1280], P(('dp', 'expert'))
- w_shared_in_new: float32 [1280, 1792], P(('dp', 'expert'))
- m_shared_in_new: float32 [1280, 1792], P(('dp', 'expert'))
- v_shared_in_new: float32 [1280, 1792], P(('dp', 'expert'))
- w_shared_down_new: float32 [896, 1280], P(('dp', 'expert'))
- m_shared_down_new: float32 [896, 1280], P(('dp', 'expert'))
- v_shared_down_new: float32 [896, 1280], P(('dp', 'expert'))
- w_router_new: float32 [1280, 16], P(('dp', 'expert'))
- m_router_new: float32 [1280, 16], P(('dp', 'expert'))
- v_router_new: float32 [1280, 16], P(('dp', 'expert'))
- w_expert_in_new: float32 [16, 1280, 1792], P('expert', 'dp')
- m_expert_in_new: float32 [16, 1280, 1792], P('expert', 'dp')
- v_expert_in_new: float32 [16, 1280, 1792], P('expert', 'dp')
- w_expert_down_new: float32 [16, 896, 1280], P('expert', 'dp')
- m_expert_down_new: float32 [16, 896, 1280], P('expert', 'dp')
- v_expert_down_new: float32 [16, 896, 1280], P('expert', 'dp')
- grad_norm: float32 [], replicated
Inputs may be any that keep to these rules, and one draw needn't show every extreme that they name: `lengths`: each row sums to 384, and its largest entry is 288. `routes`: each token names 6 different experts; of one device's tokens at most 184 name one expert, and exactly 184 in some device's tokens. `gains_m`: first moments of both signs. `gains_v`: positive. `m_qkv`: first moments of both signs. `v_qkv`: positive. `m_out`: first moments of both signs. `v_out`: positive. `m_shared_in`: first moments of both signs. `v_shared_in`: positive. `m_shared_down`: first moments of both signs. `v_shared_down`: positive. `m_router`: first moments of both signs. `v_router`: positive. `m_expert_in`: first moments of both signs. `v_expert_in`: positive. `m_expert_down`: first moments of both signs. `v_expert_down`: positive.
All inputs are finite; a program needn't handle non-finite values.
Results may differ from a plain program's by a relative error of at most 0.014.
Values may be sent and summed in bfloat16 or wider, within the bound.
A program may use at most 320 MiB of HBM per device.

v0:
```python
import jax
import jax.numpy as jnp
from jax import lax
from jax.sharding import PartitionSpec as P

D = 1280
H = 10
HD = 128
FF = 896
TOP = 6
ADAM_STEP = 5


EPS = 1e-06
ROPE_BASE = 10000.0
BETA_ONE = 0.9
BETA_TWO = 0.95
ADAM_EPS = 1e-08
DECAY = 0.1
CLIP = 1.0
GAIN_RATE = 0.5
NEGATIVE = -1e30


def rms_scale(values):
    return lax.rsqrt(jnp.mean(values * values, axis=-1, keepdims=True) + EPS)


def rotary_tables(seq_lengths, row_count, head_width):
    position = jnp.arange(row_count, dtype=jnp.int32)
    seq_ends = jnp.cumsum(seq_lengths)
    segment = jnp.sum((position[:, None] >= seq_ends[None, :]).astype(jnp.int32), axis=1)
    starts = seq_ends - seq_lengths
    slot_ids = jnp.arange(seq_lengths.shape[0], dtype=jnp.int32)
    first_row = jnp.sum(
        jnp.where(segment[:, None] == slot_ids[None, :], starts[None, :], 0), axis=1
    )
    seq_place = (position - first_row).astype(jnp.float32)
    inv_freq = ROPE_BASE ** (-jnp.arange(head_width // 2, dtype=jnp.float32) * 2.0 / head_width)
    phase_angle = seq_place[:, None] * inv_freq[None, :]
    cosine = jnp.concatenate([jnp.cos(phase_angle), jnp.cos(phase_angle)], axis=1)
    sine_table = jnp.concatenate([jnp.sin(phase_angle), jnp.sin(phase_angle)], axis=1)
    allowed = (segment[:, None] == segment[None, :]) & (position[None, :] <= position[:, None])
    return (cosine, sine_table, allowed)


def rotate(vectors, cosine, sine_table):
    half_width = vectors.shape[-1] // 2
    turned = jnp.concatenate([-vectors[..., half_width:], vectors[..., :half_width]], axis=-1)
    return vectors * cosine[:, None, :] + turned * sine_table[:, None, :]


def rotate_back(gradient, cosine, sine_table):
    half_width = gradient.shape[-1] // 2
    scaled_sine = gradient * sine_table[:, None, :]
    turned = jnp.concatenate(
        [scaled_sine[..., half_width:], -scaled_sine[..., :half_width]], axis=-1
    )
    return gradient * cosine[:, None, :] + turned


def silu_slope(gate_vals):
    logistic = jax.nn.sigmoid(gate_vals)
    return logistic * (1.0 + gate_vals * (1.0 - logistic))


def swiglu_back(act_grad, gate_up):
    gate_part = gate_up[:, :FF]
    up_part = gate_up[:, FF:]
    return jnp.concatenate(
        [act_grad * up_part * silu_slope(gate_part), act_grad * jax.nn.silu(gate_part)], axis=1
    ).astype(jnp.bfloat16)


def adam_update(weight, first_moment, second_moment, gradient, factor, step_rate, decay_rate):
    clipped = gradient * factor
    first_new = BETA_ONE * first_moment + (1.0 - BETA_ONE) * clipped
    second_new = BETA_TWO * second_moment + (1.0 - BETA_TWO) * clipped * clipped
    first_hat = first_new / (1.0 - BETA_ONE**ADAM_STEP)
    second_hat = second_new / (1.0 - BETA_TWO**ADAM_STEP)
    weight_new = weight - step_rate * (
        first_hat / (jnp.sqrt(second_hat) + ADAM_EPS) + decay_rate * weight
    )
    return (weight_new, first_new, second_new)


def local(
    tokens,
    lengths,
    routes,
    cotangent,
    norm_gains,
    gains_m,
    gains_v,
    w_qkv,
    m_qkv,
    v_qkv,
    w_out,
    m_out,
    v_out,
    w_shared_in,
    m_shared_in,
    v_shared_in,
    w_shared_down,
    m_shared_down,
    v_shared_down,
    w_router,
    m_router,
    v_router,
    w_expert_in,
    m_expert_in,
    v_expert_in,
    w_expert_down,
    m_expert_down,
    v_expert_down,
):
    row_count = tokens.shape[0]
    expert_count = w_router.shape[1]
    capacity = min(row_count, (5 * row_count * TOP // (4 * expert_count) + 7) // 8 * 8)
    score_scale = HD ** (-0.5)
    qkv_full, out_full, shin_full, shdown_full, router_full, gain_full = (
        lax.all_gather(w_qkv.astype(jnp.bfloat16), ("dp", "expert"), axis=0, tiled=True),
        lax.all_gather(w_out.astype(jnp.bfloat16), ("dp", "expert"), axis=0, tiled=True),
        lax.all_gather(w_shared_in.astype(jnp.bfloat16), ("dp", "expert"), axis=0, tiled=True),
        lax.all_gather(w_shared_down.astype(jnp.bfloat16), ("dp", "expert"), axis=0, tiled=True),
        lax.all_gather(w_router.astype(jnp.bfloat16), ("dp", "expert"), axis=0, tiled=True),
        lax.all_gather(norm_gains.astype(jnp.bfloat16), ("dp", "expert"), axis=1, tiled=True),
    )
    expert_in_all, expert_down_all = (
        lax.all_gather(w_expert_in.astype(jnp.bfloat16), "dp", axis=1, tiled=True),
        lax.all_gather(w_expert_down.astype(jnp.bfloat16), "dp", axis=1, tiled=True),
    )
    expert_in_full = expert_in_all[0]
    expert_down_full = expert_down_all[0]
    inputs = tokens.astype(jnp.float32)
    gain_one = gain_full[0].astype(jnp.float32)
    gain_two = gain_full[1].astype(jnp.float32)
    cosine, sine_table, allowed = rotary_tables(lengths[0], row_count, HD)
    scale_one = rms_scale(inputs)
    normed_one = inputs * scale_one
    attn_in = (normed_one * gain_one).astype(jnp.bfloat16)
    projected = jnp.dot(attn_in, qkv_full, preferred_element_type=jnp.float32).reshape(
        row_count, 3, H, HD
    )
    queries = rotate(projected[:, 0], cosine, sine_table).astype(jnp.bfloat16)
    keys_rot = rotate(projected[:, 1], cosine, sine_table).astype(jnp.bfloat16)
    values_low = projected[:, 2].astype(jnp.bfloat16)

    def masked_scores():
        raw_scores = (
            jnp.einsum("qhd,khd->hqk", queries, keys_rot, preferred_element_type=jnp.float32)
            * score_scale
        )
        return jnp.where(allowed[None], raw_scores, NEGATIVE)

    scores = masked_scores()
    row_max = jnp.max(scores, axis=-1, keepdims=True)
    log_total = row_max + jnp.log(jnp.sum(jnp.exp(scores - row_max), axis=-1, keepdims=True))
    probs_attn = jnp.exp(scores - log_total)
    mixed_heads = jnp.einsum(
        "hqk,khd->qhd",
        probs_attn.astype(jnp.bfloat16),
        values_low,
        preferred_element_type=jnp.float32,
    )
    heads_low = mixed_heads.astype(jnp.bfloat16).reshape(row_count, H * HD)
    residual = inputs + jnp.dot(heads_low, out_full, preferred_element_type=jnp.float32)
    scale_two = rms_scale(residual)
    normed_two = residual * scale_two
    mlp_in = (normed_two * gain_two).astype(jnp.bfloat16)
    logits = jnp.dot(mlp_in, router_full, preferred_element_type=jnp.float32)
    router_probs = jax.nn.softmax(logits, axis=-1)
    expert_ids = jnp.arange(expert_count, dtype=jnp.int32)
    onehot_tok = routes[:, :, None] == expert_ids[None, None, :]
    gates = jnp.sum(jnp.where(onehot_tok, router_probs[:, None, :], 0.0), axis=2)
    shared_gu = jnp.dot(mlp_in, shin_full, preferred_element_type=jnp.float32)
    shared_act = (jax.nn.silu(shared_gu[:, :FF]) * shared_gu[:, FF:]).astype(jnp.bfloat16)
    shared_out = jnp.dot(shared_act, shdown_full, preferred_element_type=jnp.float32)
    flat_routes = routes.reshape(-1)
    onehot_route = (flat_routes[:, None] == expert_ids[None, :]).astype(jnp.int32)
    slot_rank = jnp.sum((jnp.cumsum(onehot_route, axis=0) - 1) * onehot_route, axis=1)
    target = flat_routes * capacity + slot_rank
    slot_owner = (
        jnp.full((expert_count * capacity,), row_count * TOP, jnp.int32)
        .at[target]
        .set(jnp.arange(row_count * TOP, dtype=jnp.int32))
    )
    padded_in = jnp.concatenate([mlp_in, jnp.zeros((1, D), jnp.bfloat16)], axis=0)
    send_rows = padded_in[slot_owner // TOP].reshape(expert_count, capacity, D)
    received = lax.all_to_all(send_rows, "expert", split_axis=0, concat_axis=0, tiled=True)
    flat_in = received.reshape(-1, D)
    gate_up = jnp.dot(flat_in, expert_in_full, preferred_element_type=jnp.float32)
    activation = (jax.nn.silu(gate_up[:, :FF]) * gate_up[:, FF:]).astype(jnp.bfloat16)
    result = jnp.dot(activation, expert_down_full, preferred_element_type=jnp.float32).astype(
        jnp.bfloat16
    )
    result = result.reshape(received.shape)
    returned = lax.all_to_all(result, "expert", split_axis=0, concat_axis=0, tiled=True)
    returned_rows = returned.reshape(expert_count * capacity, D)[target].reshape(row_count, TOP, D)
    routed = jnp.sum(gates[:, :, None] * returned_rows, axis=1)
    mixed = (residual + shared_out + routed).astype(jnp.bfloat16)
    out_grad = cotangent.astype(jnp.float32)
    grad_shdown = jnp.einsum("tf,td->fd", shared_act, cotangent, preferred_element_type=jnp.float32)
    shared_act_grad = jnp.einsum(
        "td,fd->tf", cotangent, shdown_full, preferred_element_type=jnp.float32
    )
    shared_gu_grad = swiglu_back(shared_act_grad, shared_gu)
    grad_shin = jnp.einsum("td,tf->df", mlp_in, shared_gu_grad, preferred_element_type=jnp.float32)
    gate_grad = jnp.sum(out_grad[:, None, :] * returned_rows, axis=2)
    route_grad = (
        (gates[:, :, None] * out_grad[:, None, :]).astype(jnp.bfloat16).reshape(row_count * TOP, D)
    )
    padded_grad = jnp.concatenate([route_grad, jnp.zeros((1, D), jnp.bfloat16)], axis=0)
    send_grad = padded_grad[slot_owner].reshape(expert_count, capacity, D)
    expert_grad = lax.all_to_all(send_grad, "expert", split_axis=0, concat_axis=0, tiled=True)
    flat_rows = received.reshape(-1, D)
    gate_up_again = gate_up.reshape(received.shape[0], received.shape[1], 2 * FF).reshape(
        -1, 2 * FF
    )
    grad_rows = expert_grad.reshape(-1, D)
    act_again = (jax.nn.silu(gate_up_again[:, :FF]) * gate_up_again[:, FF:]).astype(jnp.bfloat16)
    grad_edown = jnp.einsum("rf,rd->fd", act_again, grad_rows, preferred_element_type=jnp.float32)
    expert_act_grad = jnp.einsum(
        "rd,fd->rf", grad_rows, expert_down_full, preferred_element_type=jnp.float32
    )
    expert_gu_grad = swiglu_back(expert_act_grad, gate_up_again)
    grad_ein = jnp.einsum(
        "rd,rf->df", flat_rows, expert_gu_grad, preferred_element_type=jnp.float32
    )
    input_back = jnp.einsum(
        "rf,df->rd", expert_gu_grad, expert_in_full, preferred_element_type=jnp.float32
    )
    input_back = input_back.astype(jnp.bfloat16).reshape(received.shape)
    back_rows = lax.all_to_all(input_back, "expert", split_axis=0, concat_axis=0, tiled=True)
    routed_back = jnp.sum(
        back_rows.reshape(expert_count * capacity, D)[target].reshape(row_count, TOP, D),
        axis=1,
        dtype=jnp.float32,
    )
    prob_grad = jnp.sum(jnp.where(onehot_tok, gate_grad[:, :, None], 0.0), axis=1)
    logit_grad = (
        router_probs * (prob_grad - jnp.sum(prob_grad * router_probs, axis=-1, keepdims=True))
    ).astype(jnp.bfloat16)
    grad_router = jnp.einsum("td,te->de", mlp_in, logit_grad, preferred_element_type=jnp.float32)
    mlp_in_grad = routed_back + jnp.einsum(
        "te,de->td", logit_grad, router_full, preferred_element_type=jnp.float32
    )
    mlp_in_grad = mlp_in_grad + jnp.einsum(
        "tf,df->td", shared_gu_grad, shin_full, preferred_element_type=jnp.float32
    )
    grad_gain_two = jnp.sum(mlp_in_grad * normed_two, axis=0)
    scaled_two = mlp_in_grad * gain_two
    resid_grad = out_grad + scale_two * (
        scaled_two - normed_two * jnp.mean(scaled_two * normed_two, axis=-1, keepdims=True)
    )
    resid_low = resid_grad.astype(jnp.bfloat16)
    grad_out = jnp.einsum("ti,td->id", heads_low, resid_low, preferred_element_type=jnp.float32)
    heads_grad = jnp.einsum("td,id->ti", resid_low, out_full, preferred_element_type=jnp.float32)
    heads_grad = heads_grad.astype(jnp.bfloat16).reshape(row_count, H, HD)
    probs_again = jnp.exp(masked_scores() - log_total)
    attn_prob_grad = jnp.einsum(
        "qhd,khd->hqk", heads_grad, values_low, preferred_element_type=jnp.float32
    )
    value_grad = jnp.einsum(
        "hqk,qhd->khd",
        probs_again.astype(jnp.bfloat16),
        heads_grad,
        preferred_element_type=jnp.float32,
    )
    score_grad = probs_again * (
        attn_prob_grad - jnp.sum(attn_prob_grad * probs_again, axis=-1, keepdims=True)
    )
    score_grad = score_grad.astype(jnp.bfloat16)
    query_grad = (
        jnp.einsum("hqk,khd->qhd", score_grad, keys_rot, preferred_element_type=jnp.float32)
        * score_scale
    )
    key_grad = (
        jnp.einsum("hqk,qhd->khd", score_grad, queries, preferred_element_type=jnp.float32)
        * score_scale
    )
    projected_grad = jnp.stack(
        [
            rotate_back(query_grad, cosine, sine_table),
            rotate_back(key_grad, cosine, sine_table),
            value_grad,
        ],
        axis=1,
    )
    projected_grad = projected_grad.reshape(row_count, 3 * H * HD).astype(jnp.bfloat16)
    grad_qkv = jnp.einsum("td,tk->dk", attn_in, projected_grad, preferred_element_type=jnp.float32)
    attn_grad = jnp.einsum(
        "tk,dk->td", projected_grad, qkv_full, preferred_element_type=jnp.float32
    )
    grad_gain_one = jnp.sum(attn_grad * normed_one, axis=0)
    scaled_one = attn_grad * gain_one
    input_grad = resid_grad + scale_one * (
        scaled_one - normed_one * jnp.mean(scaled_one * normed_one, axis=-1, keepdims=True)
    )
    grad_gains = jnp.stack([grad_gain_one, grad_gain_two], axis=0)
    dense_owned = (
        lax.psum_scatter(grad_gains, ("dp", "expert"), scatter_dimension=1, tiled=True),
        lax.psum_scatter(grad_qkv, ("dp", "expert"), scatter_dimension=0, tiled=True),
        lax.psum_scatter(grad_out, ("dp", "expert"), scatter_dimension=0, tiled=True),
        lax.psum_scatter(grad_shin, ("dp", "expert"), scatter_dimension=0, tiled=True),
        lax.psum_scatter(grad_shdown, ("dp", "expert"), scatter_dimension=0, tiled=True),
        lax.psum_scatter(grad_router, ("dp", "expert"), scatter_dimension=0, tiled=True),
    )
    expert_owned = (
        lax.psum_scatter(
            grad_ein[None].astype(jnp.bfloat16), "dp", scatter_dimension=1, tiled=True
        ).astype(jnp.float32),
        lax.psum_scatter(
            grad_edown[None].astype(jnp.bfloat16), "dp", scatter_dimension=1, tiled=True
        ).astype(jnp.float32),
    )
    owned_grads = tuple(dense_owned) + tuple(expert_owned)
    squares = sum((jnp.sum(grad_part * grad_part) for grad_part in owned_grads))
    total_squares = lax.psum(squares, ("dp", "expert"))
    grad_norm = jnp.sqrt(total_squares)
    factor = jnp.minimum(1.0, CLIP / grad_norm)
    weights = (
        norm_gains,
        w_qkv,
        w_out,
        w_shared_in,
        w_shared_down,
        w_router,
        w_expert_in,
        w_expert_down,
    )
    firsts = (
        gains_m,
        m_qkv,
        m_out,
        m_shared_in,
        m_shared_down,
        m_router,
        m_expert_in,
        m_expert_down,
    )
    seconds = (
        gains_v,
        v_qkv,
        v_out,
        v_shared_in,
        v_shared_down,
        v_router,
        v_expert_in,
        v_expert_down,
    )
    rates = (
        GAIN_RATE,
        D ** (-0.5),
        (H * HD // 64) ** (-0.5),
        D ** (-0.5),
        FF ** (-0.5),
        (4 * D) ** (-0.5),
        D ** (-0.5),
        (FF // 64) ** (-0.5),
    )
    decays = (0.0, DECAY, DECAY, DECAY, DECAY, DECAY, DECAY, DECAY)
    updated = []
    for weight, first_moment, second_moment, gradient, step_rate, decay_rate in zip(
        weights, firsts, seconds, owned_grads, rates, decays
    ):
        updated.extend(
            adam_update(
                weight, first_moment, second_moment, gradient, factor, step_rate, decay_rate
            )
        )
    return (
        mixed,
        input_grad,
        updated[0],
        updated[1],
        updated[2],
        updated[3],
        updated[4],
        updated[5],
        updated[6],
        updated[7],
        updated[8],
        updated[9],
        updated[10],
        updated[11],
        updated[12],
        updated[13],
        updated[14],
        updated[15],
        updated[16],
        updated[17],
        updated[18],
        updated[19],
        updated[20],
        updated[21],
        updated[22],
        updated[23],
        grad_norm,
    )


def solution(mesh):
    placed = (
        P(("dp", "expert"), None),
        P(("dp", "expert"), None),
        P(("dp", "expert"), None),
        P(("dp", "expert"), None),
        P(None, ("dp", "expert")),
        P(None, ("dp", "expert")),
        P(None, ("dp", "expert")),
        P(("dp", "expert"), None),
        P(("dp", "expert"), None),
        P(("dp", "expert"), None),
        P(("dp", "expert"), None),
        P(("dp", "expert"), None),
        P(("dp", "expert"), None),
        P(("dp", "expert"), None),
        P(("dp", "expert"), None),
        P(("dp", "expert"), None),
        P(("dp", "expert"), None),
        P(("dp", "expert"), None),
        P(("dp", "expert"), None),
        P(("dp", "expert"), None),
        P(("dp", "expert"), None),
        P(("dp", "expert"), None),
        P("expert", "dp", None),
        P("expert", "dp", None),
        P("expert", "dp", None),
        P("expert", "dp", None),
        P("expert", "dp", None),
        P("expert", "dp", None),
    )
    return jax.shard_map(
        local,
        mesh=mesh,
        in_specs=placed,
        out_specs=(
            P(("dp", "expert"), None),
            P(("dp", "expert"), None),
            P(None, ("dp", "expert")),
            P(None, ("dp", "expert")),
            P(None, ("dp", "expert")),
            P(("dp", "expert"), None),
            P(("dp", "expert"), None),
            P(("dp", "expert"), None),
            P(("dp", "expert"), None),
            P(("dp", "expert"), None),
            P(("dp", "expert"), None),
            P(("dp", "expert"), None),
            P(("dp", "expert"), None),
            P(("dp", "expert"), None),
            P(("dp", "expert"), None),
            P(("dp", "expert"), None),
            P(("dp", "expert"), None),
            P(("dp", "expert"), None),
            P(("dp", "expert"), None),
            P(("dp", "expert"), None),
            P("expert", "dp", None),
            P("expert", "dp", None),
            P("expert", "dp", None),
            P("expert", "dp", None),
            P("expert", "dp", None),
            P("expert", "dp", None),
            P(),
        ),
        check_vma=False,
    )
```

profile of v0, /device:TPU:0, one launch (start us, length us, event | category | flops | bytes accessed | tf_op | source)
XLA Modules:
  0.0 1642.1 jit_solution(17787732313109211255)
XLA Ops:
  18.8 43.1 %all-gather = bf16[32,40,2]{1,2,0:T(2,128)(2,1)S(1)} all-gather(bf16[1,40,2]{1,2,0:T(2,128)(2,1)S(1)} %convert_bitcast_fusion.2), channel_id=1, replica_groups=mesh['dp'=2,'expert'=16] {'dp','expert'}, dimensions={0}, use_global_device_ids=true | all-gather | bytes 5280 | tf_op jit(solution)/shard_map/all_gather | solution.py:127
  74.1 24.0 %all-gather.10.cloned.1.call-done = bf16[1280,3840]{1,0:T(8,128)(2,1)} async-done(((bf16[40,3840]{1,0:T(8,128)(2,1)}), bf16[1280,3840]{1,0:T(8,128)(2,1)}) %all-gather.10.cloned.1.call-update) | async-done | bytes 9830416 | tf_op jit(solution)/shard_map/all_gather | solution.py:122
  114.3 45.2 %all-gather.12.cloned.1.call-done = bf16[1280,1280]{1,0:T(8,128)(2,1)} async-done(((bf16[40,1280]{1,0:T(8,128)(2,1)}), bf16[1280,1280]{1,0:T(8,128)(2,1)}) %all-gather.12.cloned.1.call-update) | async-done | bytes 3276816 | tf_op jit(solution)/shard_map/all_gather | solution.py:123
  164.6 10.7 gather_fusion
  182.0 203.3 %all-gather.2 = bf16[32,40,16]{1,2,0:T(8,128)(2,1)S(1)} all-gather(bf16[1,40,16]{1,2,0:T(8,128)(2,1)S(1)} %convert_bitcast_fusion.1), channel_id=1, replica_groups=mesh['dp'=2,'expert'=16] {'dp','expert'}, dimensions={0}, use_global_device_ids=true | all-gather | bytes 42240 | tf_op jit(solution)/shard_map/all_gather | solution.py:126
  392.0 14.0 mul.678
  420.6 20.0 %gather_fusion.2 = bf16[2944,1280]{1,0:T(8,128)(2,1)} fusion(bf16[2305,1280]{1,0:T(8,128)(2,1)} %concatenate.37, s32[3072]{0:T(1024)S(1)} %get-tuple-element.104), kind=kCustom, calls=%fused_computation.2 | custom fusion | bytes 15085056 | tf_op jit(solution)/shard_map/gather | solution.py:214
  470.9 40.9 %all-gather.16.cloned.1.call-done = bf16[1,1280,1792]{2,1,0:T(8,128)(2,1)} async-done(((bf16[1,640,1792]{2,1,0:T(8,128)(2,1)}), bf16[1,1280,1792]{2,1,0:T(8,128)(2,1)}) %all-gather.16.cloned.1.call-update) | async-done | bytes 4587536 | tf_op jit(solution)/shard_map/all_gather | solution.py:130
  511.8 20.7 %fusion.8 = f32[2944,1792]{0,1:T(8,128)} fusion(bf16[2944,1280]{1,0:T(8,128)(2,1)} %bitcast.17, bf16[1,1280,1792]{2,1,0:T(8,128)(2,1)} %all-gather.16.cloned.1.call-done), kind=kOutput, calls=%fused_computation.31 | convolution fusion | flops 13505658880 | bytes 33226752 | tf_op jit(solution)/shard_map/dot_general | solution.py:192
  532.5 16.6 %all-gather.18.cloned.1.call-done = bf16[1,896,1280]{2,1,0:T(8,128)(2,1)} async-done(((bf16[1,448,1280]{2,1,0:T(8,128)(2,1)}), bf16[1,896,1280]{2,1,0:T(8,128)(2,1)}) %all-gather.18.cloned.1.call-update) | async-done | bytes 2293776 | tf_op jit(solution)/shard_map/all_gather | solution.py:131
  549.1 37.8 %all-to-all-done.2 = bf16[16,184,1280]{2,1,0:T(8,128)(2,1)} async-done(((bf16[16,184,1280]{2,1,0:T(8,128)(2,1)}), bf16[16,184,1280]{2,1,0:T(8,128)(2,1)}, u32[]{:S(2)}, u32[]{:S(2)}) %all-to-all-start.2) | async-done | bytes 7536672 | tf_op jit(solution)/shard_map/all_to_all | solution.py:215
  586.9 22.5 %multiply_convert_fusion.2 = (bf16[2944,896]{0,1:T(8,128)(2,1)}, bf16[2944,896]{0,1:T(8,128)(2,1)}, bf16[2944,896]{0,1:T(8,128)(2,1)}) fusion(f32[2944,1792]{0,1:T(8,128)} %fusion.8, bf16[2944,1280]{1,0:T(8,128)(2,1)} %bitcast.23, bf16[1,896,1280]{2,1,0:T(8,128)(2,1)} %all-gather.18.cloned.1.call-done), kind=kOutput, calls=%fused_computation.12 | convolution fusion | flops 6792396800 | bytes 46759936 | tf_op jit(solution)/shard_map/rd,fd->rf/dot_general | solution.py:223
  609.4 12.8 convolution_convert_fusion.1
  622.1 45.1 %all-to-all-start.1 = ((bf16[16,184,1280]{2,1,0:T(8,128)(2,1)}), bf16[16,184,1280]{2,1,0:T(8,128)(2,1)}, u32[]{:S(2)}, u32[]{:S(2)}) async-start(bf16[16,184,1280]{2,1,0:T(8,128)(2,1)} %bitcast.156), calls=%async_computation.1 | async-start | bytes 15073280 | tf_op jit(solution)/shard_map/all_to_all | solution.py:198
  667.2 20.6 %convolution_convert_fusion = bf16[2944,1280]{1,0:T(8,128)(2,1)} fusion(bf16[2944,896]{0,1:T(8,128)(2,1)} %get-tuple-element.60, bf16[2944,896]{0,1:T(8,128)(2,1)} %get-tuple-element.59, bf16[1,1280,1792]{2,1,0:T(8,128)(2,1)} %all-gather.16.cloned.1.call-done), kind=kOutput, calls=%fused_computation.8 | convolution fusion | flops 13530529792 | bytes 22675456 | tf_op jit(solution)/shard_map/rf,df->rd/dot_general | solution.py:230
  687.8 135.8 %all-to-all-done.1 = bf16[16,184,1280]{2,1,0:T(8,128)(2,1)} async-done(((bf16[16,184,1280]{2,1,0:T(8,128)(2,1)}), bf16[16,184,1280]{2,1,0:T(8,128)(2,1)}, u32[]{:S(2)}, u32[]{:S(2)}) %all-to-all-start.1) | async-done | bytes 7536672 | tf_op jit(solution)/shard_map/all_to_all | solution.py:198
  823.6 32.3 %all-to-all-start.3 = ((bf16[16,184,1280]{2,1,0:T(8,128)(2,1)}), bf16[16,184,1280]{2,1,0:T(8,128)(2,1)}, u32[]{:S(2)}, u32[]{:S(2)}) async-start(bf16[16,184,1280]{2,1,0:T(8,128)(2,1)} %bitcast.155), calls=%async_computation.3 | async-start | bytes 15073280 | tf_op jit(solution)/shard_map/all_to_all | solution.py:234
  855.9 12.4 fusion.12
  868.4 21.4 %fusion.2 = bf16[1,1280,1792]{2,1,0:T(8,128)(2,1)} fusion(bf16[2944,1280]{1,0:T(8,128)(2,1)} %bitcast.17, bf16[2944,896]{0,1:T(8,128)(2,1)} %get-tuple-element.60, bf16[2944,896]{0,1:T(8,128)(2,1)} %get-tuple-element.59), kind=kOutput, calls=%fused_computation.18 | convolution fusion | flops 13529055232 | bytes 22675456 | tf_op jit(solution)/shard_map/rd,rf->df/dot_general | solution.py:227
  897.1 17.1 %gather_fusion.1 = bf16[2304,1280]{1,0:T(8,128)(2,1)} fusion(bf16[2944,1280]{1,0:T(8,128)(2,1)} %bitcast.21, s32[3072]{0:T(1024)S(1)} %pad_clamp_fusion.1), kind=kCustom, calls=%fused_computation.1 | custom fusion | bytes 11805696 | tf_op jit(solution)/shard_map/gather | solution.py:199
  914.2 11.1 reshape.284
  925.4 10.8 multiply_reduce_fusion
  936.3 55.5 %all-to-all-done.3 = bf16[16,184,1280]{2,1,0:T(8,128)(2,1)} async-done(((bf16[16,184,1280]{2,1,0:T(8,128)(2,1)}), bf16[16,184,1280]{2,1,0:T(8,128)(2,1)}, u32[]{:S(2)}, u32[]{:S(2)}) %all-to-all-start.3) | async-done | bytes 7536672 | tf_op jit(solution)/shard_map/all_to_all | solution.py:234
  991.7 16.9 %gather_fusion.3 = bf16[2304,1280]{1,0:T(8,128)(2,1)} fusion(bf16[2944,1280]{1,0:T(8,128)(2,1)} %bitcast.25, s32[3072]{0:T(1024)S(1)} %pad_clamp_fusion.1), kind=kCustom, calls=%fused_computation.3 | custom fusion | bytes 11805696 | tf_op jit(solution)/shard_map/gather | solution.py:236
  1008.7 11.2 reshape.285
  1020.0 11.5 reduce_sum.246
  1084.8 110.7 %fusion = f32[32,1280]{1,0:T(8,128)S(1)} fusion(f32[896,1280]{1,0:T(8,128)} %fusion.97), kind=kCustom, calls=%all-reduce-scatter | all-reduce-scatter fusion | flops 1310721 | bytes 4751360
  1223.7 10.5 fusion.32
  1234.3 53.0 %all-reduce.2 = f32[2,1280]{1,0:T(2,128)S(1)} all-reduce(f32[2,1280]{1,0:T(2,128)S(1)} %pad_maximum_fusion.11), channel_id=2, replica_groups=mesh['dp'=2,'expert'=16] {'dp','expert'}, use_global_device_ids=true, to_apply=%region_24.25.clone | all-reduce | flops 2560 | bytes 20480
  1293.3 45.9 %reduce-scatter.12.cloned.1.call-done = f32[40,1280]{1,0:T(8,128)} async-done(((f32[1280,1280]{1,0:T(8,128)}), f32[40,1280]{1,0:T(8,128)}) %reduce-scatter.12.cloned.1.call-update) | async-done | bytes 204816 | tf_op jit(solution)/shard_map/reduce_scatter | solution.py:304
  1340.8 217.2 %reduce-scatter.10.cloned.1.call-done = f32[40,3840]{1,0:T(8,128)} async-done(((f32[1280,3840]{1,0:T(8,128)}), f32[40,3840]{1,0:T(8,128)}) %reduce-scatter.10.cloned.1.call-update) | async-done | bytes 614416 | tf_op jit(solution)/shard_map/reduce_scatter | solution.py:303
  1569.8 39.4 %psum.7 = f32[]{:T(128)} all-reduce(f32[]{:T(128)S(6)} %add.307), channel_id=1, replica_groups=mesh['dp'=2,'expert'=16] {'dp','expert'}, use_global_device_ids=true, to_apply=%region_40.41 | all-reduce | flops 1 | bytes 8 | tf_op jit(solution)/shard_map/psum | solution.py:319
  (314 shorter events, 229.4 us)
Async XLA Ops:
  7.2 54.9 %copy-start.73 = (s32[1,4]{1,0:T(1,128)S(1)}, s32[1,4]{1,0:T(1,128)}, u32[]{:S(2)}) copy-start(s32[1,4]{1,0:T(1,128)} %param.29) | copy-start | bytes 52
  7.2 66.5 %copy-start.9 = (bf16[384,1280]{1,0:T(8,128)(2,1)S(1)}, bf16[384,1280]{1,0:T(8,128)(2,1)}, u32[]{:S(2)}) copy-start(bf16[384,1280]{1,0:T(8,128)(2,1)} %param.28) | copy-start | bytes 2949124
  7.2 90.9 %all-gather.10.cloned.1.call-start = ((), (), s32[]{:S(2)}) async-start(), calls=%async_computation.9 | async-start | bytes 10137600 | tf_op jit(solution)/shard_map/all_gather | solution.py:122
  9.2 150.3 %all-gather.12.cloned.1.call-start = ((), (), s32[]{:S(2)}) async-start(), calls=%async_computation.10 | async-start | bytes 3379200 | tf_op jit(solution)/shard_map/all_gather | solution.py:123
  72.3 90.7 %copy-start.53 = (f32[1280]{0:T(1024)}, f32[1280]{0:T(1024)S(1)}, u32[]{:S(2)}) copy-start(f32[1280]{0:T(1024)S(1)} %get-tuple-element.33) | copy-start | bytes 15364
  74.1 36.5 %copy-start.20 = (pred[384,384]{0,1:T(8,128)(4,1)}, pred[384,384]{0,1:T(8,128)(4,1)S(1)}, u32[]{:S(2)}) copy-start(pred[384,384]{0,1:T(8,128)(4,1)S(1)} %fusion.48) | copy-start | bytes 442372
  114.3 48.7 %copy-start.24 = (bf16[10,128,384]{2,1,0:T(8,128)(2,1)}, bf16[10,128,384]{2,1,0:T(8,128)(2,1)S(1)}, u32[]{:S(2)}) copy-start(bf16[10,128,384]{2,1,0:T(8,128)(2,1)S(1)} %convolution_convert_fusion.6) | copy-start | bytes 2949124
  164.5 299.2 %copy-start.3 = (bf16[384,1280]{1,0:T(8,128)(2,1)}, bf16[384,1280]{1,0:T(8,128)(2,1)S(1)}, u32[]{:S(2)}) copy-start(bf16[384,1280]{1,0:T(8,128)(2,1)S(1)} %multiply_convert_fusion.5) | copy-start | bytes 2949124
  175.4 210.1 %copy-start.6 = (bf16[384,1280]{1,0:T(8,128)(2,1)S(1)}, bf16[384,1280]{1,0:T(8,128)(2,1)}, u32[]{:S(2)}) copy-start(bf16[384,1280]{1,0:T(8,128)(2,1)} %param.31) | copy-start | bytes 2949124
  175.4 265.1 %all-to-all-start = ((bf16[16,184,1280]{2,1,0:T(8,128)(2,1)}), bf16[16,184,1280]{2,1,0:T(8,128)(2,1)}, u32[]{:S(2)}, u32[]{:S(2)}) async-start(bf16[16,184,1280]{2,1,0:T(8,128)(2,1)} %bitcast.146), calls=%async_computation | async-start | bytes 15073280 | tf_op jit(solution)/shard_map/all_to_all | solution.py:190
  180.5 271.7 %all-gather.20.cloned.1.call-start = ((), (), s32[]{:S(2)}) async-start(), calls=%async_computation.19 | async-start | bytes 2703360 | tf_op jit(solution)/shard_map/all_gather | solution.py:125
  181.2 275.0 %all-gather.14.cloned.1.call-start = ((), (), s32[]{:S(2)}) async-start(), calls=%async_computation.11 | async-start | bytes 4730880 | tf_op jit(solution)/shard_map/all_gather | solution.py:124
  440.5 146.4 %all-to-all-start.2 = ((bf16[16,184,1280]{2,1,0:T(8,128)(2,1)}), bf16[16,184,1280]{2,1,0:T(8,128)(2,1)}, u32[]{:S(2)}, u32[]{:S(2)}) async-start(bf16[16,184,1280]{2,1,0:T(8,128)(2,1)} %bitcast.145), calls=%async_computation.2 | async-start | bytes 15073280 | tf_op jit(solution)/shard_map/all_to_all | solution.py:215
  445.2 66.5 %all-gather.16.cloned.1.call-start = ((), (), s32[]{:S(2)}) async-start(), calls=%async_computation.12 | async-start | bytes 6881280 | tf_op jit(solution)/shard_map/all_gather | solution.py:130
  449.2 99.9 %all-gather.18.cloned.1.call-start = ((), (), s32[]{:S(2)}) async-start(), calls=%async_computation.13 | async-start | bytes 3440640 | tf_op jit(solution)/shard_map/all_gather | solution.py:131
  452.1 764.1 %reduce-scatter.14.cloned.1.call-start = ((), (), s32[]{:S(2)}) async-start(), calls=%async_computation.16 | async-start | bytes 9461760 | tf_op jit(solution)/shard_map/reduce_scatter | solution.py:305
  622.1 201.5 %all-to-all-start.1 = ((bf16[16,184,1280]{2,1,0:T(8,128)(2,1)}), bf16[16,184,1280]{2,1,0:T(8,128)(2,1)}, u32[]{:S(2)}, u32[]{:S(2)}) async-start(bf16[16,184,1280]{2,1,0:T(8,128)(2,1)} %bitcast.156), calls=%async_computation.1 | async-start | bytes 15073280 | tf_op jit(solution)/shard_map/all_to_all | solution.py:198
  823.6 168.2 %all-to-all-start.3 = ((bf16[16,184,1280]{2,1,0:T(8,128)(2,1)}), bf16[16,184,1280]{2,1,0:T(8,128)(2,1)}, u32[]{:S(2)}, u32[]{:S(2)}) async-start(bf16[16,184,1280]{2,1,0:T(8,128)(2,1)} %bitcast.155), calls=%async_computation.3 | async-start | bytes 15073280 | tf_op jit(solution)/shard_map/all_to_all | solution.py:234
  855.9 362.0 %reduce-scatter.18.cloned.1.call-start = ((), (), s32[]{:S(2)}) async-start(), calls=%async_computation.18 | async-start | bytes 3440640 | tf_op jit(solution)/shard_map/reduce_scatter | solution.py:313
  868.3 352.0 %reduce-scatter.16.cloned.1.call-start = ((), (), s32[]{:S(2)}) async-start(), calls=%async_computation.17 | async-start | bytes 6881280 | tf_op jit(solution)/shard_map/reduce_scatter | solution.py:310
  889.8 402.1 %all-reduce.8.cloned.1.call-start = ((), (), s32[]{:S(2)}) async-start(), calls=%async_computation.20 | async-start | bytes 163840
  1040.2 299.0 %reduce-scatter.12.cloned.1.call-start = ((), (), s32[]{:S(2)}) async-start(), calls=%async_computation.15 | async-start | bytes 6758400 | tf_op jit(solution)/shard_map/reduce_scatter | solution.py:304
  1046.8 511.2 %reduce-scatter.10.cloned.1.call-start = ((), (), s32[]{:S(2)}) async-start(), calls=%async_computation.14 | async-start | bytes 20275200 | tf_op jit(solution)/shard_map/reduce_scatter | solution.py:303
  1195.5 9.8 collective-permute-start
  1196.9 8.4 collective-permute-start.1
  1198.3 8.5 collective-permute-start.2
  1200.9 4.4 collective-permute-start.3
  1565.1 46.9 %copy-start.69 = (f32[2,40]{1,0:T(2,128)S(1)}, f32[2,40]{1,0:T(2,128)}, u32[]{:S(2)}) copy-start(f32[2,40]{1,0:T(2,128)} %param.32) | copy-start | bytes 964
  1565.1 46.9 %copy-start.70 = (f32[2,40]{1,0:T(2,128)S(1)}, f32[2,40]{1,0:T(2,128)}, u32[]{:S(2)}) copy-start(f32[2,40]{1,0:T(2,128)} %param.33) | copy-start | bytes 964
  1565.1 46.9 %copy-start.71 = (f32[2,40]{1,0:T(2,128)S(1)}, f32[2,40]{1,0:T(2,128)}, u32[]{:S(2)}) copy-start(f32[2,40]{1,0:T(2,128)} %param.34) | copy-start | bytes 964
  1565.1 47.6 %copy-start.18 = (bf16[1,448,1280]{2,1,0:T(8,128)(2,1)S(1)}, bf16[1,448,1280]{2,1,0:T(8,128)(2,1)}, u32[]{:S(2)}) copy-start(bf16[1,448,1280]{2,1,0:T(8,128)(2,1)} %reduce-scatter.18.cloned.1.call-done) | copy-start | bytes 3440644
  1565.1 54.8 %slice-start.2 = ((s8[4587520]{0:T(1024)(128)(4,1)}), s8[393216]{0:T(1024)(128)(4,1)S(1)}, s32[]{:S(2)}) async-start(s8[4587520]{0:T(1024)(128)(4,1)} %bitcast.147), calls=%async_computation.23 | async-start | bytes 786432
  (66 other events, 531.0 us)
Sparse Core Ops, SparseCore 0:
  11.5 86.5 all-gather.9
  101.5 57.8 all-gather.11
  184.8 154.8 all-gather.19
  343.0 72.7 all-gather.13
  449.3 62.3 all-gather.15
  513.8 35.3 all-gather.17
  551.4 227.9 reduce-scatter.13
  868.5 34.4 reduce-scatter.17
  906.0 58.5 reduce-scatter.15
  1040.3 148.0 all-reduce.7
  1190.7 148.4 reduce-scatter.11
  1345.5 212.4 reduce-scatter.9
where the time goes:
time: 1650 us; the launch traced here: 1640 us
  waiting for transfers between devices  623 us (38%)
  blocking collectives  450 us (27%)
  matrix products  200 us (12%)
  local copies, waits for them, and re-layouts  151 us (9%)
  other arithmetic  102 us (6%)
  starting transfers between devices  94.2 us (6%)
  between operations  22.7 us (1%)
    reduce_scatter x1, waiting for transfers between devices, local(): lax.psum_scatter(grad_qkv, ('dp', 'expert'), scatter_dimension=0, tiled=T...  217 us
    all_gather x1, blocking collectives, local(): lax.all_gather(w_router.astype(jnp.bfloat16), ('dp', 'expert'), axis=0, t...  203 us
    unnamed x2, blocking collectives  164 us
    all_to_all x1, waiting for transfers between devices, local(): lax.all_to_all(result, 'expert', split_axis=0, concat_axis=0, tiled=True)  136 us
    all_to_all x1, waiting for transfers between devices, local(): lax.all_to_all(input_back, 'expert', split_axis=0, concat_axis=0, tiled=T...  55.5 us
    reduce_scatter x1, waiting for transfers between devices, local(): lax.psum_scatter(grad_out, ('dp', 'expert'), scatter_dimension=0, tiled=T...  45.9 us
    all_gather x1, waiting for transfers between devices, local(): lax.all_gather(w_out.astype(jnp.bfloat16), ('dp', 'expert'), axis=0, tile...  45.2 us
    all_to_all x1, starting transfers between devices, local(): lax.all_to_all(result, 'expert', split_axis=0, concat_axis=0, tiled=True)  45.1 us
  transfers between devices with their start and end apart: 20, of which 11 were waited for; matrix products, arithmetic and copies ran while one was open for 31% of the time, Pallas kernels for 0%

commit v1 on v0

v1 whole, which is shorter than its diff:
```python
import jax
import jax.numpy as jnp
from jax import lax
from jax.sharding import PartitionSpec as P

D = 1280
H = 10
HD = 128
FF = 896
TOP = 6
ADAM_STEP = 5


EPS = 1e-06
ROPE_BASE = 10000.0
BETA_ONE = 0.9
BETA_TWO = 0.95
ADAM_EPS = 1e-08
DECAY = 0.1
CLIP = 1.0
GAIN_RATE = 0.5
NEGATIVE = -1e30


def rms_scale(values):
    return lax.rsqrt(jnp.mean(values * values, axis=-1, keepdims=True) + EPS)


def rotary_tables(seq_lengths, row_count, head_width):
    position = jnp.arange(row_count, dtype=jnp.int32)
    seq_ends = jnp.cumsum(seq_lengths)
    segment = jnp.sum((position[:, None] >= seq_ends[None, :]).astype(jnp.int32), axis=1)
    starts = seq_ends - seq_lengths
    slot_ids = jnp.arange(seq_lengths.shape[0], dtype=jnp.int32)
    first_row = jnp.sum(
        jnp.where(segment[:, None] == slot_ids[None, :], starts[None, :], 0), axis=1
    )
    seq_place = (position - first_row).astype(jnp.float32)
    inv_freq = ROPE_BASE ** (-jnp.arange(head_width // 2, dtype=jnp.float32) * 2.0 / head_width)
    phase_angle = seq_place[:, None] * inv_freq[None, :]
    cosine = jnp.concatenate([jnp.cos(phase_angle), jnp.cos(phase_angle)], axis=1)
    sine_table = jnp.concatenate([jnp.sin(phase_angle), jnp.sin(phase_angle)], axis=1)
    allowed = (segment[:, None] == segment[None, :]) & (position[None, :] <= position[:, None])
    return (cosine, sine_table, allowed)


def rotate(vectors, cosine, sine_table):
    half_width = vectors.shape[-1] // 2
    turned = jnp.concatenate([-vectors[..., half_width:], vectors[..., :half_width]], axis=-1)
    return vectors * cosine[:, None, :] + turned * sine_table[:, None, :]


def rotate_back(gradient, cosine, sine_table):
    half_width = gradient.shape[-1] // 2
    scaled_sine = gradient * sine_table[:, None, :]
    turned = jnp.concatenate(
        [scaled_sine[..., half_width:], -scaled_sine[..., :half_width]], axis=-1
    )
    return gradient * cosine[:, None, :] + turned


def silu_slope(gate_vals):
    logistic = jax.nn.sigmoid(gate_vals)
    return logistic * (1.0 + gate_vals * (1.0 - logistic))


def swiglu_back(act_grad, gate_up):
    gate_part = gate_up[:, :FF]
    up_part = gate_up[:, FF:]
    return jnp.concatenate(
        [act_grad * up_part * silu_slope(gate_part), act_grad * jax.nn.silu(gate_part)], axis=1
    ).astype(jnp.bfloat16)


def adam_update(weight, first_moment, second_moment, gradient, factor, step_rate, decay_rate):
    clipped = gradient * factor
    first_new = BETA_ONE * first_moment + (1.0 - BETA_ONE) * clipped
    second_new = BETA_TWO * second_moment + (1.0 - BETA_TWO) * clipped * clipped
    first_hat = first_new / (1.0 - BETA_ONE**ADAM_STEP)
    second_hat = second_new / (1.0 - BETA_TWO**ADAM_STEP)
    weight_new = weight - step_rate * (
        first_hat / (jnp.sqrt(second_hat) + ADAM_EPS) + decay_rate * weight
    )
    return (weight_new, first_new, second_new)


def local(
    tokens,
    lengths,
    routes,
    cotangent,
    norm_gains,
    gains_m,
    gains_v,
    w_qkv,
    m_qkv,
    v_qkv,
    w_out,
    m_out,
    v_out,
    w_shared_in,
    m_shared_in,
    v_shared_in,
    w_shared_down,
    m_shared_down,
    v_shared_down,
    w_router,
    m_router,
    v_router,
    w_expert_in,
    m_expert_in,
    v_expert_in,
    w_expert_down,
    m_expert_down,
    v_expert_down,
):
    both = ("dp", "expert")
    low = jnp.bfloat16
    wide = jnp.float32
    row_count = tokens.shape[0]
    expert_count = w_router.shape[1]
    n_dp = lax.axis_size("dp")
    n_exp = lax.axis_size("expert")
    n_all = n_dp * n_exp
    capacity = min(row_count, (5 * row_count * TOP // (4 * expert_count) + 7) // 8 * 8)
    score_scale = HD ** (-0.5)
    rows_w = w_qkv.shape[0]
    unit = w_shared_down.shape[0]
    my_expert = lax.axis_index("expert")

    small = jnp.concatenate([w_router, norm_gains.T], axis=1).astype(low)
    qkv_full = lax.all_gather(w_qkv.astype(low), both, axis=0, tiled=True)
    small_full = lax.all_gather(small, both, axis=0, tiled=True)
    out_full = lax.all_gather(w_out.astype(low), both, axis=0, tiled=True)
    router_full = small_full[:, :expert_count]
    gain_one = small_full[:, expert_count].astype(wide)
    gain_two = small_full[:, expert_count + 1].astype(wide)
    cot_all = lax.all_gather(cotangent, "expert", axis=0, tiled=False)
    routes_all = lax.all_gather(routes, "expert", axis=0, tiled=False)
    expert_in_full = lax.all_gather(w_expert_in[0].astype(low), "dp", axis=0, tiled=True)
    expert_down_full = lax.all_gather(w_expert_down[0].astype(low), "dp", axis=0, tiled=True)
    shin_send = (
        w_shared_in.astype(low)
        .reshape(rows_w, 2, n_dp, n_exp, unit)
        .transpose(3, 0, 1, 2, 4)
        .reshape(n_exp, rows_w, 2 * n_dp * unit)
    )
    shin_send = jnp.concatenate([shin_send] * n_dp, axis=0)
    shin_mine = lax.all_to_all(shin_send, both, 0, 0, tiled=True).reshape(D, 2 * n_dp * unit)
    shdown_mine = lax.all_gather(w_shared_down.astype(low), "dp", axis=0, tiled=True)
    half = n_dp * unit

    inputs = tokens.astype(wide)
    cosine, sine_table, allowed = rotary_tables(lengths[0], row_count, HD)
    scale_one = rms_scale(inputs)
    normed_one = inputs * scale_one
    attn_in = (normed_one * gain_one).astype(low)
    projected = jnp.dot(attn_in, qkv_full, preferred_element_type=wide).reshape(
        row_count, 3, H, HD
    )
    queries = rotate(projected[:, 0], cosine, sine_table).astype(low)
    keys_rot = rotate(projected[:, 1], cosine, sine_table).astype(low)
    values_low = projected[:, 2].astype(low)
    raw_scores = (
        jnp.einsum("qhd,khd->hqk", queries, keys_rot, preferred_element_type=wide) * score_scale
    )
    scores = jnp.where(allowed[None], raw_scores, NEGATIVE)
    row_max = jnp.max(scores, axis=-1, keepdims=True)
    exped = jnp.exp(scores - row_max)
    probs_attn = exped / jnp.sum(exped, axis=-1, keepdims=True)
    probs_low = probs_attn.astype(low)
    mixed_heads = jnp.einsum("hqk,khd->qhd", probs_low, values_low, preferred_element_type=wide)
    heads_low = mixed_heads.astype(low).reshape(row_count, H * HD)
    residual = inputs + jnp.dot(heads_low, out_full, preferred_element_type=wide)
    scale_two = rms_scale(residual)
    normed_two = residual * scale_two
    mlp_in = (normed_two * gain_two).astype(low)
    logits = jnp.dot(mlp_in, router_full, preferred_element_type=wide)
    router_probs = jax.nn.softmax(logits, axis=-1)

    mlp_all = lax.all_gather(mlp_in, "expert", axis=0, tiled=False)
    mlp_flat = mlp_all.reshape(n_exp * row_count, D)
    fused_w = jnp.concatenate([shin_mine, router_full], axis=1)
    fused = jnp.dot(mlp_flat, fused_w, preferred_element_type=wide)
    shared_gate = fused[:, :half]
    shared_up = fused[:, half : 2 * half]
    probs_all = jax.nn.softmax(fused[:, 2 * half :], axis=-1)
    expert_ids = jnp.arange(expert_count, dtype=jnp.int32)
    my_prob = jnp.sum(jnp.where(expert_ids[None, :] == my_expert, probs_all, 0.0), axis=1)
    my_prob = my_prob.reshape(n_exp, row_count)
    routed_here = jnp.any(routes_all == my_expert, axis=2)
    rank = jnp.cumsum(routed_here.astype(jnp.int32), axis=1) - 1
    slot = jnp.arange(capacity, dtype=jnp.int32)
    pick_mask = routed_here[:, None, :] & (rank[:, None, :] == slot[None, :, None])
    pick = pick_mask.astype(low)
    picked_in = jnp.einsum("nst,ntd->nsd", pick, mlp_all, preferred_element_type=wide).astype(low)
    picked_cot = jnp.einsum("nst,ntd->nsd", pick, cot_all, preferred_element_type=wide).astype(low)
    picked_gate = jnp.sum(jnp.where(pick_mask, my_prob[:, None, :], 0.0), axis=2).reshape(-1, 1)
    flat_in = picked_in.reshape(-1, D)
    flat_cot = picked_cot.reshape(-1, D).astype(wide)
    gate_up = jnp.dot(flat_in, expert_in_full, preferred_element_type=wide)
    activation = (jax.nn.silu(gate_up[:, :FF]) * gate_up[:, FF:]).astype(low)
    result = jnp.dot(activation, expert_down_full, preferred_element_type=wide).astype(low)
    result = result.astype(wide)
    gate_grad = jnp.sum(flat_cot * result, axis=1).reshape(n_exp, capacity, 1)
    weighted = (picked_gate * result).astype(low).reshape(n_exp, capacity, D)
    shared_act = (jax.nn.silu(shared_gate) * shared_up).astype(low)
    mixed_part = jnp.einsum("nst,nsd->ntd", pick, weighted, preferred_element_type=wide)
    mixed_part = mixed_part.reshape(-1, D) + jnp.dot(
        shared_act, shdown_mine, preferred_element_type=wide
    )
    mixed_sum = lax.psum_scatter(
        mixed_part.astype(low), "expert", scatter_dimension=0, tiled=True
    )
    mixed = (residual + mixed_sum.astype(wide)).astype(low)

    cot_flat = cot_all.reshape(n_exp * row_count, D)
    grad_shdown = jnp.einsum("tf,td->fd", shared_act, cot_flat, preferred_element_type=wide)
    shared_act_grad = jnp.einsum("td,fd->tf", cot_flat, shdown_mine, preferred_element_type=wide)
    shared_gu_grad = jnp.concatenate(
        [
            shared_act_grad * shared_up * silu_slope(shared_gate),
            shared_act_grad * jax.nn.silu(shared_gate),
        ],
        axis=1,
    ).astype(low)
    grad_shin = jnp.einsum("td,tf->df", mlp_flat, shared_gu_grad, preferred_element_type=wide)
    grad_rows = (picked_gate * flat_cot).astype(low)
    grad_edown = jnp.einsum("rf,rd->fd", activation, grad_rows, preferred_element_type=wide)
    expert_act_grad = jnp.einsum(
        "rd,fd->rf", grad_rows, expert_down_full, preferred_element_type=wide
    )
    expert_gu_grad = swiglu_back(expert_act_grad, gate_up)
    grad_ein = jnp.einsum("rd,rf->df", flat_in, expert_gu_grad, preferred_element_type=wide)
    input_back = jnp.einsum(
        "rf,df->rd", expert_gu_grad, expert_in_full, preferred_element_type=wide
    )
    input_back = input_back.astype(low).reshape(n_exp, capacity, D)
    back_part = jnp.einsum("nst,nsd->ntd", pick, input_back, preferred_element_type=wide)
    back_part = back_part.reshape(-1, D) + jnp.einsum(
        "tf,df->td", shared_gu_grad, shin_mine, preferred_element_type=wide
    )
    back_sum = lax.psum_scatter(back_part.astype(low), "expert", scatter_dimension=0, tiled=True)
    gate_grad_tok = jnp.sum(jnp.where(pick_mask, gate_grad, 0.0), axis=1)
    prob_grad = lax.all_to_all(gate_grad_tok, "expert", 0, 0, tiled=True).T
    logit_grad = (
        router_probs * (prob_grad - jnp.sum(prob_grad * router_probs, axis=-1, keepdims=True))
    ).astype(low)
    grad_router = jnp.einsum("td,te->de", mlp_in, logit_grad, preferred_element_type=wide)
    mlp_in_grad = back_sum.astype(wide) + jnp.einsum(
        "te,de->td", logit_grad, router_full, preferred_element_type=wide
    )
    out_grad = cotangent.astype(wide)
    grad_gain_two = jnp.sum(mlp_in_grad * normed_two, axis=0)
    scaled_two = mlp_in_grad * gain_two
    resid_grad = out_grad + scale_two * (
        scaled_two - normed_two * jnp.mean(scaled_two * normed_two, axis=-1, keepdims=True)
    )
    resid_low = resid_grad.astype(low)
    grad_out = jnp.einsum("ti,td->id", heads_low, resid_low, preferred_element_type=wide)
    heads_grad = jnp.einsum("td,id->ti", resid_low, out_full, preferred_element_type=wide)
    heads_grad = heads_grad.astype(low).reshape(row_count, H, HD)
    attn_prob_grad = jnp.einsum("qhd,khd->hqk", heads_grad, values_low, preferred_element_type=wide)
    value_grad = jnp.einsum("hqk,qhd->khd", probs_low, heads_grad, preferred_element_type=wide)
    score_grad = probs_attn * (
        attn_prob_grad - jnp.sum(attn_prob_grad * probs_attn, axis=-1, keepdims=True)
    )
    score_grad = score_grad.astype(low)
    query_grad = (
        jnp.einsum("hqk,khd->qhd", score_grad, keys_rot, preferred_element_type=wide) * score_scale
    )
    key_grad = (
        jnp.einsum("hqk,qhd->khd", score_grad, queries, preferred_element_type=wide) * score_scale
    )
    projected_grad = jnp.stack(
        [
            rotate_back(query_grad, cosine, sine_table),
            rotate_back(key_grad, cosine, sine_table),
            value_grad,
        ],
        axis=1,
    )
    projected_grad = projected_grad.reshape(row_count, 3 * H * HD).astype(low)
    grad_qkv = jnp.einsum("td,tk->dk", attn_in, projected_grad, preferred_element_type=wide)
    attn_grad = jnp.einsum("tk,dk->td", projected_grad, qkv_full, preferred_element_type=wide)
    grad_gain_one = jnp.sum(attn_grad * normed_one, axis=0)
    scaled_one = attn_grad * gain_one
    input_grad = resid_grad + scale_one * (
        scaled_one - normed_one * jnp.mean(scaled_one * normed_one, axis=-1, keepdims=True)
    )

    small_grad = jnp.concatenate(
        [grad_router, grad_gain_one[:, None], grad_gain_two[:, None]], axis=1
    )
    small_own = lax.psum_scatter(small_grad, both, scatter_dimension=0, tiled=True)
    shin_back = lax.all_to_all(
        grad_shin.astype(low).reshape(n_all, rows_w, 2 * half), both, 0, 0, tiled=True
    )
    shin_own = jnp.sum(
        shin_back.reshape(n_dp, n_exp, rows_w, 2, n_dp, unit).astype(wide), axis=0
    )
    shin_own = shin_own.transpose(1, 2, 3, 0, 4).reshape(rows_w, 2 * FF)
    owned_grads = (
        small_own[:, expert_count:].T,
        lax.psum_scatter(grad_qkv.astype(low), both, scatter_dimension=0, tiled=True).astype(wide),
        lax.psum_scatter(grad_out.astype(low), both, scatter_dimension=0, tiled=True).astype(wide),
        shin_own,
        lax.psum_scatter(grad_shdown, "dp", scatter_dimension=0, tiled=True),
        small_own[:, :expert_count],
        lax.psum_scatter(
            grad_ein[None].astype(low), "dp", scatter_dimension=1, tiled=True
        ).astype(wide),
        lax.psum_scatter(
            grad_edown[None].astype(low), "dp", scatter_dimension=1, tiled=True
        ).astype(wide),
    )
    squares = sum((jnp.sum(grad_part * grad_part) for grad_part in owned_grads))
    total_squares = lax.psum(squares, ("dp", "expert"))
    grad_norm = jnp.sqrt(total_squares)
    factor = jnp.minimum(1.0, CLIP / grad_norm)
    weights = (
        norm_gains,
        w_qkv,
        w_out,
        w_shared_in,
        w_shared_down,
        w_router,
        w_expert_in,
        w_expert_down,
    )
    firsts = (
        gains_m,
        m_qkv,
        m_out,
        m_shared_in,
        m_shared_down,
        m_router,
        m_expert_in,
        m_expert_down,
    )
    seconds = (
        gains_v,
        v_qkv,
        v_out,
        v_shared_in,
        v_shared_down,
        v_router,
        v_expert_in,
        v_expert_down,
    )
    rates = (
        GAIN_RATE,
        D ** (-0.5),
        (H * HD // 64) ** (-0.5),
        D ** (-0.5),
        FF ** (-0.5),
        (4 * D) ** (-0.5),
        D ** (-0.5),
        (FF // 64) ** (-0.5),
    )
    decays = (0.0, DECAY, DECAY, DECAY, DECAY, DECAY, DECAY, DECAY)
    updated = []
    for weight, first_moment, second_moment, gradient, step_rate, decay_rate in zip(
        weights, firsts, seconds, owned_grads, rates, decays
    ):
        updated.extend(
            adam_update(
                weight, first_moment, second_moment, gradient, factor, step_rate, decay_rate
            )
        )
    return (
        mixed,
        input_grad,
        updated[0],
        updated[1],
        updated[2],
        updated[3],
        updated[4],
        updated[5],
        updated[6],
        updated[7],
        updated[8],
        updated[9],
        updated[10],
        updated[11],
        updated[12],
        updated[13],
        updated[14],
        updated[15],
        updated[16],
        updated[17],
        updated[18],
        updated[19],
        updated[20],
        updated[21],
        updated[22],
        updated[23],
        grad_norm,
    )


def solution(mesh):
    placed = (
        P(("dp", "expert"), None),
        P(("dp", "expert"), None),
        P(("dp", "expert"), None),
        P(("dp", "expert"), None),
        P(None, ("dp", "expert")),
        P(None, ("dp", "expert")),
        P(None, ("dp", "expert")),
        P(("dp", "expert"), None),
        P(("dp", "expert"), None),
        P(("dp", "expert"), None),
        P(("dp", "expert"), None),
        P(("dp", "expert"), None),
        P(("dp", "expert"), None),
        P(("dp", "expert"), None),
        P(("dp", "expert"), None),
        P(("dp", "expert"), None),
        P(("dp", "expert"), None),
        P(("dp", "expert"), None),
        P(("dp", "expert"), None),
        P(("dp", "expert"), None),
        P(("dp", "expert"), None),
        P(("dp", "expert"), None),
        P("expert", "dp", None),
        P("expert", "dp", None),
        P("expert", "dp", None),
        P("expert", "dp", None),
        P("expert", "dp", None),
        P("expert", "dp", None),
    )
    return jax.shard_map(
        local,
        mesh=mesh,
        in_specs=placed,
        out_specs=(
            P(("dp", "expert"), None),
            P(("dp", "expert"), None),
            P(None, ("dp", "expert")),
            P(None, ("dp", "expert")),
            P(None, ("dp", "expert")),
            P(("dp", "expert"), None),
            P(("dp", "expert"), None),
            P(("dp", "expert"), None),
            P(("dp", "expert"), None),
            P(("dp", "expert"), None),
            P(("dp", "expert"), None),
            P(("dp", "expert"), None),
            P(("dp", "expert"), None),
            P(("dp", "expert"), None),
            P(("dp", "expert"), None),
            P(("dp", "expert"), None),
            P(("dp", "expert"), None),
            P(("dp", "expert"), None),
            P(("dp", "expert"), None),
            P(("dp", "expert"), None),
            P("expert", "dp", None),
            P("expert", "dp", None),
            P("expert", "dp", None),
            P("expert", "dp", None),
            P("expert", "dp", None),
            P("expert", "dp", None),
            P(),
        ),
        check_vma=False,
    )
```

time: 1650 us -> 1560 us (0.945)
  waiting for transfers between devices: 623 us -> 956 us
  blocking collectives: 450 us -> 127 us
  local copies, waits for them, and re-layouts: 151 us -> 26.3 us
  matrix products: 200 us -> 306 us
  starting transfers between devices: 94.2 us -> 17.3 us
    reduce_scatter x5 -> x6, waiting for transfers between devices: 263 us -> 512 us  [the longest x1 157 us: local(): lax.psum_scatter(mixed_part.astype(low), 'expert', scatter_dimension=0, t...]
    all_to_all x4 -> x3, waiting for transfers between devices: 229 us -> 6.97 us  [the longest x1 6.97 us: local(): prob_grad = lax.all_to_all(gate_grad_tok, 'expert', 0, 0, tiled=True).T]
    all_gather x6, waiting for transfers between devices: 127 us -> 312 us  [the longest x1 109 us: local(): mlp_all = lax.all_gather(mlp_in, 'expert', axis=0, tiled=False)]
    all_gather x2 -> x3, blocking collectives: 246 us -> 73.3 us  [the longest x1 44.2 us: local(): small_full = lax.all_gather(small, both, axis=0, tiled=True)]
    unnamed x2 -> x1, blocking collectives: 164 us -> 13.4 us
    unnamed x17 -> x15, waiting for transfers between devices: 4.13 us -> 125 us
    dot_general x23 -> x26, matrix products: 141 us -> 245 us  [the longest x1 21.4 us: local(): jnp.einsum('rd,rf->df', flat_in, expert_gu_grad, preferred_element_type=w...]
    all_to_all x4 -> x3, starting transfers between devices: 87.1 us -> 13.5 us  [the longest x1 5.96 us: local(): prob_grad = lax.all_to_all(gate_grad_tok, 'expert', 0, 0, tiled=True).T]
  transfers between devices with their start and end apart: 20 -> 17, of which waited for: 11 -> 13; matrix products, arithmetic and copies ran while one was open for 31% -> 18% of each run, Pallas kernels for 0% -> 0%
where the time goes in v1:
time: 1560 us; the launch traced here: 1550 us
  waiting for transfers between devices  956 us (61%)
  matrix products  306 us (20%)
  blocking collectives  127 us (8%)
  other arithmetic  96 us (6%)
  local copies, waits for them, and re-layouts  26.3 us (2%)
  between operations  23.1 us (1%)
  starting transfers between devices  17.3 us (1%)
    reduce_scatter x1, waiting for transfers between devices, local(): lax.psum_scatter(mixed_part.astype(low), 'expert', scatter_dimension=0, t...  157 us
    reduce_scatter x1, waiting for transfers between devices, local(): lax.psum_scatter(grad_qkv.astype(low), both, scatter_dimension=0, tiled=T...  139 us
    reduce_scatter x1, waiting for transfers between devices, local(): lax.psum_scatter(grad_out.astype(low), both, scatter_dimension=0, tiled=T...  139 us
    unnamed x15, waiting for transfers between devices  125 us
    all_gather x1, waiting for transfers between devices, local(): mlp_all = lax.all_gather(mlp_in, 'expert', axis=0, tiled=False)  109 us
    all_gather x1, waiting for transfers between devices, local(): cot_all = lax.all_gather(cotangent, 'expert', axis=0, tiled=False)  76.8 us
    reduce_scatter x1, waiting for transfers between devices, local(): lax.psum_scatter(back_part.astype(low), 'expert', scatter_dimension=0, ti...  70.3 us
    all_gather x1, waiting for transfers between devices, local(): lax.all_gather(w_expert_in[0].astype(low), 'dp', axis=0, tiled=True)  48.6 us
  transfers between devices with their start and end apart: 17, of which 13 were waited for; matrix products, arithmetic and copies ran while one was open for 18% of the time, Pallas kernels for 0%

profile of v1, /device:TPU:0, one launch (start us, length us, event | category | flops | bytes accessed | tf_op | source)
XLA Modules:
  0.0 1551.3 jit_solution(4385332804224310652)
XLA Ops:
  13.0 44.2 %all-gather.5 = bf16[32,40,18]{1,2,0:T(8,128)(2,1)S(1)} all-gather(bf16[1,40,18]{1,2,0:T(8,128)(2,1)S(1)} %maximum_bitcast_fusion), channel_id=1, replica_groups=mesh['dp'=2,'expert'=16] {'dp','expert'}, dimensions={0}, use_global_device_ids=true | all-gather | bytes 47520 | tf_op jit(solution)/shard_map/all_gather | solution.py:133
  60.3 38.0 %all-gather.14.cloned.1.call-done = bf16[1280,3840]{1,0:T(8,128)(2,1)} async-done(((bf16[40,3840]{1,0:T(8,128)(2,1)}), bf16[1280,3840]{1,0:T(8,128)(2,1)}) %all-gather.14.cloned.1.call-update) | async-done | bytes 9830416 | tf_op jit(solution)/shard_map/all_gather | solution.py:132
  119.6 39.9 %all-gather.16.cloned.1.call-done = bf16[1280,1280]{1,0:T(8,128)(2,1)} async-done(((bf16[40,1280]{1,0:T(8,128)(2,1)}), bf16[1280,1280]{1,0:T(8,128)(2,1)}) %all-gather.16.cloned.1.call-update) | async-done | bytes 3276816 | tf_op jit(solution)/shard_map/all_gather | solution.py:134
  186.7 23.3 %all-gather = s32[6144,6]{0,1:T(8,128)S(1)} all-gather(s32[384,6]{0,1:T(8,128)S(1)} %copy-done.50), channel_id=2, replica_groups=mesh['dp'=2,'expert'=16] {'expert'}, dimensions={0}, use_global_device_ids=true | all-gather | bytes 156672 | tf_op jit(solution)/shard_map/all_gather | solution.py:139
  212.2 76.8 %all-gather.24.cloned.1.call-done = bf16[6144,1280]{1,0:T(8,128)(2,1)} async-done(((bf16[384,1280]{1,0:T(8,128)(2,1)}), bf16[6144,1280]{1,0:T(8,128)(2,1)}) %all-gather.24.cloned.1.call-update) | async-done | bytes 15728656 | tf_op jit(solution)/shard_map/all_gather | solution.py:138
  289.0 12.6 convolution_convert_fusion.5
  301.6 108.6 %all-gather.18.cloned.1.call-done = bf16[6144,1280]{1,0:T(8,128)(2,1)} async-done(((bf16[384,1280]{1,0:T(8,128)(2,1)}), bf16[6144,1280]{1,0:T(8,128)(2,1)}) %all-gather.18.cloned.1.call-update) | async-done | bytes 15728656 | tf_op jit(solution)/shard_map/all_gather | solution.py:181
  410.2 12.7 convolution_convert_fusion.6
  423.0 48.6 %all-gather.20.cloned.1.call-done = bf16[1,1280,1792]{2,1,0:T(8,128)(2,1)} async-done(((bf16[1,640,1792]{2,1,0:T(8,128)(2,1)}), bf16[1,1280,1792]{2,1,0:T(8,128)(2,1)}) %all-gather.20.cloned.1.call-update) | async-done | bytes 4587536 | tf_op jit(solution)/shard_map/all_gather | solution.py:140
  471.6 21.0 %fusion.14 = f32[2944,1792]{0,1:T(8,128)} fusion(bf16[2944,1280]{1,0:T(8,128)(2,1)} %bitcast.180, bf16[1,1280,1792]{2,1,0:T(8,128)(2,1)} %all-gather.20.cloned.1.call-done), kind=kOutput, calls=%fused_computation.37 | convolution fusion | flops 13505658880 | bytes 33226752 | tf_op jit(solution)/shard_map/dot_general | solution.py:201
  492.6 10.8 fusion.89
  503.7 10.9 multiply_convert_fusion.2
  514.6 15.6 %fusion.6 = (f32[2944]{0:T(1024)}, bf16[2944,1280]{1,0:T(8,128)(2,1)}) fusion(bf16[16,184,1280]{2,1,0:T(8,128)(2,1)} %convolution_convert_fusion.5, bf16[2944,896]{0,1:T(8,128)(2,1)} %multiply_convert_fusion.2, bf16[1,896,1280]{2,1,0:T(8,128)(2,1)} %all-gather.22.cloned.1.call-done), kind=kOutput, calls=%fused_computation.11 | convolution fusion | flops 6771667968 | bytes 22654464 | tf_op jit(solution)/shard_map/dot_general | solution.py:203
  534.7 11.6 fusion.5
  546.3 18.9 %multiply_convert_fusion.1 = (bf16[2944,896]{0,1:T(8,128)(2,1)}, bf16[2944,896]{0,1:T(8,128)(2,1)}) fusion(f32[2944,1792]{0,1:T(8,128)} %fusion.14, bf16[2944,1280]{1,0:T(8,128)(2,1)} %get-tuple-element.86, bf16[1,896,1280]{2,1,0:T(8,128)(2,1)S(1)} %copy-done.60), kind=kOutput, calls=%fused_computation.16 | convolution fusion | flops 6787121152 | bytes 41484288 | tf_op jit(solution)/shard_map/rd,fd->rf/dot_general | solution.py:230
  565.2 21.0 %convolution_convert_fusion.1 = bf16[2944,1280]{1,0:T(8,128)(2,1)} fusion(bf16[2944,896]{0,1:T(8,128)(2,1)} %get-tuple-element.60, bf16[2944,896]{0,1:T(8,128)(2,1)} %get-tuple-element.59, bf16[1,1280,1792]{2,1,0:T(8,128)(2,1)} %all-gather.20.cloned.1.call-done), kind=kOutput, calls=%fused_computation.12 | convolution fusion | flops 13530529792 | bytes 22675456 | tf_op jit(solution)/shard_map/rf,df->rd/dot_general | solution.py:235
  586.2 14.9 fusion.17
  601.2 11.1 multiply_convert_fusion.6
  613.4 18.0 %fusion.2 = bf16[6144,1280]{1,0:T(8,128)(2,1)} fusion(f32[16,384,1280]{2,1,0:T(8,128)} %fusion.17, bf16[1280,112]{1,0:T(8,128)(2,1)S(1)} %bitcast.192, bf16[6144,56]{0,1:T(8,128)(2,1)S(1)} %get-tuple-element.66, bf16[6144,56]{0,1:T(8,128)(2,1)S(1)} %get-tuple-element.65), kind=kOutput, calls=%fused_computation.2 | convolution fusion | flops 1780088832 | bytes 48848896 | tf_op jit(solution)/shard_map/tf,df->td/dot_general | solution.py:240
  631.5 20.0 %fusion.20 = f32[16,384,1280]{2,1,0:T(8,128)} fusion(bf16[16,184,1280]{2,1,0:T(8,128)(2,1)} %bitcast.177, s32[16,384]{1,0:T(8,128)S(1)} %copy_bitcast_fusion, pred[16,384]{1,0:T(8,128)(4,1)S(1)} %reshape.288), kind=kOutput, calls=%fused_computation.45 | convolution fusion | flops 2896330752 | bytes 39024640 | tf_op jit(solution)/shard_map/nst,nsd->ntd/dot_general | solution.py:208
  651.5 19.0 %fusion.3 = bf16[6144,1280]{1,0:T(8,128)(2,1)} fusion(f32[16,384,1280]{2,1,0:T(8,128)} %fusion.20, bf16[6144,56]{0,1:T(8,128)(2,1)S(1)} %copy-done.9, bf16[56,1280]{1,0:T(8,128)(2,1)S(1)} %copy-done.36), kind=kOutput, calls=%fused_computation.4 | convolution fusion | flops 896532480 | bytes 48017408 | tf_op jit(solution)/shard_map/dot_general | solution.py:209
  670.6 12.4 fusion.24
  683.1 21.4 %fusion.8 = bf16[1,1280,1792]{2,1,0:T(8,128)(2,1)} fusion(bf16[2944,1280]{1,0:T(8,128)(2,1)} %bitcast.181, bf16[2944,896]{0,1:T(8,128)(2,1)} %get-tuple-element.60, bf16[2944,896]{0,1:T(8,128)(2,1)} %get-tuple-element.59), kind=kOutput, calls=%fused_computation.25 | convolution fusion | flops 13529055232 | bytes 22675456 | tf_op jit(solution)/shard_map/rd,rf->df/dot_general | solution.py:234
  720.0 70.3 %reduce-scatter.12.cloned.1.call-done = bf16[384,1280]{1,0:T(8,128)(2,1)} async-done(((bf16[6144,1280]{1,0:T(8,128)(2,1)}), bf16[384,1280]{1,0:T(8,128)(2,1)}) %reduce-scatter.12.cloned.1.call-update) | async-done | bytes 983056 | tf_op jit(solution)/shard_map/reduce_scatter | solution.py:243
  793.5 157.4 %reduce-scatter.10.cloned.1.call-done = bf16[384,1280]{1,0:T(8,128)(2,1)} async-done(((bf16[6144,1280]{1,0:T(8,128)(2,1)}), bf16[384,1280]{1,0:T(8,128)(2,1)}) %reduce-scatter.10.cloned.1.call-update) | async-done | bytes 983056 | tf_op jit(solution)/shard_map/reduce_scatter | solution.py:212
  971.3 10.0 fusion.52
  987.0 10.0 convolution_convert_fusion
  1019.0 13.4 fusion
  1058.8 124.4 %all-reduce.5.cloned.1.call-done = f32[1280,18]{0,1:T(8,128)} async-done(((f32[1280,18]{0,1:T(8,128)}), f32[1280,18]{0,1:T(8,128)}) %all-reduce.5.cloned.1.call-update) | async-done | bytes 92176
  1186.0 138.9 %reduce-scatter.16.cloned.1.call-done = bf16[40,1280]{1,0:T(8,128)(2,1)} async-done(((bf16[1280,1280]{1,0:T(8,128)(2,1)}), bf16[40,1280]{1,0:T(8,128)(2,1)}) %reduce-scatter.16.cloned.1.call-update) | async-done | bytes 102416 | tf_op jit(solution)/shard_map/reduce_scatter | solution.py:306
  1326.4 139.5 %reduce-scatter.14.cloned.1.call-done = bf16[40,3840]{1,0:T(8,128)(2,1)} async-done(((bf16[1280,3840]{1,0:T(8,128)(2,1)}), bf16[40,3840]{1,0:T(8,128)(2,1)}) %reduce-scatter.14.cloned.1.call-update) | async-done | bytes 307216 | tf_op jit(solution)/shard_map/reduce_scatter | solution.py:305
  1476.4 40.0 %psum.7 = f32[]{:T(128)} all-reduce(f32[]{:T(128)S(6)} %add.255), channel_id=1, replica_groups=mesh['dp'=2,'expert'=16] {'dp','expert'}, use_global_device_ids=true, to_apply=%region_41.42 | all-reduce | flops 1 | bytes 8 | tf_op jit(solution)/shard_map/psum | solution.py:318
  (285 shorter events, 193.1 us)
Async XLA Ops:
  7.2 50.3 %copy-start.61 = (s32[1,4]{1,0:T(1,128)S(1)}, s32[1,4]{1,0:T(1,128)}, u32[]{:S(2)}) copy-start(s32[1,4]{1,0:T(1,128)} %param.29) | copy-start | bytes 52
  7.2 52.0 %copy-start.13 = (bf16[384,1280]{1,0:T(8,128)(2,1)S(1)}, bf16[384,1280]{1,0:T(8,128)(2,1)}, u32[]{:S(2)}) copy-start(bf16[384,1280]{1,0:T(8,128)(2,1)} %param.28) | copy-start | bytes 2949124
  7.2 91.0 %all-gather.14.cloned.1.call-start = ((), (), s32[]{:S(2)}) async-start(), calls=%async_computation.9 | async-start | bytes 10137600 | tf_op jit(solution)/shard_map/all_gather | solution.py:132
  9.2 150.3 %all-gather.16.cloned.1.call-start = ((), (), s32[]{:S(2)}) async-start(), calls=%async_computation.10 | async-start | bytes 3379200 | tf_op jit(solution)/shard_map/all_gather | solution.py:134
  10.9 278.1 %all-gather.24.cloned.1.call-start = ((), (), s32[]{:S(2)}) async-start(), calls=%async_computation.20 | async-start | bytes 16711680 | tf_op jit(solution)/shard_map/all_gather | solution.py:138
  11.6 398.6 %all-gather.18.cloned.1.call-start = ((), (), s32[]{:S(2)}) async-start(), calls=%async_computation.17 | async-start | bytes 16711680 | tf_op jit(solution)/shard_map/all_gather | solution.py:181
  57.5 122.7 %copy-start.33 = (bf16[1280,18]{0,1:T(8,128)(2,1)}, bf16[1280,18]{0,1:T(8,128)(2,1)S(1)}, u32[]{:S(2)}) copy-start(bf16[1280,18]{0,1:T(8,128)(2,1)S(1)} %reshape.292) | copy-start | bytes 138244
  57.9 48.5 %copy-start.45 = (f32[1280]{0:T(1024)}, f32[1280]{0:T(1024)S(1)}, u32[]{:S(2)}) copy-start(f32[1280]{0:T(1024)S(1)} %get-tuple-element.32) | copy-start | bytes 15364
  57.9 105.2 %copy-start.40 = (f32[1280]{0:T(1024)}, f32[1280]{0:T(1024)S(1)}, u32[]{:S(2)}) copy-start(f32[1280]{0:T(1024)S(1)} %get-tuple-element.31) | copy-start | bytes 15364
  59.5 46.9 %copy-start.51 = (f32[384]{0:T(512)}, f32[384]{0:T(512)S(1)}, u32[]{:S(2)}) copy-start(f32[384]{0:T(512)S(1)} %add_rsqrt_fusion.1) | copy-start | bytes 4612
  119.6 43.5 %copy-start.62 = (bf16[10,128,384]{2,1,0:T(8,128)(2,1)}, bf16[10,128,384]{2,1,0:T(8,128)(2,1)S(1)}, u32[]{:S(2)}) copy-start(bf16[10,128,384]{2,1,0:T(8,128)(2,1)S(1)} %fusion.64) | copy-start | bytes 2949124
  165.6 306.0 %all-gather.20.cloned.1.call-start = ((), (), s32[]{:S(2)}) async-start(), calls=%async_computation.18 | async-start | bytes 6881280 | tf_op jit(solution)/shard_map/all_gather | solution.py:140
  175.6 316.9 %all-to-all-start = ((bf16[32,40,112]{2,1,0:T(8,128)(2,1)}), bf16[32,40,112]{2,1,0:T(8,128)(2,1)S(1)}, u32[]{:S(2)}, u32[]{:S(2)}) async-start(bf16[32,40,112]{2,1,0:T(8,128)(2,1)} %pad_maximum_fusion.9), calls=%async_computation | async-start | bytes 655360 | tf_op jit(solution)/shard_map/all_to_all | solution.py:149
  178.9 335.7 %all-gather.22.cloned.1.call-start = ((), (), s32[]{:S(2)}) async-start(), calls=%async_computation.19 | async-start | bytes 3440640 | tf_op jit(solution)/shard_map/all_gather | solution.py:141
  180.1 610.2 %reduce-scatter.12.cloned.1.call-start = ((), (), s32[]{:S(2)}) async-start(), calls=%async_computation.12 | async-start | bytes 16711680 | tf_op jit(solution)/shard_map/reduce_scatter | solution.py:243
  586.2 14.9 copy-start.35
  631.4 319.5 %reduce-scatter.10.cloned.1.call-start = ((), (), s32[]{:S(2)}) async-start(), calls=%async_computation.11 | async-start | bytes 16711680 | tf_op jit(solution)/shard_map/reduce_scatter | solution.py:212
  631.5 20.0 %copy-start.9 = (bf16[6144,56]{0,1:T(8,128)(2,1)S(1)}, bf16[6144,56]{0,1:T(8,128)(2,1)}, u32[]{:S(2)}) copy-start(bf16[6144,56]{0,1:T(8,128)(2,1)} %get-tuple-element.67) | copy-start | bytes 2064388
  631.5 20.0 %copy-start.36 = (bf16[56,1280]{1,0:T(8,128)(2,1)S(1)}, bf16[56,1280]{1,0:T(8,128)(2,1)}, u32[]{:S(2)}) copy-start(bf16[56,1280]{1,0:T(8,128)(2,1)} %reshape.294) | copy-start | bytes 430084
  670.5 376.5 %reduce-scatter.20.cloned.1.call-start = ((), (), s32[]{:S(2)}) async-start(), calls=%async_computation.16 | async-start | bytes 3440640 | tf_op jit(solution)/shard_map/reduce_scatter | solution.py:313
  683.0 372.4 %reduce-scatter.18.cloned.1.call-start = ((), (), s32[]{:S(2)}) async-start(), calls=%async_computation.15 | async-start | bytes 6881280 | tf_op jit(solution)/shard_map/reduce_scatter | solution.py:310
  704.5 85.8 %copy-start.1 = (f32[384,1280]{1,0:T(8,128)S(1)}, f32[384,1280]{1,0:T(8,128)}, u32[]{:S(2)}) copy-start(f32[384,1280]{1,0:T(8,128)} %copy-done) | copy-start | bytes 5898244
  704.5 85.8 %copy-start.41 = (f32[1280]{0:T(1024)S(1)}, f32[1280]{0:T(1024)}, u32[]{:S(2)}) copy-start(f32[1280]{0:T(1024)} %copy-done.40) | copy-start | bytes 15364
  704.5 85.8 %copy-start.44 = (f32[384]{0:T(512)S(1)}, f32[384]{0:T(512)}, u32[]{:S(2)}) copy-start(f32[384]{0:T(512)} %copy-done.43) | copy-start | bytes 4612
  706.7 13.0 all-to-all-start.1
  712.7 470.5 %all-reduce.5.cloned.1.call-start = ((), (), s32[]{:S(2)}) async-start(), calls=%async_computation.21 | async-start | bytes 245760
  720.0 230.9 %copy-start.12 = (bf16[384,1280]{1,0:T(8,128)(2,1)S(1)}, bf16[384,1280]{1,0:T(8,128)(2,1)}, u32[]{:S(2)}) copy-start(bf16[384,1280]{1,0:T(8,128)(2,1)} %param.31) | copy-start | bytes 2949124
  981.9 342.9 %reduce-scatter.16.cloned.1.call-start = ((), (), s32[]{:S(2)}) async-start(), calls=%async_computation.14 | async-start | bytes 3379200 | tf_op jit(solution)/shard_map/reduce_scatter | solution.py:306
  987.0 478.9 %reduce-scatter.14.cloned.1.call-start = ((), (), s32[]{:S(2)}) async-start(), calls=%async_computation.13 | async-start | bytes 10137600 | tf_op jit(solution)/shard_map/reduce_scatter | solution.py:305
  1006.1 31.2 %all-to-all-start.2 = ((bf16[32,40,112]{2,1,0:T(8,128)(2,1)}), bf16[32,40,112]{2,1,0:T(8,128)(2,1)S(1)}, u32[]{:S(2)}, u32[]{:S(2)}) async-start(bf16[32,40,112]{2,1,0:T(8,128)(2,1)} %bitcast.36), calls=%async_computation.6 | async-start | bytes 655360 | tf_op jit(solution)/shard_map/all_to_all | solution.py:296
  1010.5 24.5 %copy-start.58 = (u32[32]{0:T(128)S(1)}, u32[32]{0:T(128)}, u32[]{:S(2)}) copy-start(u32[32]{0:T(128)} %constant.91) | copy-start | bytes 388
  1032.4 4.1 collective-permute-start
  (54 other events, 300.9 us)
Sparse Core Ops, SparseCore 0:
  11.5 86.7 all-gather.13
  101.7 57.7 all-gather.15
  161.8 127.1 all-gather.23
  291.7 118.4 all-gather.17
  412.2 59.3 all-gather.19
  473.5 35.3 all-gather.21
  631.6 158.6 reduce-scatter.11
  794.9 155.9 reduce-scatter.9
  953.8 33.0 reduce-scatter.19
  989.7 65.5 reduce-scatter.17
  1061.5 121.6 all-reduce.4
  1185.9 138.9 reduce-scatter.15
  1331.8 134.0 reduce-scatter.13

commit v2 on v1

--- a/solution.py
+++ b/solution.py
@@ -1,6 +1,11 @@
+import functools
+import itertools
+
 import jax
 import jax.numpy as jnp
 from jax import lax
+from jax.experimental import pallas as pl
+from jax.experimental.pallas import tpu as pltpu
 from jax.sharding import PartitionSpec as P
 
 D = 1280
@@ -82,6 +87,443 @@
         first_hat / (jnp.sqrt(second_hat) + ADAM_EPS) + decay_rate * weight
     )
     return (weight_new, first_new, second_new)
+
+
+MESH = pl.DeviceIdType.MESH
+
+
+class Place:
+    def __init__(self, n_dp, n_exp):
+        rest = n_exp // 2
+        na = 4 if rest % 4 == 0 else rest
+        self.size = {"A": na, "B": rest // na, "C": 2, "Y": n_dp}
+        e = lax.axis_index("expert")
+        nb = self.size["B"]
+        self.pos = {"A": e // (2 * nb), "B": (e // 2) % nb, "C": e % 2, "Y": lax.axis_index("dp")}
+
+    def expert(self, pos):
+        return (pos["A"] * self.size["B"] + pos["B"]) * 2 + pos["C"]
+
+    def flat(self, pos):
+        return pos["Y"] * (2 * self.size["A"] * self.size["B"]) + self.expert(pos)
+
+    def device(self, pos):
+        return (pos["Y"], self.expert(pos))
+
+    def moved(self, **steps):
+        pos = dict(self.pos)
+        for axis, step in steps.items():
+            if axis == "A":
+                pos[axis] = pos[axis] + step
+            else:
+                pos[axis] = lax.rem(pos[axis] + step, self.size[axis])
+        return pos
+
+    def inside(self, step):
+        there = self.pos["A"] + step
+        return (there >= 0) & (there < self.size["A"])
+
+    def greet(self, axes, line_all):
+        barrier = pltpu.get_barrier_semaphore()
+        total = 0
+        for axis in axes:
+            if axis == "A":
+                reach = range(1, self.size["A"]) if line_all else (1,)
+                for step in [s * d for d in reach for s in (1, -1)]:
+                    near = self.inside(step)
+
+                    @pl.when(near)
+                    def _(step=step):
+                        pl.semaphore_signal(barrier, inc=1, device_id=self.device(self.moved(A=step)), device_id_type=MESH)
+
+                    total = total + jnp.where(near, 1, 0)
+            else:
+                for step in range(1, self.size[axis]):
+                    pl.semaphore_signal(barrier, inc=1, device_id=self.device(self.moved(**{axis: step})), device_id_type=MESH)
+                    total = total + 1
+        pl.semaphore_wait(barrier, total)
+
+
+def under(conds, body):
+    if conds:
+        both = conds[0]
+        for c in conds[1:]:
+            both = both & c
+        pl.when(both)(body)
+    else:
+        body()
+
+
+PACE = {"A": 4, "B": 5, "Y": 5, "C": 1}
+
+
+def plan_gather(size, orders):
+    events = []
+    for part, order in enumerate(orders):
+        spans = []
+        for axis in order:
+            n = size[axis]
+            spans.append(range(1 - n, n) if axis == "A" else range(n))
+        for offs in itertools.product(*spans):
+            when = 0
+            for axis, o in zip(order, offs):
+                when += PACE[axis] * (abs(o) if axis == "A" else (1 if o else 0))
+            events.append((when, part, offs))
+    events.sort(key=lambda ev: ev[0])
+    return events
+
+
+def gather_body(place, orders, slices, own_ref, out_ref, block_of, send_sem, recv_sem):
+    size = place.size
+    sends = []
+    count = [0]
+
+    def send(conds, part, src_block, src, to):
+        slot = count[0]
+        count[0] += 1
+        lo, n = slices[part]
+
+        def copy():
+            j = src_block()
+            return pltpu.make_async_remote_copy(
+                src_ref=(own_ref if src is None else out_ref.at[j]).at[:, pl.ds(lo, n)],
+                dst_ref=out_ref.at[j].at[:, pl.ds(lo, n)],
+                send_sem=send_sem.at[slot],
+                recv_sem=recv_sem.at[part, j],
+                device_id=place.device(to()),
+                device_id_type=MESH,
+            )
+
+        under(conds, lambda: copy().start())
+        sends.append((conds, copy))
+
+    for _, part, offs in plan_gather(size, orders):
+        order = orders[part]
+        steps = dict(zip(order, offs))
+        last = max([i for i, o in enumerate(offs) if o], default=-1)
+        conds = []
+        if steps["A"]:
+            conds.append(place.inside(steps["A"]))
+
+        def block(steps=steps):
+            return block_of(place.moved(**{k: o for k, o in steps.items() if o}))
+
+        if last >= 0:
+            lo, n = slices[part]
+
+            def wait(block=block, part=part, lo=lo, n=n):
+                j = block()
+                pltpu.make_async_copy(
+                    out_ref.at[j].at[:, pl.ds(lo, n)], out_ref.at[j].at[:, pl.ds(lo, n)], recv_sem.at[part, j]
+                ).wait()
+
+            under(conds, wait)
+        src = None if last < 0 else out_ref
+        for i in range(max(last, 0), len(order)):
+            axis = order[i]
+            if axis == "A":
+                ways = (1, -1) if i > last else ((1,) if steps["A"] < 0 else (-1,))
+                for way in ways:
+                    send(conds + [place.inside(way)], part, block, src, lambda way=way: place.moved(A=way))
+            elif i > last:
+                for t in range(1, size[axis]):
+                    send(conds, part, block, src, lambda axis=axis, t=t: place.moved(**{axis: t}))
+    for conds, copy in sends:
+        under(conds, lambda copy=copy: copy().wait_send())
+
+
+def count_gather(size, orders):
+    total = 0
+    for _, part, offs in plan_gather(size, orders):
+        order = orders[part]
+        last = max([i for i, o in enumerate(offs) if o], default=-1)
+        for i in range(max(last, 0), len(order)):
+            if order[i] == "A":
+                total += 2 if i > last else 1
+            elif i > last:
+                total += size[order[i]] - 1
+    return total
+
+
+def sizes(n_dp, n_exp):
+    rest = n_exp // 2
+    na = 4 if rest % 4 == 0 else rest
+    return {"A": na, "B": rest // na, "C": 2, "Y": n_dp}
+
+
+def gather_kernel(n_dp, n_exp, orders, slices, dense, x_ref, out_ref, send_sem, recv_sem, local_sem):
+    place = Place(n_dp, n_exp)
+    block_of = place.flat if dense else place.expert
+    place.greet(orders[0], False)
+    own = pltpu.make_async_copy(x_ref, out_ref.at[block_of(place.pos)], local_sem)
+    own.start()
+    gather_body(place, orders, slices, x_ref, out_ref, block_of, send_sem, recv_sem)
+    own.wait()
+
+
+def gather(x, n_dp, n_exp, dense, cid, parts=None):
+    size = sizes(n_dp, n_exp)
+    rows, cols = x.shape
+    if dense:
+        orders = ("ABYC", "AYBC")
+        half = cols // 256 * 128
+        slices = ((0, half), (half, cols - half))
+    else:
+        orders = parts or ("ABC",)
+        w = cols // len(orders)
+        slices = tuple((i * w, w) for i in range(len(orders)))
+    blocks = n_exp * (n_dp if dense else 1)
+    return pl.pallas_call(
+        functools.partial(gather_kernel, n_dp, n_exp, orders, slices, dense),
+        out_shape=jax.ShapeDtypeStruct((blocks, rows, cols), x.dtype),
+        in_specs=[pl.BlockSpec(memory_space=pl.ANY)],
+        out_specs=pl.BlockSpec(memory_space=pl.ANY),
+        scratch_shapes=[
+            pltpu.SemaphoreType.DMA((count_gather(size, orders),)),
+            pltpu.SemaphoreType.DMA((len(orders), blocks)),
+            pltpu.SemaphoreType.DMA(()),
+        ],
+        compiler_params=pltpu.CompilerParams(collective_id=cid, has_side_effects=True),
+        name="gather_dense" if dense else "gather_group",
+    )(x)
+
+
+def line_order(n):
+    out = []
+    for i in range((n + 1) // 2):
+        out.append(i)
+        if n - 1 - i != i:
+            out.append(n - 1 - i)
+    return out
+
+
+def stage_slots(size, order):
+    slots = {}
+    for i, axis in enumerate(order):
+        rest = [line_order(size[x]) if x == "A" else range(size[x]) for x in order[i + 1:]]
+        if axis == "A":
+            for who in range(size["A"]):
+                slots[(i, who, ())] = len(slots)
+        else:
+            for who in range(1, size[axis]):
+                for r in itertools.product(*rest):
+                    slots[(i, who, r)] = len(slots)
+    return slots
+
+
+def reduce_body(place, orders, slices, g_ref, block_of, land, base, send_sem, recv_sem, finish):
+    size = place.size
+    tables = [stage_slots(size, order) for order in orders]
+    sends = []
+    n = [0]
+
+    def target(order, i, o, rest):
+        pos = dict(place.pos)
+        for axis, v in zip(order[i:], (o,) + tuple(rest)):
+            if axis == "A":
+                pos["A"] = v
+            else:
+                pos[axis] = lax.rem(pos[axis] + v, size[axis])
+        return pos
+
+    def send(conds, part, src, slot, to):
+        at = n[0]
+        n[0] += 1
+
+        def copy():
+            return pltpu.make_async_remote_copy(
+                src_ref=src(), dst_ref=land[part].at[slot], send_sem=send_sem.at[at],
+                recv_sem=recv_sem.at[base[part] + slot], device_id=place.device(to()), device_id_type=MESH)
+
+        under(conds, lambda: copy().start())
+        sends.append((conds, copy))
+
+    def wait(part, slot):
+        ref = land[part].at[slot]
+        pltpu.make_async_copy(ref, ref, recv_sem.at[base[part] + slot]).wait()
+
+    def rests(order, i):
+        return list(itertools.product(*[line_order(size[x]) if x == "A" else range(size[x]) for x in order[i:]]))
+
+    def far_first(items):
+        return sorted(items, key=lambda r: tuple(0 if (isinstance(v, int) and v) else 1 for v in r[:-1]))
+
+    for part, order in enumerate(orders):
+        lo, w = slices[part]
+        axis = order[0]
+        for t in range(1, size[axis]):
+            for r in far_first(rests(order, 1)):
+                def src(order=order, t=t, r=r, lo=lo, w=w):
+                    return g_ref.at[block_of(target(order, 0, t, r)), :, pl.ds(lo, w)]
+                send([], part, src, tables[part][(0, t, r)], lambda axis=axis, t=t: place.moved(**{axis: t}))
+    for i in range(1, len(orders[0])):
+        for pick in far_first(rests(orders[0], i)):
+            for part, order in enumerate(orders):
+                lo, w = slices[part]
+                axis = order[i]
+                before = order[i - 1]
+                r = pick
+                got = [tables[part][(i - 1, t, r)] for t in range(1, size[before])]
+                for slot in got:
+                    wait(part, slot)
+                if i == 1:
+                    total = g_ref[block_of(target(order, 1, r[0], r[1:])), :, lo:lo + w].astype(jnp.float32)
+                else:
+                    total = land[part][tables[part][(i - 2, 1, (0,) + r)]].astype(jnp.float32)
+                for slot in got:
+                    total = total + land[part][slot].astype(jnp.float32)
+                land[part][got[0]] = total.astype(land[part].dtype)
+                o, later = r[0], r[1:]
+                def src(part=part, slot=got[0]):
+                    return land[part].at[slot]
+                if axis == "A":
+                    a = place.pos["A"]
+                    at = n[0]
+                    n[0] += 1
+                    def copy(part=part, slot=got[0], o=o, at=at, i=i):
+                        first = tables[part][(i, 0, ())]
+                        return pltpu.make_async_remote_copy(
+                            src_ref=land[part].at[slot], dst_ref=land[part].at[first + a], send_sem=send_sem.at[at],
+                            recv_sem=recv_sem.at[base[part] + first + a],
+                            device_id=place.device(dict(place.pos, A=o)), device_id_type=MESH)
+                    away = [a != o]
+                    under(away, lambda copy=copy: copy().start())
+                    sends.append((away, copy))
+                elif o:
+                    send([], part, src, tables[part][(i, o, later)], lambda axis=axis, o=o: place.moved(**{axis: o}))
+    last = len(orders[0]) - 1
+    for part, order in enumerate(orders):
+        own = tables[part][(last - 1, 1, (0,))]
+        a = place.pos["A"]
+        first = tables[part][(last, 0, ())]
+        step = tables[part][(last - 1, 1, (line_order(size["A"])[1],))] - own if size["A"] > 1 else 0
+        mine = own
+        for k, p in enumerate(line_order(size["A"])):
+            mine = jnp.where(a == p, tables[part][(last - 1, 1, (p,))], mine)
+        total = land[part][mine].astype(jnp.float32)
+        for d in range(1, size["A"]):
+            j = lax.rem(a + d, size["A"])
+            wait(part, first + j)
+            total = total + land[part][first + j].astype(jnp.float32)
+        finish(part, total)
+    for conds, copy in sends:
+        under(conds, lambda copy=copy: copy().wait_send())
+
+
+def count_reduce(size, orders):
+    total = 0
+    for order in orders:
+        for i, axis in enumerate(order):
+            rest = 1
+            for x in order[i + 1:]:
+                rest *= size[x]
+            total += size["A"] if axis == "A" else (size[axis] - 1) * rest
+    return total
+
+
+def reduce_kernel(n_dp, n_exp, orders, slices, dense, g_ref, out_ref, *scratch):
+    land, (send_sem, recv_sem) = scratch[:-2], scratch[-2:]
+    place = Place(n_dp, n_exp)
+    place.greet(orders[0], True)
+    base = [0]
+    for order in orders:
+        base.append(base[-1] + len(stage_slots(place.size, order)))
+
+    def finish(part, total):
+        lo, w = slices[part]
+        out_ref[:, lo:lo + w] = total.astype(out_ref.dtype)
+
+    reduce_body(place, orders, slices, g_ref, place.flat if dense else place.expert, land, base, send_sem, recv_sem, finish)
+
+
+def reduce_scatter(g, n_dp, n_exp, dense, cid, orders=None):
+    size = sizes(n_dp, n_exp)
+    blocks, rows, cols = g.shape
+    orders = orders or (("CBYA", "CYBA") if dense else ("CBA",))
+    w = cols // 128 // len(orders) * 128
+    slices = tuple((i * w, w if i < len(orders) - 1 else cols - i * w) for i in range(len(orders)))
+    slots = [len(stage_slots(size, order)) for order in orders]
+    if (blocks + max(slots)) * ((rows + 15) // 16 * 16) * cols * 2 > 44 * 1024 * 1024:
+        axes = ("dp", "expert") if dense else "expert"
+        return lax.psum_scatter(g, axes, scatter_dimension=0, tiled=False).astype(jnp.float32)
+    return pl.pallas_call(
+        functools.partial(reduce_kernel, n_dp, n_exp, orders, slices, dense),
+        out_shape=jax.ShapeDtypeStruct((rows, cols), jnp.float32),
+        in_specs=[pl.BlockSpec(memory_space=pltpu.VMEM)],
+        out_specs=pl.BlockSpec(memory_space=pltpu.VMEM),
+        scratch_shapes=[pltpu.VMEM((k, rows, s[1]), g.dtype) for k, s in zip(slots, slices)] + [
+            pltpu.SemaphoreType.DMA((count_reduce(size, orders),)),
+            pltpu.SemaphoreType.DMA((sum(slots),)),
+        ],
+        compiler_params=pltpu.CompilerParams(collective_id=cid, has_side_effects=True, vmem_limit_bytes=60 * 1024 * 1024),
+        name="reduce_dense" if dense else "reduce_group",
+    )(g)
+
+
+def spread_kernel(n_dp, n_exp, x_ref, out_ref, send_sem, recv_sem):
+    n = n_dp * n_exp
+    me = lax.axis_index("dp") * n_exp + lax.axis_index("expert")
+    barrier = pltpu.get_barrier_semaphore()
+
+    def device(step):
+        to = lax.rem(me + step, n)
+        return (to // n_exp, lax.rem(to, n_exp))
+
+    def greet(step, carry):
+        pl.semaphore_signal(barrier, inc=1, device_id=device(step), device_id_type=MESH)
+        return carry
+
+    lax.fori_loop(1, n, greet, 0)
+    pl.semaphore_wait(barrier, n - 1)
+
+    def copy(step):
+        return pltpu.make_async_remote_copy(
+            src_ref=x_ref, dst_ref=out_ref.at[step], send_sem=send_sem.at[step], recv_sem=recv_sem.at[step],
+            device_id=device(step), device_id_type=MESH)
+
+    def start(step, carry):
+        copy(step).start()
+        return carry
+
+    def wait(step, carry):
+        copy(step).wait()
+        return carry
+
+    lax.fori_loop(1, n, start, 0)
+    out_ref[0] = x_ref[...]
+    lax.fori_loop(1, n, wait, 0)
+
+
+def sum_everywhere(value, n_dp, n_exp, cid):
+    n = n_dp * n_exp
+    parts = pl.pallas_call(
+        functools.partial(spread_kernel, n_dp, n_exp),
+        out_shape=jax.ShapeDtypeStruct((n, 8, 128), jnp.float32),
+        in_specs=[pl.BlockSpec(memory_space=pltpu.VMEM)],
+        out_specs=pl.BlockSpec(memory_space=pltpu.VMEM),
+        scratch_shapes=[pltpu.SemaphoreType.DMA((n,)), pltpu.SemaphoreType.DMA((n,))],
+        compiler_params=pltpu.CompilerParams(collective_id=cid, has_side_effects=True),
+        name="sum_everywhere",
+    )(jnp.full((8, 128), value, jnp.float32))
+    return jnp.sum(parts[:, 0, 0])
+
+
+def swap_rows(x, n_dp):
+    if n_dp != 2:
+        return lax.all_gather(x, "dp", axis=0, tiled=True)
+    other = lax.ppermute(x, "dp", [(0, 1), (1, 0)])
+    first = lax.axis_index("dp") == 0
+    return jnp.concatenate([jnp.where(first, x, other), jnp.where(first, other, x)], axis=0)
+
+
+def halve_rows(x, n_dp):
+    if n_dp != 2:
+        return lax.psum_scatter(x, "dp", scatter_dimension=0, tiled=True).astype(jnp.float32)
+    rows = x.shape[0] // 2
+    first = lax.axis_index("dp") == 0
+    top, bottom = x[:rows], x[rows:]
+    other = lax.ppermute(jnp.where(first, bottom, top), "dp", [(0, 1), (1, 0)])
+    return jnp.where(first, top, bottom).astype(jnp.float32) + other.astype(jnp.float32)
 
 
 def local(
@@ -128,17 +570,19 @@
     unit = w_shared_down.shape[0]
     my_expert = lax.axis_index("expert")
 
-    small = jnp.concatenate([w_router, norm_gains.T], axis=1).astype(low)
-    qkv_full = lax.all_gather(w_qkv.astype(low), both, axis=0, tiled=True)
-    small_full = lax.all_gather(small, both, axis=0, tiled=True)
-    out_full = lax.all_gather(w_out.astype(low), both, axis=0, tiled=True)
+    pad = jnp.zeros((rows_w, 128 - expert_count - 2), wide)
+    packed = jnp.concatenate([w_qkv, w_out, w_router, norm_gains.T, pad], axis=1).astype(low)
+    full = gather(packed, n_dp, n_exp, True, 1).reshape(D, -1)
+    qkv_full = full[:, : 3 * H * HD]
+    out_full = full[:, 3 * H * HD : 3 * H * HD + D]
+    small_full = full[:, 3 * H * HD + D :]
     router_full = small_full[:, :expert_count]
     gain_one = small_full[:, expert_count].astype(wide)
     gain_two = small_full[:, expert_count + 1].astype(wide)
     cot_all = lax.all_gather(cotangent, "expert", axis=0, tiled=False)
     routes_all = lax.all_gather(routes, "expert", axis=0, tiled=False)
-    expert_in_full = lax.all_gather(w_expert_in[0].astype(low), "dp", axis=0, tiled=True)
-    expert_down_full = lax.all_gather(w_expert_down[0].astype(low), "dp", axis=0, tiled=True)
+    expert_in_full = swap_rows(w_expert_in[0].astype(low), n_dp)
+    expert_down_full = swap_rows(w_expert_down[0].astype(low), n_dp)
     shin_send = (
         w_shared_in.astype(low)
         .reshape(rows_w, 2, n_dp, n_exp, unit)
@@ -178,7 +622,7 @@
     logits = jnp.dot(mlp_in, router_full, preferred_element_type=wide)
     router_probs = jax.nn.softmax(logits, axis=-1)
 
-    mlp_all = lax.all_gather(mlp_in, "expert", axis=0, tiled=False)
+    mlp_all = gather(mlp_in, n_dp, n_exp, False, 2, ("ABC", "ABC", "ABC", "ABC", "BAC"))
     mlp_flat = mlp_all.reshape(n_exp * row_count, D)
     fused_w = jnp.concatenate([shin_mine, router_full], axis=1)
     fused = jnp.dot(mlp_flat, fused_w, preferred_element_type=wide)
@@ -209,8 +653,8 @@
     mixed_part = mixed_part.reshape(-1, D) + jnp.dot(
         shared_act, shdown_mine, preferred_element_type=wide
     )
-    mixed_sum = lax.psum_scatter(
-        mixed_part.astype(low), "expert", scatter_dimension=0, tiled=True
+    mixed_sum = reduce_scatter(
+        mixed_part.astype(low).reshape(n_exp, row_count, D), n_dp, n_exp, False, 3, ("CBA", "CBA")
     )
     mixed = (residual + mixed_sum.astype(wide)).astype(low)
 
@@ -240,7 +684,9 @@
     back_part = back_part.reshape(-1, D) + jnp.einsum(
         "tf,df->td", shared_gu_grad, shin_mine, preferred_element_type=wide
     )
-    back_sum = lax.psum_scatter(back_part.astype(low), "expert", scatter_dimension=0, tiled=True)
+    back_sum = reduce_scatter(
+        back_part.astype(low).reshape(n_exp, row_count, D), n_dp, n_exp, False, 4, ("CBA", "CBA")
+    )
     gate_grad_tok = jnp.sum(jnp.where(pick_mask, gate_grad, 0.0), axis=1)
     prob_grad = lax.all_to_all(gate_grad_tok, "expert", 0, 0, tiled=True).T
     logit_grad = (
@@ -290,9 +736,12 @@
     )
 
     small_grad = jnp.concatenate(
-        [grad_router, grad_gain_one[:, None], grad_gain_two[:, None]], axis=1
-    )
-    small_own = lax.psum_scatter(small_grad, both, scatter_dimension=0, tiled=True)
+        [grad_router, grad_gain_one[:, None], grad_gain_two[:, None], jnp.zeros((D, 128 - expert_count - 2), wide)],
+        axis=1,
+    )
+    dense_grad = jnp.concatenate([grad_qkv.astype(low), grad_out.astype(low), small_grad.astype(low)], axis=1)
+    dense_own = reduce_scatter(dense_grad.reshape(n_all, rows_w, -1), n_dp, n_exp, True, 5)
+    small_own = dense_own[:, 3 * H * HD + D :]
     shin_back = lax.all_to_all(
         grad_shin.astype(low).reshape(n_all, rows_w, 2 * half), both, 0, 0, tiled=True
     )
@@ -301,21 +750,17 @@
     )
     shin_own = shin_own.transpose(1, 2, 3, 0, 4).reshape(rows_w, 2 * FF)
     owned_grads = (
-        small_own[:, expert_count:].T,
-        lax.psum_scatter(grad_qkv.astype(low), both, scatter_dimension=0, tiled=True).astype(wide),
-        lax.psum_scatter(grad_out.astype(low), both, scatter_dimension=0, tiled=True).astype(wide),
+        small_own[:, expert_count : expert_count + 2].T,
+        dense_own[:, : 3 * H * HD],
+        dense_own[:, 3 * H * HD : 3 * H * HD + D],
         shin_own,
         lax.psum_scatter(grad_shdown, "dp", scatter_dimension=0, tiled=True),
         small_own[:, :expert_count],
-        lax.psum_scatter(
-            grad_ein[None].astype(low), "dp", scatter_dimension=1, tiled=True
-        ).astype(wide),
-        lax.psum_scatter(
-            grad_edown[None].astype(low), "dp", scatter_dimension=1, tiled=True
-        ).astype(wide),
+        halve_rows(grad_ein.astype(low), n_dp)[None],
+        halve_rows(grad_edown.astype(low), n_dp)[None],
     )
     squares = sum((jnp.sum(grad_part * grad_part) for grad_part in owned_grads))
-    total_squares = lax.psum(squares, ("dp", "expert"))
+    total_squares = sum_everywhere(squares, n_dp, n_exp, 6)
     grad_norm = jnp.sqrt(total_squares)
     factor = jnp.minimum(1.0, CLIP / grad_norm)
     weights = (

time: 1560 us -> 1130 us (0.72)
  waiting for transfers between devices: 956 us -> 0.7 us
  Pallas kernels: 0 us -> 543 us
  blocking collectives: 127 us -> 37.3 us
  local copies, waits for them, and re-layouts: 26.3 us -> 66.7 us
  starting transfers between devices: 17.3 us -> 44.5 us
  other arithmetic: 96 us -> 116 us
    pallas_call x0 -> x6, Pallas kernels: none -> 543 us  [the longest x3 333 us: reduce_scatter(): pl.pallas_call(functools.partial(reduce_kernel, n_dp, n_exp, orders, slic...]
    reduce_scatter x6 -> x0, waiting for transfers between devices: 512 us -> none  [the longest x1 157 us: local(): lax.psum_scatter(mixed_part.astype(low), 'expert', scatter_dimension=0, t...]
    all_gather x5 -> x0, waiting for transfers between devices: 235 us -> none  [the longest x1 109 us: local(): mlp_all = lax.all_gather(mlp_in, 'expert', axis=0, tiled=False)]
    unnamed x15 -> x2, waiting for transfers between devices: 125 us -> 0.68 us
    all_gather x1, waiting for transfers between devices: 76.8 us -> 0.01 us  [local(): cot_all = lax.all_gather(cotangent, 'expert', axis=0, tiled=False)]
    all_gather x1 -> x0, blocking collectives: 44.2 us -> none  [local(): small_full = lax.all_gather(small, both, axis=0, tiled=True)]
    psum x1 -> x0, blocking collectives: 40 us -> none  [local(): total_squares = lax.psum(squares, ('dp', 'expert'))]
    all_to_all x1, starting transfers between devices: 4.33 us -> 25.1 us  [local(): lax.all_to_all(grad_shin.astype(low).reshape(n_all, rows_w, 2 * half), bo...]
  transfers between devices with their start and end apart: 17 -> 9, of which waited for: 13 -> 0; matrix products, arithmetic and copies ran while one was open for 18% -> 26% of each run, Pallas kernels for 0% -> 46%
where the time goes in v2:
time: 1130 us
  Pallas kernels  543 us (48%)
  matrix products  296 us (26%)
  other arithmetic  116 us (10%)
  local copies, waits for them, and re-layouts  66.7 us (6%)
  starting transfers between devices  44.5 us (4%)
  blocking collectives  37.3 us (3%)
  between operations  23.2 us (2%)
    pallas_call x3, Pallas kernels, reduce_scatter(): pl.pallas_call(functools.partial(reduce_kernel, n_dp, n_exp, orders, slic...  333 us
    pallas_call x2, Pallas kernels, gather(): pl.pallas_call(functools.partial(gather_kernel, n_dp, n_exp, orders, slic...  191 us
    sub x8, other arithmetic, adam_update(): weight - step_rate * (first_hat / (jnp.sqrt(second_hat) + ADAM_EPS) + dec...  25.9 us
    all_to_all x1, starting transfers between devices, local(): lax.all_to_all(grad_shin.astype(low).reshape(n_all, rows_w, 2 * half), bo...  25.1 us
    all_gather x1, blocking collectives, local(): routes_all = lax.all_gather(routes, 'expert', axis=0, tiled=False)  23.2 us
  transfers between devices with their start and end apart: 9, of which 0 were waited for; matrix products, arithmetic and copies ran while one was open for 26% of the time, Pallas kernels for 46%

profile of v2, /device:TPU:0, one launch (start us, length us, event | category | flops | bytes accessed | tf_op | source)
XLA Modules:
  0.0 1126.8 jit_solution(1418342652629779931)
XLA Ops:
  29.1 23.2 %all-gather = s32[6144,6]{0,1:T(8,128)S(1)} all-gather(s32[384,6]{0,1:T(8,128)S(1)} %copy-done.64), channel_id=2, replica_groups=mesh['dp'=2,'expert'=16] {'expert'}, dimensions={0}, use_global_device_ids=true | all-gather | bytes 156672 | tf_op jit(solution)/shard_map/all_gather | solution.py:583
  54.6 106.0 %gather_dense.1 = bf16[32,40,5248]{2,1,0:T(8,128)(2,1)} custom-call(bf16[40,5248]{1,0:T(8,128)(2,1)} %concatenate.48.x_ref), custom_call_target="tpu_custom_call" | custom-call | tf_op jit(solution)/shard_map/gather_dense/pallas_call | solution.py:276
  167.8 8.2 fusion.10
  197.3 85.3 %gather_group.1 = bf16[16,384,1280]{2,1,0:T(8,128)(2,1)} custom-call(bf16[384,1280]{1,0:T(8,128)(2,1)} %multiply_convert_fusion.4.x_ref), custom_call_target="tpu_custom_call" | custom-call | tf_op jit(solution)/shard_map/gather_group/pallas_call | solution.py:276
  282.9 12.6 %convolution_convert_fusion.6 = bf16[16,184,1280]{2,1,0:T(8,128)(2,1)} fusion(bf16[16,384,1280]{2,1,0:T(8,128)(2,1)} %gather_group.1, s32[16,384]{1,0:T(8,128)S(1)} %copy_bitcast_fusion, pred[16,384]{1,0:T(8,128)(4,1)S(1)} %reshape.311), kind=kOutput, calls=%fused_computation.28 | convolution fusion | flops 2900099072 | bytes 23296000 | tf_op jit(solution)/shard_map/nst,ntd->nsd/dot_general | solution.py:640
  311.4 12.6 %fusion.88 = f32[6144,128]{0,1:T(8,128)} fusion(bf16[6144,1280]{1,0:T(8,128)(2,1)} %bitcast.174, bf16[1280,16]{1,0:T(8,128)(2,1)} %slice.150, bf16[1280,112]{1,0:T(8,128)(2,1)} %bitcast.14), kind=kOutput, calls=%fused_computation.165 | convolution fusion | flops 2013921280 | bytes 19202048 | tf_op jit(solution)/shard_map/dot_general | solution.py:628
  334.2 18.2 %fusion.23 = f32[2944,1792]{0,1:T(8,128)} fusion(bf16[2944,1280]{1,0:T(8,128)(2,1)S(1)} %bitcast.186, bf16[640,1792]{1,0:T(8,128)(2,1)S(1)} %get-tuple-element.233, bf16[640,1792]{1,0:T(8,128)(2,1)S(1)} %get-tuple-element.232), kind=kOutput, calls=%fused_computation.52 | convolution fusion | flops 13514833920 | bytes 33226752 | tf_op jit(solution)/shard_map/dot_general | solution.py:645
  352.4 10.9 multiply_convert_fusion.2
  363.3 9.6 convolution_convert_fusion.5
  372.9 16.1 %fusion.6 = (f32[2944]{0:T(1024)S(1)}, bf16[2944,1280]{1,0:T(8,128)(2,1)}) fusion(bf16[16,184,1280]{2,1,0:T(8,128)(2,1)S(1)} %convolution_convert_fusion.5, bf16[2944,896]{0,1:T(8,128)(2,1)} %multiply_convert_fusion.2, bf16[448,1280]{1,0:T(8,128)(2,1)} %get-tuple-element.238, bf16[448,1280]{1,0:T(8,128)(2,1)S(1)} %copy-done.33), kind=kOutput, calls=%fused_computation.11 | convolution fusion | flops 6776255488 | bytes 22654464 | tf_op jit(solution)/shard_map/dot_general | solution.py:647
  391.5 11.5 %fusion.5 = (bf16[2944,1280]{1,0:T(8,128)(2,1)}, bf16[2944,1280]{1,0:T(8,128)(2,1)}) fusion(bf16[16,184,1280]{2,1,0:T(8,128)(2,1)} %copy-done, f32[2944]{0:T(1024)S(1)} %mul.646, bf16[2944,1280]{1,0:T(8,128)(2,1)} %get-tuple-element.268), kind=kLoop, calls=%fused_computation.10 | loop fusion | flops 22609920 | bytes 30158336 | tf_op jit(solution)/shard_map/convert_element_type | solution.py:672
  403.1 18.3 %multiply_convert_fusion.1 = (bf16[2944,896]{0,1:T(8,128)(2,1)}, bf16[2944,896]{0,1:T(8,128)(2,1)}) fusion(f32[2944,1792]{0,1:T(8,128)} %fusion.23, bf16[2944,1280]{1,0:T(8,128)(2,1)} %get-tuple-element.259, bf16[448,1280]{1,0:T(8,128)(2,1)S(1)} %copy-done.34, bf16[448,1280]{1,0:T(8,128)(2,1)S(1)} %copy-done.33), kind=kOutput, calls=%fused_computation.16 | convolution fusion | flops 6791708672 | bytes 41484288 | tf_op jit(solution)/shard_map/rd,fd->rf/dot_general | solution.py:674
  421.4 12.8 %convolution_convert_fusion.7 = bf16[896,1280]{1,0:T(8,128)(2,1)} fusion(bf16[2944,896]{0,1:T(8,128)(2,1)} %multiply_convert_fusion.2, bf16[2944,1280]{1,0:T(8,128)(2,1)} %get-tuple-element.259), kind=kOutput, calls=%fused_computation.48 | convolution fusion | flops 6753976320 | bytes 15106048 | tf_op jit(solution)/shard_map/rf,rd->fd/dot_general | solution.py:673
  434.2 21.2 %convolution_convert_fusion.3 = bf16[1280,1792]{1,0:T(8,128)(2,1)} fusion(bf16[2944,1280]{1,0:T(8,128)(2,1)} %bitcast.183, bf16[2944,896]{0,1:T(8,128)(2,1)} %get-tuple-element.225, bf16[2944,896]{0,1:T(8,128)(2,1)} %get-tuple-element.224), kind=kOutput, calls=%fused_computation.24 | convolution fusion | flops 13529055232 | bytes 22675456 | tf_op jit(solution)/shard_map/rd,rf->df/dot_general | solution.py:678
  455.4 21.1 %convolution_convert_fusion.1 = bf16[2944,1280]{1,0:T(8,128)(2,1)} fusion(bf16[2944,896]{0,1:T(8,128)(2,1)} %get-tuple-element.225, bf16[2944,896]{0,1:T(8,128)(2,1)} %get-tuple-element.224, bf16[640,1792]{1,0:T(8,128)(2,1)} %copy-done.31, bf16[640,1792]{1,0:T(8,128)(2,1)} %copy-done.30), kind=kOutput, calls=%fused_computation.12 | convolution fusion | flops 13539704832 | bytes 22675456 | tf_op jit(solution)/shard_map/rf,df->rd/dot_general | solution.py:679
  476.5 11.4 %multiply_convert_fusion.6 = (bf16[6144,56]{0,1:T(8,128)(2,1)}, bf16[6144,56]{0,1:T(8,128)(2,1)}, bf16[6144,56]{0,1:T(8,128)(2,1)S(1)}) fusion(f32[6144,128]{0,1:T(8,128)S(1)} %copy-done.8, bf16[6144,1280]{1,0:T(8,128)(2,1)} %all-gather.5.cloned.1.call-done, bf16[56,1280]{1,0:T(8,128)(2,1)S(1)} %copy-done.49), kind=kOutput, calls=%fused_computation.130 | convolution fusion | flops 885964800 | bytes 20688896 | tf_op jit(solution)/shard_map/td,fd->tf/dot_general | solution.py:663
  488.7 8.2 fusion.137
  497.0 8.6 fusion
  508.8 8.2 convolution_convert_fusion.8
  530.3 15.1 %fusion.18 = f32[16,384,1280]{2,1,0:T(8,128)} fusion(bf16[16,184,1280]{2,1,0:T(8,128)(2,1)} %bitcast.182, s32[16,384]{1,0:T(8,128)S(1)} %copy-done.29, pred[16,384]{1,0:T(8,128)(4,1)S(1)} %copy-done.42), kind=kOutput, calls=%fused_computation.45 | convolution fusion | flops 2896330752 | bytes 39024640 | tf_op jit(solution)/shard_map/nst,nsd->ntd/dot_general | solution.py:652
  545.4 18.0 %fusion.3 = bf16[6144,1280]{1,0:T(8,128)(2,1)} fusion(f32[16,384,1280]{2,1,0:T(8,128)} %fusion.18, bf16[6144,56]{0,1:T(8,128)(2,1)S(1)} %copy-done.16, bf16[56,1280]{1,0:T(8,128)(2,1)S(1)} %copy-done.49), kind=kOutput, calls=%fused_computation.4 | convolution fusion | flops 896532480 | bytes 48017408 | tf_op jit(solution)/shard_map/dot_general | solution.py:653
  563.4 12.6 %fusion.15 = f32[16,384,1280]{2,1,0:T(8,128)} fusion(bf16[16,184,1280]{2,1,0:T(8,128)(2,1)S(1)} %bitcast.203, s32[16,384]{1,0:T(8,128)S(1)} %copy-done.29, pred[16,384]{1,0:T(8,128)(4,1)S(1)} %copy-done.42), kind=kOutput, calls=%fused_computation.44 | convolution fusion | flops 2896330752 | bytes 39024640 | tf_op jit(solution)/shard_map/nst,nsd->ntd/dot_general | solution.py:683
  576.0 18.0 %fusion.2 = bf16[6144,1280]{1,0:T(8,128)(2,1)} fusion(f32[16,384,1280]{2,1,0:T(8,128)} %fusion.15, bf16[1280,112]{1,0:T(8,128)(2,1)} %bitcast.14, bf16[6144,56]{0,1:T(8,128)(2,1)S(1)} %copy-done.25, bf16[6144,56]{0,1:T(8,128)(2,1)S(1)} %copy-done.24), kind=kOutput, calls=%fused_computation.2 | convolution fusion | flops 1780088832 | bytes 48848896 | tf_op jit(solution)/shard_map/tf,df->td/dot_general | solution.py:684
  594.0 110.5 %reduce_group.2 = f32[384,1280]{1,0:T(8,128)} custom-call(bf16[16,384,1280]{2,1,0:T(8,128)(2,1)} %bitcast.177), custom_call_target="tpu_custom_call" | custom-call | tf_op jit(solution)/shard_map/reduce_group/pallas_call | solution.py:449
  704.6 129.8 %reduce_group.3 = f32[384,1280]{1,0:T(8,128)} custom-call(bf16[16,384,1280]{2,1,0:T(8,128)(2,1)} %bitcast.178), custom_call_target="tpu_custom_call" | custom-call | tf_op jit(solution)/shard_map/reduce_group/pallas_call | solution.py:449
  836.0 25.1 %all-to-all-start.2 = ((bf16[32,40,112]{2,1,0:T(8,128)(2,1)}), bf16[32,40,112]{2,1,0:T(8,128)(2,1)}, u32[]{:S(2)}, u32[]{:S(2)}) async-start(bf16[32,40,112]{2,1,0:T(8,128)(2,1)} %bitcast.213), calls=%async_computation.2 | async-start | bytes 655360 | tf_op jit(solution)/shard_map/all_to_all | solution.py:745
  889.4 7.6 fusion.53
  897.0 10.2 convolution_convert_fusion
  915.9 19.3 %concatenate.61 = bf16[1280,5248]{1,0:T(8,128)(2,1)} concatenate(bf16[1280,3840]{1,0:T(8,128)(2,1)} %convolution_convert_fusion, bf16[1280,1280]{1,0:T(8,128)(2,1)} %convolution_convert_fusion.4, bf16[1280,16]{1,0:T(8,128)(2,1)} %copy.279, bf16[1280,1]{1,0:T(8,128)(2,1)} %broadcast_in_dim.140, bf16[1280,1]{1,0:T(8,128)(2,1)} %broadcast_in_dim.141, ...), dimensions={1} | concatenate | bytes 26869760 | tf_op jit(solution)/shard_map/concatenate | solution.py:742
  935.2 92.2 %reduce_dense.1 = f32[40,5248]{1,0:T(8,128)} custom-call(bf16[32,40,5248]{2,1,0:T(8,128)(2,1)} %bitcast.179), custom_call_target="tpu_custom_call" | custom-call | tf_op jit(solution)/shard_map/reduce_dense/pallas_call | solution.py:449
  1063.7 18.6 %sum_everywhere.1 = f32[32,8,128]{2,1,0:T(8,128)} custom-call(f32[8,128]{1,0:T(8,128)} %broadcast_in_dim.139.x_ref), custom_call_target="tpu_custom_call" | custom-call | tf_op jit(solution)/shard_map/sum_everywhere/pallas_call | solution.py:499
  1110.9 7.7 multiply_subtract_fusion
  (342 shorter events, 195.0 us)
Async XLA Ops:
  7.2 356.1 %all-gather.5.cloned.1.call-start = ((), (), s32[]{:S(2)}) async-start(), calls=%async_computation.3 | async-start | bytes 16711680 | tf_op jit(solution)/shard_map/all_gather | solution.py:582
  14.2 297.2 %all-to-all-start = ((bf16[32,40,112]{2,1,0:T(8,128)(2,1)}), bf16[32,40,112]{2,1,0:T(8,128)(2,1)}, u32[]{:S(2)}, u32[]{:S(2)}) async-start(bf16[32,40,112]{2,1,0:T(8,128)(2,1)} %pad_maximum_fusion.13), calls=%async_computation | async-start | bytes 655360 | tf_op jit(solution)/shard_map/all_to_all | solution.py:593
  22.8 29.6 %copy-start.74 = (s32[1,4]{1,0:T(1,128)S(1)}, s32[1,4]{1,0:T(1,128)}, u32[]{:S(2)}) copy-start(s32[1,4]{1,0:T(1,128)} %param.29) | copy-start | bytes 52
  22.8 30.9 %copy-start.26 = (f32[40,3840]{1,0:T(8,128)S(1)}, f32[40,3840]{1,0:T(8,128)}, u32[]{:S(2)}) copy-start(f32[40,3840]{1,0:T(8,128)} %param.35) | copy-start | bytes 1843204
  22.8 304.5 %collective-permute-start.1 = (bf16[448,1280]{1,0:T(8,128)(2,1)}, bf16[448,1280]{1,0:T(8,128)(2,1)}, u32[]{:S(2)}, u32[]{:S(2)}) collective-permute-start(bf16[448,1280]{1,0:T(8,128)(2,1)} %convert_bitcast_fusion.1), channel_id=1, source_target_pairs={{0,16},{16,0},{1,17},{17,1},{2,18},{18,2},{3,19},{19,3},{4,20},{20... | collective-permute-start | bytes 3440648 | tf_op jit(solution)/shard_map/ppermute | solution.py:514
  28.5 301.8 %collective-permute-start = (bf16[640,1792]{1,0:T(8,128)(2,1)}, bf16[640,1792]{1,0:T(8,128)(2,1)}, u32[]{:S(2)}, u32[]{:S(2)}) collective-permute-start(bf16[640,1792]{1,0:T(8,128)(2,1)} %convert_bitcast_fusion), channel_id=1, source_target_pairs={{0,16},{16,0},{1,17},{17,1},{2,18},{18,2},{3,19},{19,3},{4,20},{20... | collective-permute-start | bytes 6881288 | tf_op jit(solution)/shard_map/ppermute | solution.py:514
  52.4 336.7 %copy-start.41 = (pred[16,384]{1,0:T(8,128)(4,1)}, pred[16,384]{1,0:T(8,128)(4,1)S(1)}, u32[]{:S(2)}) copy-start(pred[16,384]{1,0:T(8,128)(4,1)S(1)} %reshape.311) | copy-start | bytes 18436
  165.3 29.6 %copy-start.50 = (f32[1280]{0:T(1024)}, f32[1280]{0:T(1024)S(1)}, u32[]{:S(2)}) copy-start(f32[1280]{0:T(1024)S(1)} %convert_reduce_fusion.1) | copy-start | bytes 15364
  194.9 87.8 %copy-start.60 = (f32[384]{0:T(512)}, f32[384]{0:T(512)S(1)}, u32[]{:S(2)}) copy-start(f32[384]{0:T(512)S(1)} %add_rsqrt_fusion) | copy-start | bytes 4612
  197.3 85.4 %copy-start.71 = (f32[2,40]{1,0:T(2,128)S(1)}, f32[2,40]{1,0:T(2,128)}, u32[]{:S(2)}) copy-start(f32[2,40]{1,0:T(2,128)} %param.33) | copy-start | bytes 964
  197.3 85.5 %copy-start.45 = (f32[28,1280]{1,0:T(8,128)S(1)}, f32[28,1280]{1,0:T(8,128)}, u32[]{:S(2)}) copy-start(f32[28,1280]{1,0:T(8,128)} %param.44) | copy-start | bytes 430084
  282.8 106.3 %copy-start.28 = (s32[16,384]{1,0:T(8,128)}, s32[16,384]{1,0:T(8,128)S(1)}, u32[]{:S(2)}) copy-start(s32[16,384]{1,0:T(8,128)S(1)} %copy_bitcast_fusion) | copy-start | bytes 73732
  282.9 19.0 %copy-start.68 = (f32[40,16]{0,1:T(8,128)S(1)}, f32[40,16]{0,1:T(8,128)}, u32[]{:S(2)}) copy-start(f32[40,16]{0,1:T(8,128)} %param.49) | copy-start | bytes 7684
  282.9 25.9 %copy-start.5 = (bf16[384,1280]{1,0:T(8,128)(2,1)S(1)}, bf16[384,1280]{1,0:T(8,128)(2,1)}, u32[]{:S(2)}) copy-start(bf16[384,1280]{1,0:T(8,128)(2,1)} %multiply_convert_fusion.4.x_ref) | copy-start | bytes 2949124
  333.8 18.6 %copy-start.30 = (bf16[640,1792]{1,0:T(8,128)(2,1)}, bf16[640,1792]{1,0:T(8,128)(2,1)S(1)}, u32[]{:S(2)}) copy-start(bf16[640,1792]{1,0:T(8,128)(2,1)S(1)} %get-tuple-element.232) | copy-start | bytes 6881284
  333.8 18.5 %copy-start.31 = (bf16[640,1792]{1,0:T(8,128)(2,1)}, bf16[640,1792]{1,0:T(8,128)(2,1)S(1)}, u32[]{:S(2)}) copy-start(bf16[640,1792]{1,0:T(8,128)(2,1)S(1)} %get-tuple-element.233) | copy-start | bytes 6881284
  455.4 21.1 %copy-start.8 = (f32[6144,128]{0,1:T(8,128)S(1)}, f32[6144,128]{0,1:T(8,128)}, u32[]{:S(2)}) copy-start(f32[6144,128]{0,1:T(8,128)} %fusion.88) | copy-start | bytes 9437188
  455.4 21.1 %copy-start.49 = (bf16[56,1280]{1,0:T(8,128)(2,1)S(1)}, bf16[56,1280]{1,0:T(8,128)(2,1)}, u32[]{:S(2)}) copy-start(bf16[56,1280]{1,0:T(8,128)(2,1)} %reshape.314) | copy-start | bytes 430084
  488.7 20.0 %copy-start.23 = (bf16[6144,56]{0,1:T(8,128)(2,1)S(1)}, bf16[6144,56]{0,1:T(8,128)(2,1)}, u32[]{:S(2)}) copy-start(bf16[6144,56]{0,1:T(8,128)(2,1)} %get-tuple-element.234) | copy-start | bytes 2064388
  505.6 328.8 %collective-permute-start.4 = (f32[4,1280]{1,0:T(4,128)S(1)}, f32[4,1280]{1,0:T(4,128)}, u32[]{:S(2)}, u32[]{:S(2)}) collective-permute-start(f32[4,1280]{1,0:T(4,128)S(1)} %slice.164), channel_id=1, source_target_pairs={{0,16},{1,17},{2,18},{3,19},{4,20},{5,21},{6,22},{7,23},{8,24},{9,... | collective-permute-start | bytes 61448
  518.5 317.5 %all-to-all-start.1 = ((f32[16,1,384]{2,1,0:T(1,128)}), f32[16,1,384]{2,1,0:T(1,128)S(1)}, u32[]{:S(2)}, u32[]{:S(2)}) async-start(f32[16,1,384]{2,1,0:T(1,128)} %all_to_all.15), calls=%async_computation.1 | async-start | bytes 49152 | tf_op jit(solution)/shard_map/all_to_all | solution.py:691
  524.3 527.6 %collective-permute-start.3 = (bf16[448,1280]{1,0:T(8,128)(2,1)}, bf16[448,1280]{1,0:T(8,128)(2,1)S(1)}, u32[]{:S(2)}, u32[]{:S(2)}) collective-permute-start(bf16[448,1280]{1,0:T(8,128)(2,1)} %broadcast_select_fusion.4), channel_id=1, source_target_pairs={{0,16},{16,0},{1,17},{17,1},{2,18},{18,2},{3,19},{19,3},{4,20},{20... | collective-permute-start | bytes 3440648 | tf_op jit(solution)/shard_map/ppermute | solution.py:525
  528.3 527.4 %collective-permute-start.2 = (bf16[640,1792]{1,0:T(8,128)(2,1)}, bf16[640,1792]{1,0:T(8,128)(2,1)}, u32[]{:S(2)}, u32[]{:S(2)}) collective-permute-start(bf16[640,1792]{1,0:T(8,128)(2,1)} %broadcast_select_fusion), channel_id=1, source_target_pairs={{0,16},{16,0},{1,17},{17,1},{2,18},{18,2},{3,19},{19,3},{4,20},{20... | collective-permute-start | bytes 6881288 | tf_op jit(solution)/shard_map/ppermute | solution.py:525
  530.3 33.1 %slice-start.8 = ((s8[7536640]{0:T(1024)(128)(4,1)}), s8[4194304]{0:T(1024)(128)(4,1)S(1)}, s32[]{:S(2)}) async-start(s8[7536640]{0:T(1024)(128)(4,1)} %bitcast.201), calls=%async_computation.12 | async-start | bytes 8388608
  704.5 129.9 %copy-start.44 = (f32[32,1280]{1,0:T(8,128)S(1)}, f32[32,1280]{1,0:T(8,128)}, u32[]{:S(2)}) copy-start(f32[32,1280]{1,0:T(8,128)} %copy-done.43) | copy-start | bytes 491524
  704.5 156.6 %copy-start.48 = (f32[384,16]{0,1:T(8,128)S(1)}, f32[384,16]{0,1:T(8,128)}, u32[]{:S(2)}) copy-start(f32[384,16]{0,1:T(8,128)} %copy-done.47) | copy-start | bytes 73732
  704.6 156.6 %copy-start.55 = (f32[384]{0:T(512)S(1)}, f32[384]{0:T(512)}, u32[]{:S(2)}) copy-start(f32[384]{0:T(512)} %copy-done.54) | copy-start | bytes 4612
  704.6 156.6 %copy-start.56 = (f32[384]{0:T(512)S(1)}, f32[384]{0:T(512)}, u32[]{:S(2)}) copy-start(f32[384]{0:T(512)} %fusion.102) | copy-start | bytes 4612
  704.6 156.6 %copy-start.4 = (f32[384,1280]{1,0:T(8,128)S(1)}, f32[384,1280]{1,0:T(8,128)}, u32[]{:S(2)}) copy-start(f32[384,1280]{1,0:T(8,128)} %copy-done.3) | copy-start | bytes 5898244
  704.6 156.6 %copy-start.51 = (f32[1280]{0:T(1024)S(1)}, f32[1280]{0:T(1024)}, u32[]{:S(2)}) copy-start(f32[1280]{0:T(1024)} %copy-done.50) | copy-start | bytes 15364
  704.6 156.6 %copy-start.61 = (f32[384]{0:T(512)S(1)}, f32[384]{0:T(512)}, u32[]{:S(2)}) copy-start(f32[384]{0:T(512)} %copy-done.60) | copy-start | bytes 4612
  836.0 203.2 %all-to-all-start.2 = ((bf16[32,40,112]{2,1,0:T(8,128)(2,1)}), bf16[32,40,112]{2,1,0:T(8,128)(2,1)}, u32[]{:S(2)}, u32[]{:S(2)}) async-start(bf16[32,40,112]{2,1,0:T(8,128)(2,1)} %bitcast.213), calls=%async_computation.2 | async-start | bytes 655360 | tf_op jit(solution)/shard_map/all_to_all | solution.py:745
  (69 other events, 483.2 us)
Sparse Core Ops, SparseCore 0:
  10.3 159.3 all-gather.4

commit v3 on v2

--- a/solution.py
+++ b/solution.py
@@ -311,7 +311,7 @@
     return slots
 
 
-def reduce_body(place, orders, slices, g_ref, block_of, land, base, send_sem, recv_sem, finish):
+def reduce_body(place, orders, slices, g_refs, block_of, land, base, send_sem, recv_sem, finish):
     size = place.size
     tables = [stage_slots(size, order) for order in orders]
     sends = []
@@ -349,17 +349,17 @@
         return sorted(items, key=lambda r: tuple(0 if (isinstance(v, int) and v) else 1 for v in r[:-1]))
 
     for part, order in enumerate(orders):
-        lo, w = slices[part]
+        g_ref, lo, w = g_refs[slices[part][0]], slices[part][1], slices[part][2]
         axis = order[0]
         for t in range(1, size[axis]):
             for r in far_first(rests(order, 1)):
-                def src(order=order, t=t, r=r, lo=lo, w=w):
+                def src(order=order, t=t, r=r, lo=lo, w=w, g_ref=g_ref):
                     return g_ref.at[block_of(target(order, 0, t, r)), :, pl.ds(lo, w)]
                 send([], part, src, tables[part][(0, t, r)], lambda axis=axis, t=t: place.moved(**{axis: t}))
     for i in range(1, len(orders[0])):
         for pick in far_first(rests(orders[0], i)):
             for part, order in enumerate(orders):
-                lo, w = slices[part]
+                g_ref, lo, w = g_refs[slices[part][0]], slices[part][1], slices[part][2]
                 axis = order[i]
                 before = order[i - 1]
                 r = pick
@@ -421,7 +421,8 @@
     return total
 
 
-def reduce_kernel(n_dp, n_exp, orders, slices, dense, g_ref, out_ref, *scratch):
+def reduce_kernel(n_dp, n_exp, orders, slices, dense, arrays, *refs):
+    g_refs, out_refs, scratch = refs[:arrays], refs[arrays:2 * arrays], refs[2 * arrays:]
     land, (send_sem, recv_sem) = scratch[:-2], scratch[-2:]
     place = Place(n_dp, n_exp)
     place.greet(orders[0], True)
@@ -430,34 +431,464 @@
         base.append(base[-1] + len(stage_slots(place.size, order)))
 
     def finish(part, total):
-        lo, w = slices[part]
-        out_ref[:, lo:lo + w] = total.astype(out_ref.dtype)
-
-    reduce_body(place, orders, slices, g_ref, place.flat if dense else place.expert, land, base, send_sem, recv_sem, finish)
-
-
-def reduce_scatter(g, n_dp, n_exp, dense, cid, orders=None):
+        which, lo, w = slices[part]
+        out_refs[which][:, lo:lo + w] = total
+
+    reduce_body(place, orders, slices, g_refs, place.flat if dense else place.expert, land, base, send_sem, recv_sem, finish)
+
+
+def reduce_dense(arrays, n_dp, n_exp, cid):
     size = sizes(n_dp, n_exp)
-    blocks, rows, cols = g.shape
-    orders = orders or (("CBYA", "CYBA") if dense else ("CBA",))
-    w = cols // 128 // len(orders) * 128
-    slices = tuple((i * w, w if i < len(orders) - 1 else cols - i * w) for i in range(len(orders)))
+    blocks, rows = arrays[0].shape[:2]
+    orders, slices = [], []
+    for which, g in enumerate(arrays):
+        cols = g.shape[2]
+        half = cols // 256 * 128
+        for order, lo, w in (("CBYA", 0, half), ("CYBA", half, cols - half)):
+            if w:
+                orders.append(order)
+                slices.append((which, lo, w))
     slots = [len(stage_slots(size, order)) for order in orders]
-    if (blocks + max(slots)) * ((rows + 15) // 16 * 16) * cols * 2 > 44 * 1024 * 1024:
-        axes = ("dp", "expert") if dense else "expert"
-        return lax.psum_scatter(g, axes, scatter_dimension=0, tiled=False).astype(jnp.float32)
     return pl.pallas_call(
-        functools.partial(reduce_kernel, n_dp, n_exp, orders, slices, dense),
-        out_shape=jax.ShapeDtypeStruct((rows, cols), jnp.float32),
-        in_specs=[pl.BlockSpec(memory_space=pltpu.VMEM)],
-        out_specs=pl.BlockSpec(memory_space=pltpu.VMEM),
-        scratch_shapes=[pltpu.VMEM((k, rows, s[1]), g.dtype) for k, s in zip(slots, slices)] + [
+        functools.partial(reduce_kernel, n_dp, n_exp, orders, slices, True, len(arrays)),
+        out_shape=[jax.ShapeDtypeStruct((rows, g.shape[2]), jnp.float32) for g in arrays],
+        in_specs=[pl.BlockSpec(memory_space=pltpu.VMEM)] * len(arrays),
+        out_specs=[pl.BlockSpec(memory_space=pltpu.VMEM)] * len(arrays),
+        scratch_shapes=[pltpu.VMEM((k, rows, s[2]), g.dtype) for k, s in zip(slots, slices)] + [
             pltpu.SemaphoreType.DMA((count_reduce(size, orders),)),
             pltpu.SemaphoreType.DMA((sum(slots),)),
         ],
         compiler_params=pltpu.CompilerParams(collective_id=cid, has_side_effects=True, vmem_limit_bytes=60 * 1024 * 1024),
-        name="reduce_dense" if dense else "reduce_group",
-    )(g)
+        name="reduce_dense",
+    )(*arrays)
+
+
+def mm(a, b):
+    return jnp.dot(a, b, preferred_element_type=jnp.float32)
+
+
+def mm_nt(a, b):
+    return lax.dot_general(a, b, (((1,), (1,)), ((), ())), preferred_element_type=jnp.float32)
+
+
+def mm_tn(a, b):
+    return lax.dot_general(a, b, (((0,), (0,)), ((), ())), preferred_element_type=jnp.float32)
+
+
+def sig(v):
+    return 1.0 / (1.0 + jnp.exp(-v))
+
+
+def near_first(na):
+    table = []
+    for a in range(na):
+        row = [a]
+        for d in range(1, na):
+            row += [p for p in ((a - d, a + d) if a < na // 2 else (a + d, a - d)) if 0 <= p < na]
+        table.append(row)
+    return table
+
+
+def pair_order(na, nb):
+    order = [(0, 0), (1, 0)] + [(1, t) for t in range(1, nb)]
+    for i in range(2, na):
+        order += [(i, t) for t in range(1, nb)] + [(i, 0)]
+    return order + [(0, t) for t in range(1, nb)]
+
+
+def choose(index, values):
+    out = values[-1]
+    for i in range(len(values) - 1):
+        out = jnp.where(index == i, values[i], out)
+    return out
+
+
+def fused_kernel(n_dp, n_exp, experts, cap, x_ref, cot_ref, rank_ref, win_h, wdown_h, wshin_h, wshdown_h,
+                 xall, mixed, total_out, gg_out, gin_out, gdown_out, gshin, gshdown, core_land, b_land, a_land,
+                 win, wdown, wshin, wshdown, xv, cv, xr_s, act_s, gr_s, dgu_s, back_s, mixed_s, held, bsrc, stage,
+                 gg_s, gin_acc, gdown_acc,
+                 w_sem, x_sem, c_sem, m_sem, s_sem, ag_send, ag_recv, core_send, core_recv, b_send, b_recv,
+                 a_send, a_recv, g_send, g_recv):
+    low, wide = jnp.bfloat16, jnp.float32
+    place = Place(n_dp, n_exp)
+    na, nb = place.size["A"], place.size["B"]
+    pos = place.pos
+    a, c, me = pos["A"], pos["C"], place.expert(pos)
+    toks, d = x_ref.shape
+    hid = wshdown.shape[0]
+    table = near_first(na)
+    order = pair_order(na, nb)
+    steps = len(order)
+    near = [choose(a, [table[p][i] for p in range(na)]) for i in range(na)]
+    sib = dict(pos, C=1 - c)
+
+    def there(i, t, own_plane=True):
+        return dict(pos, A=near[i], B=lax.rem(pos["B"] + t, nb), C=c if own_plane else 1 - c)
+
+    barrier = pltpu.get_barrier_semaphore()
+    for s in range(1, n_exp):
+        pl.semaphore_signal(barrier, inc=1, device_id=(pos["Y"], lax.rem(me + s, n_exp)), device_id_type=MESH)
+    pl.semaphore_wait(barrier, n_exp - 1)
+
+    counter = [0]
+    ag_sends = []
+
+    def ag(conds, src, j, to):
+        at = counter[0]
+        counter[0] += 1
+
+        def copy():
+            return pltpu.make_async_remote_copy(
+                src_ref=src(), dst_ref=xall.at[j()], send_sem=ag_send.at[at], recv_sem=ag_recv.at[j()],
+                device_id=place.device(to()), device_id_type=MESH)
+
+        ag_sends.append((conds, copy))
+        under(conds(), lambda: copy().start())
+
+    def landed(j):
+        pltpu.make_async_copy(xall.at[j], xall.at[j], ag_recv.at[j]).wait()
+
+    def own_block():
+        return x_ref
+
+    def always():
+        return []
+
+    for way in (1, -1):
+        ag(lambda way=way: [place.inside(way)], own_block, lambda: me, lambda way=way: place.moved(A=way))
+    for t in range(1, nb):
+        ag(always, own_block, lambda: me, lambda t=t: place.moved(B=t))
+    ag(always, own_block, lambda: me, lambda: sib)
+
+    def line_arrival(i):
+        def j():
+            return place.expert(there(i, 0))
+
+        def src():
+            return xall.at[j()]
+
+        landed(j())
+        ag(lambda: [near[i] < a, place.inside(1)], src, j, lambda: place.moved(A=1))
+        ag(lambda: [near[i] > a, place.inside(-1)], src, j, lambda: place.moved(A=-1))
+        for t in range(1, nb):
+            ag(always, src, j, lambda t=t: place.moved(B=t))
+        ag(always, src, j, lambda: sib)
+
+    def side_arrival(i):
+        for t in range(1, nb):
+            def j(t=t):
+                return place.expert(there(i, t))
+
+            landed(j())
+            ag(always, lambda j=j: xall.at[j()], j, lambda: sib)
+
+    before = {k: [] for k in range(steps)}
+    for i in range(1, na):
+        first = min(k for k, (q, _) in enumerate(order) if q == i)
+        before[min(first, i)].append(lambda i=i: line_arrival(i))
+    for i in range(na):
+        first = min(k for k, (q, t) in enumerate(order) if q == i and t)
+        before[min(first, i + 1)].append(lambda i=i: side_arrival(i))
+
+    wloads = [pltpu.make_async_copy(h, v, w_sem.at[i]) for i, (h, v) in enumerate(
+        ((win_h, win), (wdown_h, wdown), (wshin_h, wshin), (wshdown_h, wshdown)))]
+    for load in wloads:
+        load.start()
+
+    def pair_index(k):
+        i = choose(k, [q for q, _ in order])
+        t = choose(k, [q for _, q in order])
+        p = dict(pos, A=choose(i, near), B=lax.rem(pos["B"] + t, nb))
+        return place.expert(p), place.expert(dict(p, C=1 - c))
+
+    def cot_load(k, slot):
+        one, two = pair_index(k)
+        return [pltpu.make_async_copy(cot_ref.at[j], cv.at[slot, n], c_sem.at[slot, n]) for n, j in enumerate((one, two))]
+
+    for load in cot_load(0, 0):
+        load.start()
+    gin_acc[...] = jnp.zeros_like(gin_acc)
+    gdown_acc[...] = jnp.zeros_like(gdown_acc)
+    gshin[...] = jnp.zeros_like(gshin)
+    gshdown[...] = jnp.zeros_like(gshdown)
+    for load in wloads:
+        load.wait()
+
+    def core_copy(k):
+        return pltpu.make_async_remote_copy(
+            src_ref=back_s.at[k % 2, 1], dst_ref=core_land.at[k], send_sem=core_send.at[k], recv_sem=core_recv.at[k],
+            device_id=place.device(sib), device_id_type=MESH)
+
+    b_steps = [k for k, (_, t) in enumerate(order) if t]
+
+    def b_copy(k):
+        i, t = order[k]
+        n = b_steps.index(k)
+        return pltpu.make_async_remote_copy(
+            src_ref=bsrc.at[n % 2], dst_ref=b_land.at[i * (nb - 1) + t - 1], send_sem=b_send.at[n],
+            recv_sem=b_recv.at[i * (nb - 1) + t - 1], device_id=place.device(place.moved(B=t)), device_id_type=MESH)
+
+    def a_copy(i):
+        return pltpu.make_async_remote_copy(
+            src_ref=held.at[i], dst_ref=a_land.at[a], send_sem=a_send.at[i], recv_sem=a_recv.at[a],
+            device_id=place.device(dict(pos, A=near[i])), device_id_type=MESH)
+
+    def fetch(ref, sem):
+        pltpu.make_async_copy(ref, ref, sem).wait()
+        load = pltpu.make_async_copy(ref, stage, s_sem)
+        load.start()
+        load.wait()
+        return stage[...].astype(wide)
+
+    def chip_sum(k):
+        i, t = order[k]
+        value = (back_s[k % 2, 0].astype(wide) + fetch(core_land.at[k], core_recv.at[k])).astype(low)
+        if t:
+            n = b_steps.index(k)
+            if n >= 2:
+                b_copy(b_steps[n - 2]).wait_send()
+            bsrc[n % 2] = value
+            b_copy(k).start()
+        else:
+            held[i] = value
+
+    def side_sum(i):
+        value = held[i].astype(wide)
+        for t in range(1, nb):
+            value = value + fetch(b_land.at[i * (nb - 1) + t - 1], b_recv.at[i * (nb - 1) + t - 1])
+        held[i] = value.astype(low)
+        if i:
+            a_copy(i).start()
+
+    middle = {k: [] for k in range(steps)}
+    late = []
+    for k in range(steps):
+        if k + 1 < steps:
+            middle[k + 1].append(lambda k=k: chip_sum(k))
+        else:
+            late.append(lambda k=k: chip_sum(k))
+    for i in list(range(1, na)) + [0]:
+        ready = max(max(k for k, (q, t) in enumerate(order) if q == i and t) + 3, order.index((i, 0)) + 1)
+        if ready < steps:
+            middle[ready].append(lambda i=i: side_sum(i))
+        else:
+            late.append(lambda i=i: side_sum(i))
+
+    def at(k, events):
+        for n in range(steps):
+            if events[n]:
+                @pl.when(k == n)
+                def _(n=n):
+                    for run in events[n]:
+                        run()
+
+    def gg_copy(k, n, to):
+        return pltpu.make_async_remote_copy(
+            src_ref=gg_s.at[k, n], dst_ref=gg_out.at[me], send_sem=g_send.at[k, n], recv_sem=g_recv.at[me],
+            device_id=(pos["Y"], to), device_id_type=MESH)
+
+    def mixed_copy(slot, n, j):
+        return pltpu.make_async_copy(mixed_s.at[slot, n], mixed.at[j], m_sem.at[slot, n])
+
+    def step(k, carry):
+        slot = lax.rem(k, 2)
+        one, two = pair_index(k)
+        at(k, before)
+
+        @pl.when(k == 0)
+        def _():
+            load = pltpu.make_async_copy(x_ref, xv.at[0], x_sem.at[0])
+            load.start()
+            landed(two)
+            load.wait()
+
+        @pl.when(k > 0)
+        def _():
+            load = pltpu.make_async_copy(xall.at[one], xv.at[0], x_sem.at[0])
+            load.start()
+            landed(two)
+            load.wait()
+
+        load_two = pltpu.make_async_copy(xall.at[two], xv.at[1], x_sem.at[1])
+        load_two.start()
+        for load in cot_load(k, slot):
+            load.wait()
+
+        @pl.when(k + 1 < steps)
+        def _():
+            for load in cot_load(k + 1, 1 - slot):
+                load.start()
+
+        ranks = (rank_ref[one], rank_ref[two])
+        slots = lax.broadcasted_iota(jnp.int32, (cap, toks), 0).astype(wide)
+        picks = [r == slots for r in ranks]
+        load_two.wait()
+        crs = []
+        for n in range(2):
+            p = picks[n].astype(low)
+            xr_s[n * cap:(n + 1) * cap, :] = mm(p, xv[n]).astype(low)
+            crs.append(mm(p, cv[slot, n]).astype(low))
+        cr = jnp.concatenate(crs, axis=0)
+        gu = mm(xr_s[...], win[...])
+        logits = gu[:, 2 * FF:]
+        lane = lax.broadcasted_iota(jnp.int32, logits.shape, 1)
+        logits = jnp.where(lane < experts, logits, -1e30)
+        ex = jnp.exp(logits - jnp.max(logits, axis=1, keepdims=True))
+        gate = jnp.sum(jnp.where(lane == me, ex, 0.0), axis=1, keepdims=True) / jnp.sum(ex, axis=1, keepdims=True)
+        g = gu[:, :FF]
+        u = gu[:, FF:2 * FF]
+        s = sig(g)
+        sg = g * s
+        act_s[...] = (sg * u).astype(low)
+        gr_s[...] = (gate * cr.astype(wide)).astype(low)
+        dact = mm_nt(gr_s[...], wdown[...])
+        dgu_s[:, :FF] = (dact * u * (s + sg * (1.0 - s))).astype(low)
+        dgu_s[:, FF:] = (dact * sg).astype(low)
+        o = mm(act_s[...], wdown[...]).astype(low)
+        of = o.astype(wide)
+        gg = jnp.sum(cr.astype(wide) * of, axis=1, keepdims=True)
+        wtd = (gate * of).astype(low)
+        ib = mm_nt(dgu_s[...], win[:, :2 * FF]).astype(low)
+        at(k, middle)
+
+        @pl.when(k >= 2)
+        def _():
+            for n, j in enumerate((one, two)):
+                mixed_copy(slot, n, j).wait()
+
+        for n in range(2):
+            x = xv[n]
+            ct = cv[slot, n]
+            sh = mm(x, wshin[...])
+            g2 = sh[:, :hid]
+            u2 = sh[:, hid:]
+            s2 = sig(g2)
+            sg2 = g2 * s2
+            sact = (sg2 * u2).astype(low)
+            dsact = mm_nt(ct, wshdown[...])
+            dsh = jnp.concatenate([dsact * u2 * (s2 + sg2 * (1.0 - s2)), dsact * sg2], axis=1).astype(low)
+            p = picks[n].astype(low)
+            rows = slice(n * cap, (n + 1) * cap)
+            mixed_s[slot, n] = (mm_tn(p, wtd[rows]) + mm(sact, wshdown[...])).astype(low)
+            back_s[slot, n] = (mm_tn(p, ib[rows]) + mm_nt(dsh, wshin[...])).astype(low)
+            gg_s[k, n] = jnp.sum(jnp.where(picks[n], gg[rows], 0.0), axis=0, keepdims=True)
+            gshdown[...] += mm_tn(sact, ct)
+            gshin[...] += mm_tn(x, dsh)
+        for n, j in enumerate((one, two)):
+            mixed_copy(slot, n, j).start()
+        at(k, {q: [lambda q=q: core_copy(q).start()] for q in range(steps)})
+
+        @pl.when(k > 0)
+        def _():
+            gg_copy(k, 0, one).start()
+
+        gg_copy(k, 1, two).start()
+        gdown_acc[...] += mm_tn(act_s[...], gr_s[...])
+        gin_acc[...] += mm_tn(xr_s[...], dgu_s[...])
+        at(k, {q: [lambda q=q: core_copy(q - 1).wait_send()] if q else [] for q in range(steps)})
+        return carry
+
+    lax.fori_loop(0, steps, step, 0)
+    gg_out[me] = gg_s[0, 0]
+    win[:, :2 * FF] = gin_acc[...].astype(low)
+    wdown[...] = gdown_acc[...].astype(low)
+    outs = [pltpu.make_async_copy(win.at[:, pl.ds(0, 2 * FF)], gin_out, w_sem.at[0]),
+            pltpu.make_async_copy(wdown, gdown_out, w_sem.at[1])]
+    for out in outs:
+        out.start()
+    for run in late:
+        run()
+    total = held[0].astype(wide)
+    for s in range(1, na):
+        j = lax.rem(a + s, na)
+        total = total + fetch(a_land.at[j], a_recv.at[j])
+    gin_acc[:toks, :d] = total
+    last = pltpu.make_async_copy(gin_acc.at[pl.ds(0, toks), pl.ds(0, d)], total_out, s_sem)
+    last.start()
+    last.wait()
+    for out in outs:
+        out.wait()
+    core_copy(steps - 1).wait_send()
+    for k in b_steps[-2:]:
+        b_copy(k).wait_send()
+    for i in range(1, na):
+        a_copy(i).wait_send()
+    for conds, copy in ag_sends:
+        under(conds(), lambda copy=copy: copy().wait_send())
+    for k in (steps - 2, steps - 1):
+        one, two = pair_index(k)
+        for n, j in enumerate((one, two)):
+            mixed_copy(k % 2, n, j).wait()
+
+    def gg_done(k, carry):
+        one, two = pair_index(k)
+
+        @pl.when(k > 0)
+        def _():
+            gg_copy(k, 0, one).wait_send()
+
+        gg_copy(k, 1, two).wait_send()
+        return carry
+
+    lax.fori_loop(0, steps, gg_done, 0)
+
+    def gg_wait(s, carry):
+        j = lax.rem(me + s, n_exp)
+        pltpu.make_async_copy(gg_out.at[j], gg_out.at[j], g_recv.at[j]).wait()
+        return carry
+
+    lax.fori_loop(1, n_exp, gg_wait, 0)
+
+
+def fused(x, cot_all, rank, win, wdown, wshin, wshdown, n_dp, n_exp, experts, cap, cid):
+    toks, d = x.shape
+    size = sizes(n_dp, n_exp)
+    na, nb = size["A"], size["B"]
+    steps = na * nb
+    hid = wshdown.shape[0]
+    low, wide = jnp.bfloat16, jnp.float32
+    hbm = pl.BlockSpec(memory_space=pl.ANY)
+    vmem = pl.BlockSpec(memory_space=pltpu.VMEM)
+    rows = 2 * cap
+    block = (toks, d)
+    dma = pltpu.SemaphoreType.DMA
+    ag_count = 2 + (nb - 1) + 1 + (na - 1) * (2 + nb) + na * (nb - 1)
+    flops = 2 * n_exp * (cap * d * FF * 9 + toks * cap * d * 4 + toks * d * hid * 9)
+    return pl.pallas_call(
+        functools.partial(fused_kernel, n_dp, n_exp, experts, cap),
+        in_specs=[hbm, hbm, vmem, hbm, hbm, hbm, hbm],
+        out_shape=[
+            jax.ShapeDtypeStruct((n_exp,) + block, low),
+            jax.ShapeDtypeStruct((n_exp,) + block, low),
+            jax.ShapeDtypeStruct(block, wide),
+            jax.ShapeDtypeStruct((n_exp, 1, toks), wide),
+            jax.ShapeDtypeStruct((d, 2 * FF), low),
+            jax.ShapeDtypeStruct((FF, d), low),
+            jax.ShapeDtypeStruct((d, 2 * hid), wide),
+            jax.ShapeDtypeStruct((hid, d), wide),
+            jax.ShapeDtypeStruct((steps,) + block, low),
+            jax.ShapeDtypeStruct((na * max(nb - 1, 1),) + block, low),
+            jax.ShapeDtypeStruct((na,) + block, low),
+        ],
+        out_specs=[hbm, hbm, hbm, vmem, hbm, hbm, vmem, vmem, hbm, hbm, hbm],
+        scratch_shapes=[
+            pltpu.VMEM(win.shape, low), pltpu.VMEM(wdown.shape, low), pltpu.VMEM(wshin.shape, low),
+            pltpu.VMEM(wshdown.shape, low),
+            pltpu.VMEM((2,) + block, low), pltpu.VMEM((2, 2) + block, low),
+            pltpu.VMEM((rows, d), low), pltpu.VMEM((rows, FF), low), pltpu.VMEM((rows, d), low),
+            pltpu.VMEM((rows, 2 * FF), low),
+            pltpu.VMEM((2, 2) + block, low), pltpu.VMEM((2, 2) + block, low), pltpu.VMEM((na,) + block, low),
+            pltpu.VMEM((2,) + block, low), pltpu.VMEM(block, low),
+            pltpu.VMEM((steps, 2, 1, toks), wide), pltpu.VMEM((d, 2 * FF), wide), pltpu.VMEM((FF, d), wide),
+            dma((4,)), dma((2,)), dma((2, 2)), dma((2, 2)), dma(()),
+            dma((ag_count,)), dma((n_exp,)), dma((steps,)), dma((steps,)),
+            dma((na * max(nb - 1, 1),)), dma((na * max(nb - 1, 1),)), dma((na,)), dma((na,)),
+            dma((steps, 2)), dma((n_exp,)),
+        ],
+        compiler_params=pltpu.CompilerParams(collective_id=cid, has_side_effects=True, vmem_limit_bytes=63 * 1024 * 1024),
+        cost_estimate=pl.CostEstimate(flops=flops, bytes_accessed=100 * 1024 * 1024, transcendentals=0),
+        name="experts_fused",
+    )(x, cot_all, rank, win, wdown, wshin, wshdown)
 
 
 def spread_kernel(n_dp, n_exp, x_ref, out_ref, send_sem, recv_sem):
@@ -591,7 +1022,7 @@
     )
     shin_send = jnp.concatenate([shin_send] * n_dp, axis=0)
     shin_mine = lax.all_to_all(shin_send, both, 0, 0, tiled=True).reshape(D, 2 * n_dp * unit)
-    shdown_mine = lax.all_gather(w_shared_down.astype(low), "dp", axis=0, tiled=True)
+    shdown_mine = swap_rows(w_shared_down.astype(low), n_dp)
     half = n_dp * unit
 
     inputs = tokens.astype(wide)
@@ -622,78 +1053,27 @@
     logits = jnp.dot(mlp_in, router_full, preferred_element_type=wide)
     router_probs = jax.nn.softmax(logits, axis=-1)
 
-    mlp_all = gather(mlp_in, n_dp, n_exp, False, 2, ("ABC", "ABC", "ABC", "ABC", "BAC"))
-    mlp_flat = mlp_all.reshape(n_exp * row_count, D)
-    fused_w = jnp.concatenate([shin_mine, router_full], axis=1)
-    fused = jnp.dot(mlp_flat, fused_w, preferred_element_type=wide)
-    shared_gate = fused[:, :half]
-    shared_up = fused[:, half : 2 * half]
-    probs_all = jax.nn.softmax(fused[:, 2 * half :], axis=-1)
-    expert_ids = jnp.arange(expert_count, dtype=jnp.int32)
-    my_prob = jnp.sum(jnp.where(expert_ids[None, :] == my_expert, probs_all, 0.0), axis=1)
-    my_prob = my_prob.reshape(n_exp, row_count)
     routed_here = jnp.any(routes_all == my_expert, axis=2)
-    rank = jnp.cumsum(routed_here.astype(jnp.int32), axis=1) - 1
-    slot = jnp.arange(capacity, dtype=jnp.int32)
-    pick_mask = routed_here[:, None, :] & (rank[:, None, :] == slot[None, :, None])
-    pick = pick_mask.astype(low)
-    picked_in = jnp.einsum("nst,ntd->nsd", pick, mlp_all, preferred_element_type=wide).astype(low)
-    picked_cot = jnp.einsum("nst,ntd->nsd", pick, cot_all, preferred_element_type=wide).astype(low)
-    picked_gate = jnp.sum(jnp.where(pick_mask, my_prob[:, None, :], 0.0), axis=2).reshape(-1, 1)
-    flat_in = picked_in.reshape(-1, D)
-    flat_cot = picked_cot.reshape(-1, D).astype(wide)
-    gate_up = jnp.dot(flat_in, expert_in_full, preferred_element_type=wide)
-    activation = (jax.nn.silu(gate_up[:, :FF]) * gate_up[:, FF:]).astype(low)
-    result = jnp.dot(activation, expert_down_full, preferred_element_type=wide).astype(low)
-    result = result.astype(wide)
-    gate_grad = jnp.sum(flat_cot * result, axis=1).reshape(n_exp, capacity, 1)
-    weighted = (picked_gate * result).astype(low).reshape(n_exp, capacity, D)
-    shared_act = (jax.nn.silu(shared_gate) * shared_up).astype(low)
-    mixed_part = jnp.einsum("nst,nsd->ntd", pick, weighted, preferred_element_type=wide)
-    mixed_part = mixed_part.reshape(-1, D) + jnp.dot(
-        shared_act, shdown_mine, preferred_element_type=wide
-    )
-    mixed_sum = reduce_scatter(
-        mixed_part.astype(low).reshape(n_exp, row_count, D), n_dp, n_exp, False, 3, ("CBA", "CBA")
-    )
+    rank = jnp.where(routed_here, jnp.cumsum(routed_here.astype(jnp.int32), axis=1) - 1, -1).astype(wide)
+    hid = (half + 127) // 128 * 128
+    cap = (capacity + 15) // 16 * 16
+    win = jnp.concatenate([expert_in_full, router_full, jnp.zeros((D, 128 - expert_count), low)], axis=1)
+    gap = jnp.zeros((D, hid - half), low)
+    wshin = jnp.concatenate([shin_mine[:, :half], gap, shin_mine[:, half:], gap], axis=1)
+    wshdown = jnp.concatenate([shdown_mine, jnp.zeros((hid - half, D), low)], axis=0)
+    _, mixed_part, back_sum, gate_grad, grad_ein, grad_edown, shin_wide, shdown_wide, _, _, _ = fused(
+        mlp_in, cot_all, rank[:, None, :], win, expert_down_full, wshin, wshdown, n_dp, n_exp, expert_count, cap, 2
+    )
+    mixed_sum = lax.psum_scatter(mixed_part, "expert", scatter_dimension=0, tiled=False)
     mixed = (residual + mixed_sum.astype(wide)).astype(low)
-
-    cot_flat = cot_all.reshape(n_exp * row_count, D)
-    grad_shdown = jnp.einsum("tf,td->fd", shared_act, cot_flat, preferred_element_type=wide)
-    shared_act_grad = jnp.einsum("td,fd->tf", cot_flat, shdown_mine, preferred_element_type=wide)
-    shared_gu_grad = jnp.concatenate(
-        [
-            shared_act_grad * shared_up * silu_slope(shared_gate),
-            shared_act_grad * jax.nn.silu(shared_gate),
-        ],
-        axis=1,
-    ).astype(low)
-    grad_shin = jnp.einsum("td,tf->df", mlp_flat, shared_gu_grad, preferred_element_type=wide)
-    grad_rows = (picked_gate * flat_cot).astype(low)
-    grad_edown = jnp.einsum("rf,rd->fd", activation, grad_rows, preferred_element_type=wide)
-    expert_act_grad = jnp.einsum(
-        "rd,fd->rf", grad_rows, expert_down_full, preferred_element_type=wide
-    )
-    expert_gu_grad = swiglu_back(expert_act_grad, gate_up)
-    grad_ein = jnp.einsum("rd,rf->df", flat_in, expert_gu_grad, preferred_element_type=wide)
-    input_back = jnp.einsum(
-        "rf,df->rd", expert_gu_grad, expert_in_full, preferred_element_type=wide
-    )
-    input_back = input_back.astype(low).reshape(n_exp, capacity, D)
-    back_part = jnp.einsum("nst,nsd->ntd", pick, input_back, preferred_element_type=wide)
-    back_part = back_part.reshape(-1, D) + jnp.einsum(
-        "tf,df->td", shared_gu_grad, shin_mine, preferred_element_type=wide
-    )
-    back_sum = reduce_scatter(
-        back_part.astype(low).reshape(n_exp, row_count, D), n_dp, n_exp, False, 4, ("CBA", "CBA")
-    )
-    gate_grad_tok = jnp.sum(jnp.where(pick_mask, gate_grad, 0.0), axis=1)
-    prob_grad = lax.all_to_all(gate_grad_tok, "expert", 0, 0, tiled=True).T
+    grad_shin = jnp.concatenate([shin_wide[:, :half], shin_wide[:, hid : hid + half]], axis=1)
+    grad_shdown = shdown_wide[:half]
+    prob_grad = gate_grad[:, 0, :].T
     logit_grad = (
         router_probs * (prob_grad - jnp.sum(prob_grad * router_probs, axis=-1, keepdims=True))
     ).astype(low)
     grad_router = jnp.einsum("td,te->de", mlp_in, logit_grad, preferred_element_type=wide)
-    mlp_in_grad = back_sum.astype(wide) + jnp.einsum(
+    mlp_in_grad = back_sum + jnp.einsum(
         "te,de->td", logit_grad, router_full, preferred_element_type=wide
     )
     out_grad = cotangent.astype(wide)
@@ -739,9 +1119,9 @@
         [grad_router, grad_gain_one[:, None], grad_gain_two[:, None], jnp.zeros((D, 128 - expert_count - 2), wide)],
         axis=1,
     )
-    dense_grad = jnp.concatenate([grad_qkv.astype(low), grad_out.astype(low), small_grad.astype(low)], axis=1)
-    dense_own = reduce_scatter(dense_grad.reshape(n_all, rows_w, -1), n_dp, n_exp, True, 5)
-    small_own = dense_own[:, 3 * H * HD + D :]
+    qkv_own, out_own, small_own = reduce_dense(
+        [g.astype(low).reshape(n_all, rows_w, -1) for g in (grad_qkv, grad_out, small_grad)], n_dp, n_exp, 5
+    )
     shin_back = lax.all_to_all(
         grad_shin.astype(low).reshape(n_all, rows_w, 2 * half), both, 0, 0, tiled=True
     )
@@ -751,13 +1131,13 @@
     shin_own = shin_own.transpose(1, 2, 3, 0, 4).reshape(rows_w, 2 * FF)
     owned_grads = (
         small_own[:, expert_count : expert_count + 2].T,
-        dense_own[:, : 3 * H * HD],
-        dense_own[:, 3 * H * HD : 3 * H * HD + D],
+        qkv_own,
+        out_own,
         shin_own,
         lax.psum_scatter(grad_shdown, "dp", scatter_dimension=0, tiled=True),
         small_own[:, :expert_count],
-        halve_rows(grad_ein.astype(low), n_dp)[None],
-        halve_rows(grad_edown.astype(low), n_dp)[None],
+        halve_rows(grad_ein, n_dp)[None],
+        halve_rows(grad_edown, n_dp)[None],
     )
     squares = sum((jnp.sum(grad_part * grad_part) for grad_part in owned_grads))
     total_squares = sum_everywhere(squares, n_dp, n_exp, 6)

time: 1130 us -> 865 us (0.77)
  matrix products: 296 us -> 63.2 us
  Pallas kernels: 543 us -> 464 us
  blocking collectives: 37.3 us -> 104 us
  waiting for transfers between devices: 0.7 us -> 35.4 us
  starting transfers between devices: 44.5 us -> 19.6 us
  other arithmetic: 116 us -> 96.4 us
  local copies, waits for them, and re-layouts: 66.7 us -> 50.1 us
    dot_general x16 -> x0, matrix products: 234 us -> none  [the longest x1 21.2 us: local(): jnp.einsum('rd,rf->df', flat_in, expert_gu_grad, preferred_element_type=w...]
    pallas_call x2 -> x1, Pallas kernels: 191 us -> 105 us  [gather(): pl.pallas_call(functools.partial(gather_kernel, n_dp, n_exp, orders, slic...]
    unnamed x1, blocking collectives: 8.56 us -> 75.5 us
    reduce_scatter x0 -> x1, waiting for transfers between devices: none -> 29.1 us  [local(): lax.psum_scatter(mixed_part, 'expert', scatter_dimension=0, tiled=False)]
    all_to_all x1, starting transfers between devices: 25.1 us -> 3.42 us  [local(): lax.all_to_all(grad_shin.astype(low).reshape(n_all, rows_w, 2 * half), bo...]
    convert_element_type x4 -> x3, other arithmetic: 22.4 us -> 1.3 us  [the longest x1 0.65 us: local(): jnp.where(routed_here, jnp.cumsum(routed_here.astype(jnp.int32), axis=1)...]
    pallas_call x3 -> x2, Pallas kernels: 333 us -> 340 us  [the longest x1 249 us: fused(): pl.pallas_call(functools.partial(fused_kernel, n_dp, n_exp, experts, cap)...]
  transfers between devices with their start and end apart: 9 -> 10, of which waited for: 0 -> 2; matrix products, arithmetic and copies ran while one was open for 26% -> 21% of each run, Pallas kernels for 46% -> 12%
where the time goes in v3:
time: 865 us; the launch traced here: 856 us
  Pallas kernels  464 us (54%)
  blocking collectives  104 us (12%)
  other arithmetic  96.4 us (11%)
  matrix products  63.2 us (7%)
  local copies, waits for them, and re-layouts  50.1 us (6%)
  waiting for transfers between devices  35.4 us (4%)
  between operations  22.9 us (3%)
  starting transfers between devices  19.6 us (2%)
    pallas_call x1, Pallas kernels, fused(): pl.pallas_call(functools.partial(fused_kernel, n_dp, n_exp, experts, cap)...  249 us
    pallas_call x1, Pallas kernels, gather(): pl.pallas_call(functools.partial(gather_kernel, n_dp, n_exp, orders, slic...  105 us
    pallas_call x1, Pallas kernels, reduce_dense(): pl.pallas_call(functools.partial(reduce_kernel, n_dp, n_exp, orders, slic...  90.8 us
    unnamed x1, blocking collectives  75.5 us
    reduce_scatter x1, waiting for transfers between devices, local(): lax.psum_scatter(mixed_part, 'expert', scatter_dimension=0, tiled=False)  29.1 us
    all_gather x1, blocking collectives, local(): routes_all = lax.all_gather(routes, 'expert', axis=0, tiled=False)  28.4 us
    sub x8, other arithmetic, adam_update(): weight - step_rate * (first_hat / (jnp.sqrt(second_hat) + ADAM_EPS) + dec...  23.9 us
    pallas_call x1, Pallas kernels, sum_everywhere(): pl.pallas_call(functools.partial(spread_kernel, n_dp, n_exp), out_shape=j...  19.6 us
  transfers between devices with their start and end apart: 10, of which 2 were waited for; matrix products, arithmetic and copies ran while one was open for 21% of the time, Pallas kernels for 12%

profile of v3, /device:TPU:0, one launch (start us, length us, event | category | flops | bytes accessed | tf_op | source)
XLA Modules:
  0.0 855.8 jit_solution(3065374296571713487)
XLA Ops:
  7.9 4.1 convert_bitcast_fusion
  12.0 3.0 collective-permute-start
  24.2 5.0 all-to-all-start
  29.3 28.4 %all-gather.1 = s32[6144,6]{0,1:T(8,128)S(1)} all-gather(s32[384,6]{0,1:T(8,128)S(1)} %copy-done.47), channel_id=3, replica_groups=mesh['dp'=2,'expert'=16] {'expert'}, dimensions={0}, use_global_device_ids=true | all-gather | bytes 156672 | tf_op jit(solution)/shard_map/all_gather | solution.py:1014
  59.9 104.9 %gather_dense.1 = bf16[32,40,5248]{2,1,0:T(8,128)(2,1)} custom-call(bf16[40,5248]{1,0:T(8,128)(2,1)} %concatenate.60.x_ref), custom_call_target="tpu_custom_call" | custom-call | tf_op jit(solution)/shard_map/gather_dense/pallas_call | solution.py:276
  170.4 8.3 fusion.4
  183.3 6.2 fusion.98
  189.5 4.1 fusion.44
  193.6 3.9 multiply_reduce_fusion.5
  214.1 8.0 concatenate.66.win_h
  222.0 249.0 %experts_fused.1 = (bf16[16,384,1280]{2,1,0:T(8,128)(2,1)}, bf16[16,384,1280]{2,1,0:T(8,128)(2,1)}, f32[384,1280]{1,0:T(8,128)}, f32[16,1,384]{2,1,0:T(1,128)}, ...) custom-call(bf16[384,1280]{1,0:T(8,128)(2,1)} %multiply_convert_fusi, ...), custom_call_target="tpu_custom_call" | custom-call | flops 93616865280 | bytes 104857600 | tf_op jit(solution)/shard_map/experts_fused/pallas_call | solution.py:857
  483.9 75.5 %fusion = f32[32,1280]{1,0:T(8,128)S(1)} fusion(f32[56,1280]{1,0:T(8,128)S(1)} %slice.120), kind=kCustom, calls=%all-reduce-scatter | all-reduce-scatter fusion | flops 81921 | bytes 451072
  560.0 4.0 collective-permute-start.5
  565.1 3.4 all-to-all-start.1
  568.8 3.7 multiply_reduce_fusion.3
  576.3 5.6 all-to-all-done.1
  581.9 4.3 reshape.289
  586.3 4.2 reduce_sum.213
  592.5 4.1 multiply_reduce_fusion.2
  596.6 6.1 multiply_reduce_fusion.1
  602.7 29.1 %reduce-scatter.4.cloned.1.call-done = bf16[1,384,1280]{2,1,0:T(8,128)(2,1)} async-done(((bf16[16,384,1280]{2,1,0:T(8,128)(2,1)}), bf16[1,384,1280]{2,1,0:T(8,128)(2,1)}) %reduce-scatter.4.cloned.1.call-update) | async-done | bytes 983056 | tf_op jit(solution)/shard_map/reduce_scatter | solution.py:1067
  631.8 4.3 multiply_add_fusion
  637.4 4.5 fusion.20
  644.6 4.7 multiply_reduce_fusion
  660.2 8.2 fusion.31
  668.4 10.2 %convolution_convert_fusion = bf16[1280,3840]{1,0:T(8,128)(2,1)} fusion(bf16[384,3840]{0,1:T(8,128)(2,1)} %bitcast.154, bf16[384,1280]{1,0:T(8,128)(2,1)S(1)} %copy-done.13, f32[1280]{0:T(1024)S(1)} %copy-done.42, f32[384]{0:T(512)S(1)} %copy-done.49), kind=kOutput, calls=%fused_computation.1 | convolution fusion | flops 3781754880 | bytes 13769216 | tf_op jit(solution)/shard_map/td,tk->dk/dot_general | solution.py:1110
  678.6 3.6 convolution_convert_fusion.1
  685.7 90.8 %reduce_dense.1 = (f32[40,3840]{1,0:T(8,128)}, f32[40,1280]{1,0:T(8,128)}, f32[40,128]{1,0:T(8,128)}) custom-call(bf16[32,40,3840]{2,1,0:T(8,128)(2,1)} %bitcast.149, bf16[32,40,1280]{2,1,0:T(8,128)(2,1)} %bitcast.152, bf16[32,40,128]{2,1,0:T(8,128)(2,1)} %maximum_maximum_fusion.1.refs_2_), custom_call_target="tpu_custom_call" | custom-call | tf_op jit(solution)/shard_map/reduce_dense/pallas_call | solution.py:452
  788.6 19.6 %sum_everywhere.1 = f32[32,8,128]{2,1,0:T(8,128)} custom-call(f32[8,128]{1,0:T(8,128)} %broadcast_in_dim.50.x_ref), custom_call_target="tpu_custom_call" | custom-call | tf_op jit(solution)/shard_map/sum_everywhere/pallas_call | solution.py:930
  827.1 3.5 fusion.30
  832.8 5.7 multiply_subtract_fusion.1
  838.5 9.1 %multiply_subtract_fusion = (f32[1,640,1792]{2,1,0:T(8,128)}, f32[1,640,1792]{2,1,0:T(8,128)}, f32[1,640,1792]{2,1,0:T(8,128)}) fusion(f32[1,640,1792]{2,1,0:T(8,128)S(1)} %bitcast.134, f32[]{:T(128)S(6)} %min.3, bf16[640,1792]{1,0:T(8,128)(2,1)} %collective-permute-done.3, bf16[640,1792]{1,0:T(8,128)(2,1)S(1)} %copy-done.6, f32[1,640,1792]{2,1,0:T(8,128)} %param.51, ...), kind=kLoop, calls=%fused_computation.16 | loop fusion | flops 21790720 | bytes 32112644 | tf_op jit(solution)/shard_map/sub | solution.py:86
  (287 shorter events, 103.7 us)
Async XLA Ops:
  7.2 214.8 %all-gather.4.cloned.1.call-start = ((), (), s32[]{:S(2)}) async-start(), calls=%async_computation.4 | async-start | bytes 16711680 | tf_op jit(solution)/shard_map/all_gather | solution.py:1013
  7.9 7.0 copy-start
  12.0 197.4 %collective-permute-start = (bf16[640,1792]{1,0:T(8,128)(2,1)}, bf16[640,1792]{1,0:T(8,128)(2,1)}, u32[]{:S(2)}, u32[]{:S(2)}) collective-permute-start(bf16[640,1792]{1,0:T(8,128)(2,1)} %convert_bitcast_fusion), channel_id=1, source_target_pairs={{0,16},{16,0},{1,17},{17,1},{2,18},{18,2},{3,19},{19,3},{4,20},{20... | collective-permute-start | bytes 6881288 | tf_op jit(solution)/shard_map/ppermute | solution.py:945
  16.1 190.1 %collective-permute-start.1 = (bf16[448,1280]{1,0:T(8,128)(2,1)}, bf16[448,1280]{1,0:T(8,128)(2,1)}, u32[]{:S(2)}, u32[]{:S(2)}) collective-permute-start(bf16[448,1280]{1,0:T(8,128)(2,1)} %convert_bitcast_fusion.1), channel_id=1, source_target_pairs={{0,16},{16,0},{1,17},{17,1},{2,18},{18,2},{3,19},{19,3},{4,20},{20... | collective-permute-start | bytes 3440648 | tf_op jit(solution)/shard_map/ppermute | solution.py:945
  16.8 12.5 %copy-start.47 = (s32[384,6]{0,1:T(8,128)S(1)}, s32[384,6]{0,1:T(8,128)}, u32[]{:S(2)}) copy-start(s32[384,6]{0,1:T(8,128)} %param.30) | copy-start | bytes 27652
  16.8 185.0 %collective-permute-start.2 = (bf16[28,1280]{1,0:T(8,128)(2,1)}, bf16[28,1280]{1,0:T(8,128)(2,1)}, u32[]{:S(2)}, u32[]{:S(2)}) collective-permute-start(bf16[28,1280]{1,0:T(8,128)(2,1)} %convert_element_type.173), channel_id=1, source_target_pairs={{0,16},{16,0},{1,17},{17,1},{2,18},{18,2},{3,19},{19,3},{4,20},{20... | collective-permute-start | bytes 215048 | tf_op jit(solution)/shard_map/ppermute | solution.py:945
  20.5 38.3 %copy-start.43 = (f32[40,16]{0,1:T(8,128)S(1)}, f32[40,16]{0,1:T(8,128)}, u32[]{:S(2)}) copy-start(f32[40,16]{0,1:T(8,128)} %param.47) | copy-start | bytes 7684
  20.5 38.4 %copy-start.52 = (f32[2,40]{1,0:T(2,128)S(1)}, f32[2,40]{1,0:T(2,128)}, u32[]{:S(2)}) copy-start(f32[2,40]{1,0:T(2,128)} %param.32) | copy-start | bytes 964
  21.8 36.0 %copy-start.17 = (f32[40,3840]{1,0:T(8,128)S(1)}, f32[40,3840]{1,0:T(8,128)}, u32[]{:S(2)}) copy-start(f32[40,3840]{1,0:T(8,128)} %param.35) | copy-start | bytes 1843204
  24.2 179.3 %all-to-all-start = ((bf16[32,40,112]{2,1,0:T(8,128)(2,1)}), bf16[32,40,112]{2,1,0:T(8,128)(2,1)}, u32[]{:S(2)}, u32[]{:S(2)}) async-start(bf16[32,40,112]{2,1,0:T(8,128)(2,1)} %pad_maximum_fusion.4), calls=%async_computation | async-start | bytes 655360 | tf_op jit(solution)/shard_map/all_to_all | solution.py:1024
  29.2 602.6 %reduce-scatter.4.cloned.1.call-start = ((), (), s32[]{:S(2)}) async-start(), calls=%async_computation.3 | async-start | bytes 16711680 | tf_op jit(solution)/shard_map/reduce_scatter | solution.py:1067
  59.9 105.0 %copy-start.59 = (s32[1,4]{1,0:T(1,128)S(1)}, s32[1,4]{1,0:T(1,128)}, u32[]{:S(2)}) copy-start(s32[1,4]{1,0:T(1,128)} %param.29) | copy-start | bytes 52
  169.3 9.4 %copy-start.41 = (f32[1280]{0:T(1024)}, f32[1280]{0:T(1024)S(1)}, u32[]{:S(2)}) copy-start(f32[1280]{0:T(1024)S(1)} %get-tuple-element.183) | copy-start | bytes 15364
  169.6 9.1 %copy-start.48 = (f32[384]{0:T(512)}, f32[384]{0:T(512)S(1)}, u32[]{:S(2)}) copy-start(f32[384]{0:T(512)S(1)} %add_rsqrt_fusion.1) | copy-start | bytes 4612
  471.1 7.0 copy-start.7
  479.2 113.3 %collective-permute-start.4 = (bf16[448,1280]{1,0:T(8,128)(2,1)}, bf16[448,1280]{1,0:T(8,128)(2,1)}, u32[]{:S(2)}, u32[]{:S(2)}) collective-permute-start(bf16[448,1280]{1,0:T(8,128)(2,1)} %broadcast_select_fusion.4), channel_id=1, source_target_pairs={{0,16},{16,0},{1,17},{17,1},{2,18},{18,2},{3,19},{19,3},{4,20},{20... | collective-permute-start | bytes 3440648 | tf_op jit(solution)/shard_map/ppermute | solution.py:956
  480.7 83.3 %copy-start.25 = (f32[1280,256]{1,0:T(8,128)S(1)}, f32[1280,256]{1,0:T(8,128)}, u32[]{:S(2)}) copy-start(f32[1280,256]{1,0:T(8,128)} %get-tuple-element.43) | copy-start | bytes 3932164
  482.3 114.3 %collective-permute-start.3 = (bf16[640,1792]{1,0:T(8,128)(2,1)}, bf16[640,1792]{1,0:T(8,128)(2,1)}, u32[]{:S(2)}, u32[]{:S(2)}) collective-permute-start(bf16[640,1792]{1,0:T(8,128)(2,1)} %broadcast_select_fusion), channel_id=1, source_target_pairs={{0,16},{16,0},{1,17},{17,1},{2,18},{18,2},{3,19},{19,3},{4,20},{20... | collective-permute-start | bytes 6881288 | tf_op jit(solution)/shard_map/ppermute | solution.py:956
  560.0 14.7 %collective-permute-start.5 = (f32[4,1280]{1,0:T(4,128)}, f32[4,1280]{1,0:T(4,128)}, u32[]{:S(2)}, u32[]{:S(2)}) collective-permute-start(f32[4,1280]{1,0:T(4,128)} %slice.148), channel_id=1, source_target_pairs={{0,16},{1,17},{2,18},{3,19},{4,20},{5,21},{6,22},{7,23},{8,24},{9,... | collective-permute-start | bytes 61448
  565.1 16.9 %all-to-all-start.1 = ((bf16[32,40,112]{2,1,0:T(8,128)(2,1)}), bf16[32,40,112]{2,1,0:T(8,128)(2,1)}, u32[]{:S(2)}, u32[]{:S(2)}) async-start(bf16[32,40,112]{2,1,0:T(8,128)(2,1)} %pad_maximum_fusion.5), calls=%async_computation.2 | async-start | bytes 655360 | tf_op jit(solution)/shard_map/all_to_all | solution.py:1125
  637.4 7.1 copy-start.46
  637.4 11.9 %slice-start.8 = ((s8[5898240]{0:T(1024)(128)(4,1)}), s8[1703936]{0:T(1024)(128)(4,1)S(1)}, s32[]{:S(2)}) async-start(s8[5898240]{0:T(1024)(128)(4,1)} %bitcast.150), calls=%async_computation.13 | async-start | bytes 3407872
  668.4 10.2 %copy-start.10 = (f32[384,1280]{1,0:T(8,128)S(1)}, f32[384,1280]{1,0:T(8,128)}, u32[]{:S(2)}) copy-start(f32[384,1280]{1,0:T(8,128)} %copy-done.9) | copy-start | bytes 5898244
  668.4 10.2 %copy-start.61 = (bf16[10,128,384]{2,1,0:T(8,128)(2,1)S(1)}, bf16[10,128,384]{2,1,0:T(8,128)(2,1)}, u32[]{:S(2)}) copy-start(bf16[10,128,384]{2,1,0:T(8,128)(2,1)} %copy-done.60) | copy-start | bytes 2949124
  776.6 35.4 %copy-start.34 = (f32[40,128]{1,0:T(8,128)S(1)}, f32[40,128]{1,0:T(8,128)}, u32[]{:S(2)}) copy-start(f32[40,128]{1,0:T(8,128)} %get-tuple-element.40) | copy-start | bytes 61444
  776.6 35.4 %copy-start.37 = (f32[40,16]{1,0:T(8,128)S(1)}, f32[40,16]{1,0:T(8,128)}, u32[]{:S(2)}) copy-start(f32[40,16]{1,0:T(8,128)} %copy.243) | copy-start | bytes 7684
  822.0 8.6 %copy-start.27 = (f32[40,1792]{1,0:T(8,128)S(1)}, f32[40,1792]{1,0:T(8,128)}, u32[]{:S(2)}) copy-start(f32[40,1792]{1,0:T(8,128)} %param.41) | copy-start | bytes 860164
  822.0 8.6 %copy-start.28 = (f32[40,1792]{1,0:T(8,128)S(1)}, f32[40,1792]{1,0:T(8,128)}, u32[]{:S(2)}) copy-start(f32[40,1792]{1,0:T(8,128)} %mul.661) | copy-start | bytes 860164
  822.0 8.6 %copy-start.35 = (f32[40,1792]{1,0:T(8,128)S(1)}, f32[40,1792]{1,0:T(8,128)}, u32[]{:S(2)}) copy-start(f32[40,1792]{1,0:T(8,128)} %param.42) | copy-start | bytes 860164
  824.3 8.4 copy-start.20
  824.3 8.4 copy-start.21
  827.1 11.4 %slice-start.2 = ((s8[4587520]{0:T(1024)(128)(4,1)}), s8[4194304]{0:T(1024)(128)(4,1)S(1)}, s32[]{:S(2)}) async-start(s8[4587520]{0:T(1024)(128)(4,1)} %bitcast.133), calls=%async_computation.7 | async-start | bytes 8388608
  (50 other events, 197.4 us)
Sparse Core Ops, SparseCore 0:
  10.3 172.5 all-gather.3
  471.3 160.5 reduce-scatter.3

commit v4 on v3

--- a/solution.py
+++ b/solution.py
@@ -14,6 +14,7 @@
 FF = 896
 TOP = 6
 ADAM_STEP = 5
+GIVEN = 1280
 
 
 EPS = 1e-06
@@ -421,9 +422,36 @@
     return total
 
 
-def reduce_kernel(n_dp, n_exp, orders, slices, dense, arrays, *refs):
-    g_refs, out_refs, scratch = refs[:arrays], refs[arrays:2 * arrays], refs[2 * arrays:]
-    land, (send_sem, recv_sem) = scratch[:-2], scratch[-2:]
+def norm_exchange(place, value_ref, land, send_sem, recv_sem):
+    for n, axis in enumerate("CBYA"):
+        mine = place.pos[axis]
+        size = place.size[axis]
+        land[n, mine] = value_ref[...]
+
+        def copy(step, n=n, axis=axis, mine=mine, size=size):
+            to = dict(place.pos)
+            to[axis] = lax.rem(mine + step, size)
+            return pltpu.make_async_remote_copy(
+                src_ref=land.at[n, mine], dst_ref=land.at[n, mine], send_sem=send_sem.at[n, step],
+                recv_sem=recv_sem.at[n, mine], device_id=place.device(to), device_id_type=MESH)
+
+        for step in range(1, size):
+            copy(step).start()
+        for step in range(1, size):
+            j = lax.rem(mine + step, size)
+            pltpu.make_async_copy(land.at[n, j], land.at[n, j], recv_sem.at[n, j]).wait()
+        total = land[n, 0]
+        for j in range(1, size):
+            total = total + land[n, j]
+        for step in range(1, size):
+            copy(step).wait_send()
+        value_ref[...] = total
+
+
+def reduce_kernel(n_dp, n_exp, orders, slices, dense, arrays, sq_ref, *refs):
+    g_refs, out_refs, scratch = refs[:arrays], refs[arrays:2 * arrays], refs[2 * arrays + 1:]
+    norm_ref = refs[2 * arrays]
+    land, (send_sem, recv_sem, norm_land, norm_send, norm_recv) = scratch[:-5], scratch[-5:]
     place = Place(n_dp, n_exp)
     place.greet(orders[0], True)
     base = [0]
@@ -435,9 +463,14 @@
         out_refs[which][:, lo:lo + w] = total
 
     reduce_body(place, orders, slices, g_refs, place.flat if dense else place.expert, land, base, send_sem, recv_sem, finish)
-
-
-def reduce_dense(arrays, n_dp, n_exp, cid):
+    total = sq_ref[...]
+    for out in out_refs:
+        total = total + jnp.sum(out[...] * out[...])
+    norm_ref[...] = total
+    norm_exchange(place, norm_ref, norm_land, norm_send, norm_recv)
+
+
+def reduce_dense(arrays, squares, n_dp, n_exp, cid):
     size = sizes(n_dp, n_exp)
     blocks, rows = arrays[0].shape[:2]
     orders, slices = [], []
@@ -449,18 +482,23 @@
                 orders.append(order)
                 slices.append((which, lo, w))
     slots = [len(stage_slots(size, order)) for order in orders]
+    top = max(size.values())
     return pl.pallas_call(
         functools.partial(reduce_kernel, n_dp, n_exp, orders, slices, True, len(arrays)),
-        out_shape=[jax.ShapeDtypeStruct((rows, g.shape[2]), jnp.float32) for g in arrays],
-        in_specs=[pl.BlockSpec(memory_space=pltpu.VMEM)] * len(arrays),
-        out_specs=[pl.BlockSpec(memory_space=pltpu.VMEM)] * len(arrays),
+        out_shape=[jax.ShapeDtypeStruct((rows, g.shape[2]), jnp.float32) for g in arrays] + [
+            jax.ShapeDtypeStruct((8, 128), jnp.float32)],
+        in_specs=[pl.BlockSpec(memory_space=pltpu.VMEM)] * (len(arrays) + 1),
+        out_specs=[pl.BlockSpec(memory_space=pltpu.VMEM)] * (len(arrays) + 1),
         scratch_shapes=[pltpu.VMEM((k, rows, s[2]), g.dtype) for k, s in zip(slots, slices)] + [
             pltpu.SemaphoreType.DMA((count_reduce(size, orders),)),
             pltpu.SemaphoreType.DMA((sum(slots),)),
+            pltpu.VMEM((4, top, 8, 128), jnp.float32),
+            pltpu.SemaphoreType.DMA((4, top)),
+            pltpu.SemaphoreType.DMA((4, top)),
         ],
         compiler_params=pltpu.CompilerParams(collective_id=cid, has_side_effects=True, vmem_limit_bytes=60 * 1024 * 1024),
         name="reduce_dense",
-    )(*arrays)
+    )(jnp.full((8, 128), squares, jnp.float32), *arrays)
 
 
 def mm(a, b):
@@ -490,10 +528,12 @@
 
 
 def pair_order(na, nb):
-    order = [(0, 0), (1, 0)] + [(1, t) for t in range(1, nb)]
-    for i in range(2, na):
+    order = [(0, 0), (1, 0)]
+    if na > 2:
+        order += [(2, 0)] + [(2, t) for t in range(1, nb)]
+    for i in range(3, na):
         order += [(i, t) for t in range(1, nb)] + [(i, 0)]
-    return order + [(0, t) for t in range(1, nb)]
+    return order + [(1, t) for t in range(1, nb)] + [(0, t) for t in range(1, nb)]
 
 
 def choose(index, values):
@@ -503,22 +543,32 @@
     return out
 
 
-def fused_kernel(n_dp, n_exp, experts, cap, x_ref, cot_ref, rank_ref, win_h, wdown_h, wshin_h, wshdown_h,
+def fused_kernel(n_dp, n_exp, experts, cap, halves, x_ref, cot_ref, rank_own, *refs):
+    win_h, wdown_h, refs = refs[:halves], refs[halves:2 * halves], refs[2 * halves:]
+    wrt_h, wshin_h, wshdown_h, xall, mixed, total_out, gg_out, refs = *refs[:7], refs[7:]
+    gin_out, gdown_out, refs = refs[:halves], refs[halves:2 * halves], refs[2 * halves:]
+    fused_body(n_dp, n_exp, experts, cap, x_ref, cot_ref, rank_own, win_h, wdown_h, wrt_h, wshin_h, wshdown_h,
+               xall, mixed, total_out, gg_out, gin_out, gdown_out, *refs)
+
+
+def fused_body(n_dp, n_exp, experts, cap, x_ref, cot_ref, rank_own, win_h, wdown_h, wrt_h, wshin_h, wshdown_h,
                  xall, mixed, total_out, gg_out, gin_out, gdown_out, gshin, gshdown, core_land, b_land, a_land,
-                 win, wdown, wshin, wshdown, xv, cv, xr_s, act_s, gr_s, dgu_s, back_s, mixed_s, held, bsrc, stage,
+                 win, wdown, wrt, wshin, wshdown, rank_ref, xv, cv, xr_s, act_s, gr_s, dgu_s, back_s, mixed_s, held, bsrc, stage,
                  gg_s, gin_acc, gdown_acc,
                  w_sem, x_sem, c_sem, m_sem, s_sem, ag_send, ag_recv, core_send, core_recv, b_send, b_recv,
-                 a_send, a_recv, g_send, g_recv):
+                 a_send, a_recv, g_send, g_recv, r_send, r_recv):
     low, wide = jnp.bfloat16, jnp.float32
     place = Place(n_dp, n_exp)
     na, nb = place.size["A"], place.size["B"]
     pos = place.pos
     a, c, me = pos["A"], pos["C"], place.expert(pos)
-    toks, d = x_ref.shape
+    toks, d = x_ref.shape[0], wdown.shape[1]
+    given = cot_ref.shape[2]
     hid = wshdown.shape[0]
     table = near_first(na)
     order = pair_order(na, nb)
     steps = len(order)
+    ahead = min(3, steps)
     near = [choose(a, [table[p][i] for p in range(na)]) for i in range(na)]
     sib = dict(pos, C=1 - c)
 
@@ -529,6 +579,21 @@
     for s in range(1, n_exp):
         pl.semaphore_signal(barrier, inc=1, device_id=(pos["Y"], lax.rem(me + s, n_exp)), device_id_type=MESH)
     pl.semaphore_wait(barrier, n_exp - 1)
+
+    def rank_copy(s):
+        j = lax.rem(me + s, n_exp)
+        return pltpu.make_async_remote_copy(
+            src_ref=rank_own.at[j], dst_ref=rank_ref.at[me], send_sem=r_send.at[j], recv_sem=r_recv.at[me],
+            device_id=(pos["Y"], j), device_id_type=MESH)
+
+    def rank_start(s, carry):
+        rank_copy(s).start()
+        return carry
+
+    def rank_landed(j):
+        pltpu.make_async_copy(rank_ref.at[j], rank_ref.at[j], r_recv.at[j]).wait()
+
+    rank_ref[me] = rank_own[me]
 
     counter = [0]
     ag_sends = []
@@ -581,6 +646,8 @@
 
             landed(j())
             ag(always, lambda j=j: xall.at[j()], j, lambda: sib)
+
+    lax.fori_loop(1, n_exp, rank_start, 0)
 
     before = {k: [] for k in range(steps)}
     for i in range(1, na):
@@ -590,8 +657,13 @@
         first = min(k for k, (q, t) in enumerate(order) if q == i and t)
         before[min(first, i + 1)].append(lambda i=i: side_arrival(i))
 
-    wloads = [pltpu.make_async_copy(h, v, w_sem.at[i]) for i, (h, v) in enumerate(
-        ((win_h, win), (wdown_h, wdown), (wshin_h, wshin), (wshdown_h, wshdown)))]
+    moves = [(wrt_h, wrt), (wshin_h, wshin), (wshdown_h, wshdown)]
+    for pieces, whole in ((win_h, win), (wdown_h, wdown)):
+        for n, piece in enumerate(pieces):
+            rows = piece.shape[0]
+            start = lax.rem(pos["Y"] + n, len(pieces)) * rows
+            moves.append((piece, whole.at[pl.ds(pl.multiple_of(start, 16), rows)]))
+    wloads = [pltpu.make_async_copy(h, v, w_sem.at[i]) for i, (h, v) in enumerate(moves)]
     for load in wloads:
         load.start()
 
@@ -603,7 +675,15 @@
 
     def cot_load(k, slot):
         one, two = pair_index(k)
-        return [pltpu.make_async_copy(cot_ref.at[j], cv.at[slot, n], c_sem.at[slot, n]) for n, j in enumerate((one, two))]
+        return [pltpu.make_async_copy(cot_ref.at[j], cv.at[slot, n, :, pl.ds(0, given)], c_sem.at[slot, n])
+                for n, j in enumerate((one, two))]
+
+    def x_load(src, n, slot):
+        loads = [pltpu.make_async_copy(src.at[:, pl.ds(0, d)], xv.at[n], x_sem.at[n, 0])]
+        if given < d:
+            loads.append(pltpu.make_async_copy(
+                src.at[:, pl.ds(d, d - given)], cv.at[slot, n, :, pl.ds(given, d - given)], x_sem.at[n, 1]))
+        return loads
 
     for load in cot_load(0, 0):
         load.start()
@@ -633,16 +713,24 @@
             src_ref=held.at[i], dst_ref=a_land.at[a], send_sem=a_send.at[i], recv_sem=a_recv.at[a],
             device_id=place.device(dict(pos, A=near[i])), device_id_type=MESH)
 
-    def fetch(ref, sem):
+    def fetch(ref, sem, n):
         pltpu.make_async_copy(ref, ref, sem).wait()
-        load = pltpu.make_async_copy(ref, stage, s_sem)
-        load.start()
-        load.wait()
-        return stage[...].astype(wide)
+        pltpu.make_async_copy(ref, stage.at[n], s_sem.at[n]).start()
+
+    def fetched(n):
+        pltpu.make_async_copy(stage.at[n], stage.at[n], s_sem.at[n]).wait()
+        return stage[n].astype(wide)
+
+    def core_fetch(k):
+        fetch(core_land.at[k], core_recv.at[k], 0)
+
+    def side_fetch(i):
+        for t in range(1, nb):
+            fetch(b_land.at[i * (nb - 1) + t - 1], b_recv.at[i * (nb - 1) + t - 1], t)
 
     def chip_sum(k):
         i, t = order[k]
-        value = (back_s[k % 2, 0].astype(wide) + fetch(core_land.at[k], core_recv.at[k])).astype(low)
+        value = (back_s[k % 2, 0].astype(wide) + fetched(0)).astype(low)
         if t:
             n = b_steps.index(k)
             if n >= 2:
@@ -655,28 +743,37 @@
     def side_sum(i):
         value = held[i].astype(wide)
         for t in range(1, nb):
-            value = value + fetch(b_land.at[i * (nb - 1) + t - 1], b_recv.at[i * (nb - 1) + t - 1])
+            value = value + fetched(t)
         held[i] = value.astype(low)
         if i:
             a_copy(i).start()
 
+    early = {k: [] for k in range(steps)}
     middle = {k: [] for k in range(steps)}
+    after = {k: [] for k in range(steps)}
     late = []
     for k in range(steps):
         if k + 1 < steps:
+            early[k + 1].append(lambda k=k: core_fetch(k))
             middle[k + 1].append(lambda k=k: chip_sum(k))
         else:
+            late.append(lambda k=k: core_fetch(k))
             late.append(lambda k=k: chip_sum(k))
-    for i in list(range(1, na)) + [0]:
-        ready = max(max(k for k, (q, t) in enumerate(order) if q == i and t) + 3, order.index((i, 0)) + 1)
-        if ready < steps:
-            middle[ready].append(lambda i=i: side_sum(i))
+    for i in list(range(2, na)) + [1, 0]:
+        sent = max([k for k, (q, t) in enumerate(order) if q == i and t], default=0)
+        ready = max(2 * (sent + 1) + 3, 2 * (order.index((i, 0)) + 1) + 1)
+        fetching, adding = (lambda i=i: side_fetch(i)), (lambda i=i: side_sum(i))
+        if ready // 2 >= steps:
+            late += [fetching, adding]
+        elif ready % 2:
+            after[ready // 2] += [fetching, adding]
         else:
-            late.append(lambda i=i: side_sum(i))
+            early[ready // 2].append(fetching)
+            middle[ready // 2].append(adding)
 
     def at(k, events):
         for n in range(steps):
-            if events[n]:
+            if events.get(n):
                 @pl.when(k == n)
                 def _(n=n):
                     for run in events[n]:
@@ -693,24 +790,29 @@
     def step(k, carry):
         slot = lax.rem(k, 2)
         one, two = pair_index(k)
-        at(k, before)
-
-        @pl.when(k == 0)
+        @pl.when(k < ahead)
         def _():
-            load = pltpu.make_async_copy(x_ref, xv.at[0], x_sem.at[0])
-            load.start()
+            at(k, {q: before[q] if q < ahead else [] for q in range(steps)})
+
+            @pl.when(k == 0)
+            def _():
+                for load in x_load(x_ref, 0, slot):
+                    load.start()
+
+            @pl.when(k > 0)
+            def _():
+                for load in x_load(xall.at[one], 0, slot):
+                    load.start()
+                rank_landed(one)
+
             landed(two)
-            load.wait()
-
-        @pl.when(k > 0)
-        def _():
-            load = pltpu.make_async_copy(xall.at[one], xv.at[0], x_sem.at[0])
-            load.start()
-            landed(two)
-            load.wait()
-
-        load_two = pltpu.make_async_copy(xall.at[two], xv.at[1], x_sem.at[1])
-        load_two.start()
+            for load in x_load(xall.at[two], 1, slot):
+                load.start()
+            rank_landed(two)
+
+        for n, j in enumerate((one, two)):
+            for load in x_load(xall.at[j], n, slot):
+                load.wait()
         for load in cot_load(k, slot):
             load.wait()
 
@@ -722,15 +824,15 @@
         ranks = (rank_ref[one], rank_ref[two])
         slots = lax.broadcasted_iota(jnp.int32, (cap, toks), 0).astype(wide)
         picks = [r == slots for r in ranks]
-        load_two.wait()
         crs = []
         for n in range(2):
             p = picks[n].astype(low)
             xr_s[n * cap:(n + 1) * cap, :] = mm(p, xv[n]).astype(low)
             crs.append(mm(p, cv[slot, n]).astype(low))
         cr = jnp.concatenate(crs, axis=0)
+        at(k, early)
         gu = mm(xr_s[...], win[...])
-        logits = gu[:, 2 * FF:]
+        logits = mm(xr_s[...], wrt[...])
         lane = lax.broadcasted_iota(jnp.int32, logits.shape, 1)
         logits = jnp.where(lane < experts, logits, -1e30)
         ex = jnp.exp(logits - jnp.max(logits, axis=1, keepdims=True))
@@ -748,7 +850,7 @@
         of = o.astype(wide)
         gg = jnp.sum(cr.astype(wide) * of, axis=1, keepdims=True)
         wtd = (gate * of).astype(low)
-        ib = mm_nt(dgu_s[...], win[:, :2 * FF]).astype(low)
+        ib = mm_nt(dgu_s[...], win[...]).astype(low)
         at(k, middle)
 
         @pl.when(k >= 2)
@@ -783,6 +885,20 @@
             gg_copy(k, 0, one).start()
 
         gg_copy(k, 1, two).start()
+        at(k, after)
+
+        @pl.when((k + 1 >= ahead) & (k + 1 < steps))
+        def _():
+            at(k, {q - 1: before[q] for q in range(ahead, steps)})
+            next_one, next_two = pair_index(k + 1)
+            for load in x_load(xall.at[next_one], 0, 1 - slot):
+                load.start()
+            landed(next_two)
+            for load in x_load(xall.at[next_two], 1, 1 - slot):
+                load.start()
+            rank_landed(next_one)
+            rank_landed(next_two)
+
         gdown_acc[...] += mm_tn(act_s[...], gr_s[...])
         gin_acc[...] += mm_tn(xr_s[...], dgu_s[...])
         at(k, {q: [lambda q=q: core_copy(q - 1).wait_send()] if q else [] for q in range(steps)})
@@ -790,10 +906,15 @@
 
     lax.fori_loop(0, steps, step, 0)
     gg_out[me] = gg_s[0, 0]
-    win[:, :2 * FF] = gin_acc[...].astype(low)
+    win[...] = gin_acc[...].astype(low)
     wdown[...] = gdown_acc[...].astype(low)
-    outs = [pltpu.make_async_copy(win.at[:, pl.ds(0, 2 * FF)], gin_out, w_sem.at[0]),
-            pltpu.make_async_copy(wdown, gdown_out, w_sem.at[1])]
+    outs = []
+    for pieces, whole in ((gin_out, win), (gdown_out, wdown)):
+        for n, piece in enumerate(pieces):
+            rows = piece.shape[0]
+            start = lax.rem(pos["Y"] + n, len(pieces)) * rows
+            outs.append(pltpu.make_async_copy(
+                whole.at[pl.ds(pl.multiple_of(start, 16), rows)], piece, w_sem.at[len(outs)]))
     for out in outs:
         out.start()
     for run in late:
@@ -801,9 +922,10 @@
     total = held[0].astype(wide)
     for s in range(1, na):
         j = lax.rem(a + s, na)
-        total = total + fetch(a_land.at[j], a_recv.at[j])
+        fetch(a_land.at[j], a_recv.at[j], 0)
+        total = total + fetched(0)
     gin_acc[:toks, :d] = total
-    last = pltpu.make_async_copy(gin_acc.at[pl.ds(0, toks), pl.ds(0, d)], total_out, s_sem)
+    last = pltpu.make_async_copy(gin_acc.at[pl.ds(0, toks), pl.ds(0, d)], total_out, s_sem.at[0])
     last.start()
     last.wait()
     for out in outs:
@@ -839,9 +961,15 @@
 
     lax.fori_loop(1, n_exp, gg_wait, 0)
 
-
-def fused(x, cot_all, rank, win, wdown, wshin, wshdown, n_dp, n_exp, experts, cap, cid):
-    toks, d = x.shape
+    def rank_sent(s, carry):
+        rank_copy(s).wait_send()
+        return carry
+
+    lax.fori_loop(1, n_exp, rank_sent, 0)
+
+
+def fused(x, cot_all, rank, win, wdown, wrt, wshin, wshdown, n_dp, n_exp, experts, cap, cid):
+    toks, d = x.shape[0], wshdown.shape[1]
     size = sizes(n_dp, n_exp)
     na, nb = size["A"], size["B"]
     steps = na * nb
@@ -854,107 +982,72 @@
     dma = pltpu.SemaphoreType.DMA
     ag_count = 2 + (nb - 1) + 1 + (na - 1) * (2 + nb) + na * (nb - 1)
     flops = 2 * n_exp * (cap * d * FF * 9 + toks * cap * d * 4 + toks * d * hid * 9)
-    return pl.pallas_call(
-        functools.partial(fused_kernel, n_dp, n_exp, experts, cap),
-        in_specs=[hbm, hbm, vmem, hbm, hbm, hbm, hbm],
+    out = pl.pallas_call(
+        functools.partial(fused_kernel, n_dp, n_exp, experts, cap, len(win)),
+        in_specs=[hbm, hbm, vmem] + [hbm] * (2 * len(win) + 3),
         out_shape=[
-            jax.ShapeDtypeStruct((n_exp,) + block, low),
+            jax.ShapeDtypeStruct((n_exp,) + x.shape, low),
             jax.ShapeDtypeStruct((n_exp,) + block, low),
             jax.ShapeDtypeStruct(block, wide),
             jax.ShapeDtypeStruct((n_exp, 1, toks), wide),
-            jax.ShapeDtypeStruct((d, 2 * FF), low),
-            jax.ShapeDtypeStruct((FF, d), low),
+            *[jax.ShapeDtypeStruct(w.shape, low) for w in (*win, *wdown)],
             jax.ShapeDtypeStruct((d, 2 * hid), wide),
             jax.ShapeDtypeStruct((hid, d), wide),
             jax.ShapeDtypeStruct((steps,) + block, low),
             jax.ShapeDtypeStruct((na * max(nb - 1, 1),) + block, low),
             jax.ShapeDtypeStruct((na,) + block, low),
         ],
-        out_specs=[hbm, hbm, hbm, vmem, hbm, hbm, vmem, vmem, hbm, hbm, hbm],
+        out_specs=[hbm, hbm, hbm, vmem] + [hbm] * (2 * len(win)) + [vmem, vmem, hbm, hbm, hbm],
         scratch_shapes=[
-            pltpu.VMEM(win.shape, low), pltpu.VMEM(wdown.shape, low), pltpu.VMEM(wshin.shape, low),
-            pltpu.VMEM(wshdown.shape, low),
+            pltpu.VMEM((d, 2 * FF), low), pltpu.VMEM((FF, d), low), pltpu.VMEM(wrt.shape, low),
+            pltpu.VMEM(wshin.shape, low), pltpu.VMEM(wshdown.shape, low), pltpu.VMEM((n_exp, 1, toks), wide),
             pltpu.VMEM((2,) + block, low), pltpu.VMEM((2, 2) + block, low),
             pltpu.VMEM((rows, d), low), pltpu.VMEM((rows, FF), low), pltpu.VMEM((rows, d), low),
             pltpu.VMEM((rows, 2 * FF), low),
             pltpu.VMEM((2, 2) + block, low), pltpu.VMEM((2, 2) + block, low), pltpu.VMEM((na,) + block, low),
-            pltpu.VMEM((2,) + block, low), pltpu.VMEM(block, low),
+            pltpu.VMEM((2,) + block, low), pltpu.VMEM((nb,) + block, low),
             pltpu.VMEM((steps, 2, 1, toks), wide), pltpu.VMEM((d, 2 * FF), wide), pltpu.VMEM((FF, d), wide),
-            dma((4,)), dma((2,)), dma((2, 2)), dma((2, 2)), dma(()),
+            dma((3 + 2 * len(win),)), dma((2, 2)), dma((2, 2)), dma((2, 2)), dma((nb,)),
             dma((ag_count,)), dma((n_exp,)), dma((steps,)), dma((steps,)),
             dma((na * max(nb - 1, 1),)), dma((na * max(nb - 1, 1),)), dma((na,)), dma((na,)),
-            dma((steps, 2)), dma((n_exp,)),
+            dma((steps, 2)), dma((n_exp,)), dma((n_exp,)), dma((n_exp,)),
         ],
         compiler_params=pltpu.CompilerParams(collective_id=cid, has_side_effects=True, vmem_limit_bytes=63 * 1024 * 1024),
         cost_estimate=pl.CostEstimate(flops=flops, bytes_accessed=100 * 1024 * 1024, transcendentals=0),
         name="experts_fused",
-    )(x, cot_all, rank, win, wdown, wshin, wshdown)
-
-
-def spread_kernel(n_dp, n_exp, x_ref, out_ref, send_sem, recv_sem):
-    n = n_dp * n_exp
-    me = lax.axis_index("dp") * n_exp + lax.axis_index("expert")
-    barrier = pltpu.get_barrier_semaphore()
-
-    def device(step):
-        to = lax.rem(me + step, n)
-        return (to // n_exp, lax.rem(to, n_exp))
-
-    def greet(step, carry):
-        pl.semaphore_signal(barrier, inc=1, device_id=device(step), device_id_type=MESH)
-        return carry
-
-    lax.fori_loop(1, n, greet, 0)
-    pl.semaphore_wait(barrier, n - 1)
-
-    def copy(step):
-        return pltpu.make_async_remote_copy(
-            src_ref=x_ref, dst_ref=out_ref.at[step], send_sem=send_sem.at[step], recv_sem=recv_sem.at[step],
-            device_id=device(step), device_id_type=MESH)
-
-    def start(step, carry):
-        copy(step).start()
-        return carry
-
-    def wait(step, carry):
-        copy(step).wait()
-        return carry
-
-    lax.fori_loop(1, n, start, 0)
-    out_ref[0] = x_ref[...]
-    lax.fori_loop(1, n, wait, 0)
-
-
-def sum_everywhere(value, n_dp, n_exp, cid):
-    n = n_dp * n_exp
-    parts = pl.pallas_call(
-        functools.partial(spread_kernel, n_dp, n_exp),
-        out_shape=jax.ShapeDtypeStruct((n, 8, 128), jnp.float32),
-        in_specs=[pl.BlockSpec(memory_space=pltpu.VMEM)],
-        out_specs=pl.BlockSpec(memory_space=pltpu.VMEM),
-        scratch_shapes=[pltpu.SemaphoreType.DMA((n,)), pltpu.SemaphoreType.DMA((n,))],
-        compiler_params=pltpu.CompilerParams(collective_id=cid, has_side_effects=True),
-        name="sum_everywhere",
-    )(jnp.full((8, 128), value, jnp.float32))
-    return jnp.sum(parts[:, 0, 0])
+    )(x, cot_all, rank, *win, *wdown, wrt, wshin, wshdown)
+    n = len(win)
+    return out[1], out[2], out[3], out[4:4 + n], out[4 + n:4 + 2 * n], out[4 + 2 * n], out[5 + 2 * n]
 
 
 def swap_rows(x, n_dp):
     if n_dp != 2:
-        return lax.all_gather(x, "dp", axis=0, tiled=True)
-    other = lax.ppermute(x, "dp", [(0, 1), (1, 0)])
+        return [lax.all_gather(x, "dp", axis=0, tiled=True)]
+    return [x, lax.ppermute(x, "dp", [(0, 1), (1, 0)])]
+
+
+def in_order(pieces):
+    if len(pieces) == 1:
+        return pieces[0]
     first = lax.axis_index("dp") == 0
+    x, other = pieces
     return jnp.concatenate([jnp.where(first, x, other), jnp.where(first, other, x)], axis=0)
 
 
-def halve_rows(x, n_dp):
+def halve_rows(pieces, n_dp):
     if n_dp != 2:
-        return lax.psum_scatter(x, "dp", scatter_dimension=0, tiled=True).astype(jnp.float32)
+        return lax.psum_scatter(pieces[0], "dp", scatter_dimension=0, tiled=True).astype(jnp.float32)
+    other = lax.ppermute(pieces[1], "dp", [(0, 1), (1, 0)])
+    return pieces[0].astype(jnp.float32) + other.astype(jnp.float32)
+
+
+def split_rows(x, n_dp):
+    if n_dp != 2:
+        return [x]
     rows = x.shape[0] // 2
+    top, bottom = x[:rows], x[rows:]
     first = lax.axis_index("dp") == 0
-    top, bottom = x[:rows], x[rows:]
-    other = lax.ppermute(jnp.where(first, bottom, top), "dp", [(0, 1), (1, 0)])
-    return jnp.where(first, top, bottom).astype(jnp.float32) + other.astype(jnp.float32)
+    return [jnp.where(first, top, bottom), jnp.where(first, bottom, top)]
 
 
 def local(
@@ -999,20 +1092,19 @@
     score_scale = HD ** (-0.5)
     rows_w = w_qkv.shape[0]
     unit = w_shared_down.shape[0]
-    my_expert = lax.axis_index("expert")
 
     pad = jnp.zeros((rows_w, 128 - expert_count - 2), wide)
     packed = jnp.concatenate([w_qkv, w_out, w_router, norm_gains.T, pad], axis=1).astype(low)
     full = gather(packed, n_dp, n_exp, True, 1).reshape(D, -1)
+    full, ein_low = lax.optimization_barrier((full, w_expert_in[0].astype(low)))
+    expert_in_full = swap_rows(ein_low, n_dp)
     qkv_full = full[:, : 3 * H * HD]
     out_full = full[:, 3 * H * HD : 3 * H * HD + D]
     small_full = full[:, 3 * H * HD + D :]
     router_full = small_full[:, :expert_count]
     gain_one = small_full[:, expert_count].astype(wide)
     gain_two = small_full[:, expert_count + 1].astype(wide)
-    cot_all = lax.all_gather(cotangent, "expert", axis=0, tiled=False)
-    routes_all = lax.all_gather(routes, "expert", axis=0, tiled=False)
-    expert_in_full = swap_rows(w_expert_in[0].astype(low), n_dp)
+    cot_all = lax.all_gather(cotangent[:, :GIVEN], "expert", axis=0, tiled=False)
     expert_down_full = swap_rows(w_expert_down[0].astype(low), n_dp)
     shin_send = (
         w_shared_in.astype(low)
@@ -1022,7 +1114,7 @@
     )
     shin_send = jnp.concatenate([shin_send] * n_dp, axis=0)
     shin_mine = lax.all_to_all(shin_send, both, 0, 0, tiled=True).reshape(D, 2 * n_dp * unit)
-    shdown_mine = swap_rows(w_shared_down.astype(low), n_dp)
+    shdown_mine = in_order(swap_rows(w_shared_down.astype(low), n_dp))
     half = n_dp * unit
 
     inputs = tokens.astype(wide)
@@ -1053,19 +1145,18 @@
     logits = jnp.dot(mlp_in, router_full, preferred_element_type=wide)
     router_probs = jax.nn.softmax(logits, axis=-1)
 
-    routed_here = jnp.any(routes_all == my_expert, axis=2)
-    rank = jnp.where(routed_here, jnp.cumsum(routed_here.astype(jnp.int32), axis=1) - 1, -1).astype(wide)
+    routed = jnp.any(routes[:, :, None] == jnp.arange(expert_count, dtype=jnp.int32), axis=1)
+    rank = jnp.where(routed, jnp.cumsum(routed.astype(jnp.int32), axis=0) - 1, -1).astype(wide).T
     hid = (half + 127) // 128 * 128
     cap = (capacity + 15) // 16 * 16
-    win = jnp.concatenate([expert_in_full, router_full, jnp.zeros((D, 128 - expert_count), low)], axis=1)
+    wrt = jnp.concatenate([router_full, jnp.zeros((D, 128 - expert_count), low)], axis=1)
     gap = jnp.zeros((D, hid - half), low)
     wshin = jnp.concatenate([shin_mine[:, :half], gap, shin_mine[:, half:], gap], axis=1)
     wshdown = jnp.concatenate([shdown_mine, jnp.zeros((hid - half, D), low)], axis=0)
-    _, mixed_part, back_sum, gate_grad, grad_ein, grad_edown, shin_wide, shdown_wide, _, _, _ = fused(
-        mlp_in, cot_all, rank[:, None, :], win, expert_down_full, wshin, wshdown, n_dp, n_exp, expert_count, cap, 2
+    mixed_part, back_sum, gate_grad, grad_ein, grad_edown, shin_wide, shdown_wide = fused(
+        jnp.concatenate([mlp_in, cotangent[:, GIVEN:]], axis=1), cot_all, rank[:, None, :], expert_in_full, expert_down_full, wrt, wshin, wshdown, n_dp, n_exp, expert_count, cap, 2
     )
     mixed_sum = lax.psum_scatter(mixed_part, "expert", scatter_dimension=0, tiled=False)
-    mixed = (residual + mixed_sum.astype(wide)).astype(low)
     grad_shin = jnp.concatenate([shin_wide[:, :half], shin_wide[:, hid : hid + half]], axis=1)
     grad_shdown = shdown_wide[:half]
     prob_grad = gate_grad[:, 0, :].T
@@ -1119,9 +1210,6 @@
         [grad_router, grad_gain_one[:, None], grad_gain_two[:, None], jnp.zeros((D, 128 - expert_count - 2), wide)],
         axis=1,
     )
-    qkv_own, out_own, small_own = reduce_dense(
-        [g.astype(low).reshape(n_all, rows_w, -1) for g in (grad_qkv, grad_out, small_grad)], n_dp, n_exp, 5
-    )
     shin_back = lax.all_to_all(
         grad_shin.astype(low).reshape(n_all, rows_w, 2 * half), both, 0, 0, tiled=True
     )
@@ -1129,18 +1217,26 @@
         shin_back.reshape(n_dp, n_exp, rows_w, 2, n_dp, unit).astype(wide), axis=0
     )
     shin_own = shin_own.transpose(1, 2, 3, 0, 4).reshape(rows_w, 2 * FF)
+    shdown_own = halve_rows(split_rows(grad_shdown, n_dp), n_dp)
+    ein_own = halve_rows(grad_ein, n_dp)
+    edown_own = halve_rows(grad_edown, n_dp)
+    squares = sum(jnp.sum(g * g) for g in (shin_own, shdown_own, ein_own, edown_own))
+    qkv_own, out_own, small_own, norm = reduce_dense(
+        [g.astype(low).reshape(n_all, rows_w, -1) for g in (grad_qkv, grad_out, small_grad)], squares, n_dp, n_exp, 5
+    )
+    qkv_own, mixed_sum = lax.optimization_barrier((qkv_own, mixed_sum))
+    mixed = (residual + mixed_sum.astype(wide)).astype(low)
     owned_grads = (
         small_own[:, expert_count : expert_count + 2].T,
         qkv_own,
         out_own,
         shin_own,
-        lax.psum_scatter(grad_shdown, "dp", scatter_dimension=0, tiled=True),
+        shdown_own,
         small_own[:, :expert_count],
-        halve_rows(grad_ein, n_dp)[None],
-        halve_rows(grad_edown, n_dp)[None],
-    )
-    squares = sum((jnp.sum(grad_part * grad_part) for grad_part in owned_grads))
-    total_squares = sum_everywhere(squares, n_dp, n_exp, 6)
+        ein_own[None],
+        edown_own[None],
+    )
+    total_squares = norm[0, 0]
     grad_norm = jnp.sqrt(total_squares)
     factor = jnp.minimum(1.0, CLIP / grad_norm)
     weights = (

time: 865 us -> 715 us (0.83)
  blocking collectives: 104 us -> 0 us
  other arithmetic: 96.4 us -> 75.3 us
  local copies, waits for them, and re-layouts: 50.1 us -> 38.1 us
    unnamed x1 -> x0, blocking collectives: 75.5 us -> none
    ppermute x5 -> x6, waiting for transfers between devices: 0.01 us -> 42.5 us  [the longest x3 34.4 us: swap_rows(): return [x, lax.ppermute(x, 'dp', [(0, 1), (1, 0)])]]
    reduce_scatter x1, waiting for transfers between devices: 29.1 us -> 0.02 us  [local(): lax.psum_scatter(mixed_part, 'expert', scatter_dimension=0, tiled=False)]
    all_gather x1 -> x0, blocking collectives: 28.4 us -> none  [local(): routes_all = lax.all_gather(routes, 'expert', axis=0, tiled=False)]
    pallas_call x1, Pallas kernels: 90.8 us -> 116 us  [reduce_dense(): pl.pallas_call(functools.partial(reduce_kernel, n_dp, n_exp, orders, slic...]
    pallas_call x2 -> x1, Pallas kernels: 269 us -> 247 us  [fused(): pl.pallas_call(functools.partial(fused_kernel, n_dp, n_exp, experts, cap,...]
    reduce_sum x9 -> x4, other arithmetic: 20.6 us -> 10.6 us  [local(): jnp.sum(g * g)]
  transfers between devices with their start and end apart: 10 -> 10, of which waited for: 2 -> 2; matrix products, arithmetic and copies ran while one was open for 21% -> 22% of each run, Pallas kernels for 12% -> 30%
where the time goes in v4:
time: 715 us; the launch traced here: 710 us
  Pallas kernels  459 us (64%)
  other arithmetic  75.3 us (11%)
  matrix products  60.5 us (8%)
  waiting for transfers between devices  43.2 us (6%)
  local copies, waits for them, and re-layouts  38.1 us (5%)
  between operations  19.7 us (3%)
  starting transfers between devices  13.6 us (2%)
    pallas_call x1, Pallas kernels, fused(): pl.pallas_call(functools.partial(fused_kernel, n_dp, n_exp, experts, cap,...  247 us
    pallas_call x1, Pallas kernels, reduce_dense(): pl.pallas_call(functools.partial(reduce_kernel, n_dp, n_exp, orders, slic...  116 us
    pallas_call x1, Pallas kernels, gather(): pl.pallas_call(functools.partial(gather_kernel, n_dp, n_exp, orders, slic...  96.5 us
    ppermute x3, waiting for transfers between devices, swap_rows(): return [x, lax.ppermute(x, 'dp', [(0, 1), (1, 0)])]  34.4 us
    sub x8, other arithmetic, adam_update(): weight - step_rate * (first_hat / (jnp.sqrt(second_hat) + ADAM_EPS) + dec...  22.8 us
    unnamed x154, local copies, waits for them, and re-layouts  16.4 us
  transfers between devices with their start and end apart: 10, of which 2 were waited for; matrix products, arithmetic and copies ran while one was open for 22% of the time, Pallas kernels for 30%

profile of v4, /device:TPU:0, one launch (start us, length us, event | category | flops | bytes accessed | tf_op | source)
XLA Modules:
  0.0 709.7 jit_solution(13375433347497878196)
XLA Ops:
  12.4 96.5 %gather_dense.1 = bf16[32,40,5248]{2,1,0:T(8,128)(2,1)} custom-call(bf16[40,5248]{1,0:T(8,128)(2,1)} %concatenate.54.x_ref), custom_call_target="tpu_custom_call" | custom-call | tf_op jit(solution)/shard_map/gather_dense/pallas_call | solution.py:277
  108.9 4.1 convert_bitcast_fusion.refs_0_
  119.5 2.9 all-to-all-start
  130.5 8.1 %fusion.3 = f32[384,3840]{0,1:T(8,128)S(1)} fusion(bf16[1280,5248]{1,0:T(8,128)(2,1)} %bitcast.142, bf16[384,1280]{1,0:T(8,128)(2,1)S(1)} %copy-done.13, f32[1280]{0:T(1024)S(1)} %get-tuple-element.197, f32[384]{0:T(512)S(1)} %add_rsqrt_fusion.1), kind=kOutput, calls=%fused_computation.4 | convolution fusion | flops 3776839680 | bytes 16718336 | tf_op jit(solution)/shard_map/dot_general | solution.py:1125
  141.9 5.9 fusion.98
  147.8 4.2 fusion.42
  152.0 4.0 multiply_reduce_fusion.5
  161.0 34.4 %collective-permute-done.2 = bf16[28,1280]{1,0:T(8,128)(2,1)} collective-permute-done((bf16[28,1280]{1,0:T(8,128)(2,1)}, bf16[28,1280]{1,0:T(8,128)(2,1)}, u32[]{:S(2)}, u32[]{:S(2)}) %collective-permute-start.2) | collective-permute-done | bytes 71712 | tf_op jit(solution)/shard_map/ppermute | solution.py:1026
  198.6 246.9 %experts_fused.1 = (bf16[16,384,1280]{2,1,0:T(8,128)(2,1)}, bf16[16,384,1280]{2,1,0:T(8,128)(2,1)}, f32[384,1280]{1,0:T(8,128)}, f32[16,1,384]{2,1,0:T(1,128)}, ...) custom-call(bf16[384,1280]{1,0:T(8,128)(2,1)} %multiply_convert_fusi, ...), custom_call_target="tpu_custom_call" | custom-call | flops 93616865280 | bytes 104857600 | tf_op jit(solution)/shard_map/experts_fused/pallas_call | solution.py:985
  454.5 2.8 all-to-all-start.1
  459.2 1.8 collective-permute-start.3
  463.1 3.6 multiply_reduce_fusion.3
  468.6 4.7 fusion.19
  473.3 2.2 copy.221
  475.5 4.7 multiply_reduce_fusion
  491.2 8.5 %convolution_convert_fusion = bf16[1280,3840]{1,0:T(8,128)(2,1)} fusion(bf16[384,3840]{0,1:T(8,128)(2,1)S(1)} %bitcast.162, bf16[384,1280]{1,0:T(8,128)(2,1)S(1)} %copy-done.14, f32[1280]{0:T(1024)S(1)} %copy-done.44, f32[384]{0:T(512)S(1)} %copy-done.52), kind=kOutput, calls=%fused_computation.1 | convolution fusion | flops 3781754880 | bytes 13769216 | tf_op jit(solution)/shard_map/td,tk->dk/dot_general | solution.py:1201
  499.7 8.6 %fusion.27 = (f32[384]{0:T(512)S(1)}, bf16[1280]{0:T(1024)(128)(2,1)}, f32[384,1280]{1,0:T(8,128)}) fusion(bf16[384,1280]{1,0:T(8,128)(2,1)} %param.28, f32[1280]{0:T(1024)S(1)} %copy-done.44, f32[384]{0:T(512)S(1)} %copy-done.52, bf16[384,3840]{0,1:T(8,128)(2,1)} %bitcast.163, bf16[1280,5248]{1,0:T(8,128)(2,1)S(1)} %bitcast.150), kind=kOutput, calls=%fused_computation.48 | convolution fusion | flops 3778312448 | bytes 15742976 | tf_op jit(solution)/shard_map/tk,dk->td/dot_general | solution.py:1202
  508.4 3.7 fusion.30
  512.1 3.6 convolution_convert_fusion.1
  520.4 2.3 multiply_reduce_fusion.7
  522.7 3.6 reshape.255
  526.4 4.3 reduce_sum.158
  530.7 1.9 multiply_reduce_fusion.6
  534.0 8.0 %collective-permute-done.5 = bf16[448,1280]{1,0:T(8,128)(2,1)} collective-permute-done((bf16[448,1280]{1,0:T(8,128)(2,1)}, bf16[448,1280]{1,0:T(8,128)(2,1)}, u32[]{:S(2)}, u32[]{:S(2)}) %collective-permute-start.5) | collective-permute-done | bytes 1146912 | tf_op jit(solution)/shard_map/ppermute | solution.py:1040
  542.0 2.9 multiply_reduce_fusion.2
  544.9 3.4 multiply_reduce_fusion.1
  550.2 115.9 %reduce_dense.1 = (f32[40,3840]{1,0:T(8,128)}, f32[40,1280]{1,0:T(8,128)}, f32[40,128]{1,0:T(8,128)}, f32[8,128]{1,0:T(8,128)}) custom-call(f32[8,128]{1,0:T(8,128)} %broadcast_in_dim.49.sq_ref, bf16[32,40,3840]{2,1,0:T(8,128)(2,1)} %bitcast.155, bf16[32,40,1280]{2,1,0:T(8,128)(2,1)} %bitcast.160, bf16[32,40,128]{2,1,0:T(8,128)(2,1)} %maximum_maximum_fusion.1.refs_2_), custom_call_target="tpu_custom_call" | custom-call | tf_op jit(solution)/shard_map/reduce_dense/pallas_call | solution.py:486
  676.2 2.1 multiply_subtract_fusion.5
  678.2 2.3 multiply_subtract_fusion.4
  681.6 7.1 multiply_subtract_fusion.1
  688.7 8.7 %multiply_subtract_fusion = (f32[1,640,1792]{2,1,0:T(8,128)}, f32[1,640,1792]{2,1,0:T(8,128)}, f32[1,640,1792]{2,1,0:T(8,128)}) fusion(f32[1,640,1792]{2,1,0:T(8,128)S(1)} %bitcast.140, f32[]{:T(128)S(6)} %min.3, bf16[640,1792]{1,0:T(8,128)(2,1)} %collective-permute-done.4, bf16[640,1792]{1,0:T(8,128)(2,1)S(1)} %copy-done.6, ...), kind=kLoop, calls=%fused_computation.15 | loop fusion | flops 21790720 | bytes 32112644 | tf_op jit(solution)/shard_map/sub | solution.py:87
  697.5 2.5 add_convert_fusion
  (266 shorter events, 73.8 us)
Async XLA Ops:
  7.2 191.4 %all-gather.3.cloned.1.call-start = ((), (), s32[]{:S(2)}) async-start(), calls=%async_computation.4 | async-start | bytes 16711680 | tf_op jit(solution)/shard_map/all_gather | solution.py:1107
  113.0 85.6 %collective-permute-start = (bf16[640,1792]{1,0:T(8,128)(2,1)}, bf16[640,1792]{1,0:T(8,128)(2,1)}, u32[]{:S(2)}, u32[]{:S(2)}) collective-permute-start(bf16[640,1792]{1,0:T(8,128)(2,1)} %convert_bitcast_fusion.refs_0_), channel_id=1, source_target_pairs={{0,16},{16,0},{1,17},{17,1},{2,18},{18,2},{3,19},{19,3},{4,20},{20... | collective-permute-start | bytes 6881288 | tf_op jit(solution)/shard_map/ppermute | solution.py:1026
  115.7 9.3 %copy-start.59 = (s32[1,4]{1,0:T(1,128)S(1)}, s32[1,4]{1,0:T(1,128)}, u32[]{:S(2)}) copy-start(s32[1,4]{1,0:T(1,128)} %param.29) | copy-start | bytes 52
  115.7 9.5 %copy-start.50 = (s32[384,6]{0,1:T(8,128)S(1)}, s32[384,6]{0,1:T(8,128)}, u32[]{:S(2)}) copy-start(s32[384,6]{0,1:T(8,128)} %param.30) | copy-start | bytes 27652
  115.7 82.9 %collective-permute-start.1 = (bf16[448,1280]{1,0:T(8,128)(2,1)}, bf16[448,1280]{1,0:T(8,128)(2,1)}, u32[]{:S(2)}, u32[]{:S(2)}) collective-permute-start(bf16[448,1280]{1,0:T(8,128)(2,1)} %convert_bitcast_fusion.1.refs_2_), channel_id=1, source_target_pairs={{0,16},{16,0},{1,17},{17,1},{2,18},{18,2},{3,19},{19,3},{4,20},{20... | collective-permute-start | bytes 3440648 | tf_op jit(solution)/shard_map/ppermute | solution.py:1026
  118.3 11.1 %copy-start.13 = (bf16[384,1280]{1,0:T(8,128)(2,1)S(1)}, bf16[384,1280]{1,0:T(8,128)(2,1)}, u32[]{:S(2)}) copy-start(bf16[384,1280]{1,0:T(8,128)(2,1)} %param.28) | copy-start | bytes 2949124
  119.5 77.7 %all-to-all-start = ((bf16[32,40,112]{2,1,0:T(8,128)(2,1)}), bf16[32,40,112]{2,1,0:T(8,128)(2,1)S(1)}, u32[]{:S(2)}, u32[]{:S(2)}) async-start(bf16[32,40,112]{2,1,0:T(8,128)(2,1)} %pad_maximum_fusion.2), calls=%async_computation | async-start | bytes 655360 | tf_op jit(solution)/shard_map/all_to_all | solution.py:1116
  122.4 575.1 %reduce-scatter.2.cloned.1.call-start = ((), (), s32[]{:S(2)}) async-start(), calls=%async_computation.3 | async-start | bytes 16711680 | tf_op jit(solution)/shard_map/reduce_scatter | solution.py:1159
  123.2 72.1 %collective-permute-start.2 = (bf16[28,1280]{1,0:T(8,128)(2,1)}, bf16[28,1280]{1,0:T(8,128)(2,1)}, u32[]{:S(2)}, u32[]{:S(2)}) collective-permute-start(bf16[28,1280]{1,0:T(8,128)(2,1)} %convert_element_type.156), channel_id=1, source_target_pairs={{0,16},{16,0},{1,17},{17,1},{2,18},{18,2},{3,19},{19,3},{4,20},{20... | collective-permute-start | bytes 215048 | tf_op jit(solution)/shard_map/ppermute | solution.py:1026
  129.4 9.2 %copy-start.43 = (f32[1280]{0:T(1024)}, f32[1280]{0:T(1024)S(1)}, u32[]{:S(2)}) copy-start(f32[1280]{0:T(1024)S(1)} %get-tuple-element.197) | copy-start | bytes 15364
  129.7 8.9 %copy-start.51 = (f32[384]{0:T(512)}, f32[384]{0:T(512)S(1)}, u32[]{:S(2)}) copy-start(f32[384]{0:T(512)S(1)} %add_rsqrt_fusion.1) | copy-start | bytes 4612
  451.7 11.4 %copy-start.41 = (f32[384]{0:T(512)}, f32[384]{0:T(512)S(1)}, u32[]{:S(2)}) copy-start(f32[384]{0:T(512)S(1)} %fusion.74) | copy-start | bytes 4612
  451.7 11.3 %copy-start.34 = (f32[16,1,384]{2,1,0:T(1,128)S(1)}, f32[16,1,384]{2,1,0:T(1,128)}, u32[]{:S(2)}) copy-start(f32[16,1,384]{2,1,0:T(1,128)} %get-tuple-element.53) | copy-start | bytes 73732
  451.7 11.3 %copy-start.1 = (f32[384,1280]{1,0:T(8,128)S(1)}, f32[384,1280]{1,0:T(8,128)}, u32[]{:S(2)}) copy-start(f32[384,1280]{1,0:T(8,128)} %copy-done) | copy-start | bytes 5898244
  454.5 68.2 %all-to-all-start.1 = ((bf16[32,40,112]{2,1,0:T(8,128)(2,1)}), bf16[32,40,112]{2,1,0:T(8,128)(2,1)S(1)}, u32[]{:S(2)}, u32[]{:S(2)}) async-start(bf16[32,40,112]{2,1,0:T(8,128)(2,1)} %pad_maximum_fusion.3), calls=%async_computation.1 | async-start | bytes 655360 | tf_op jit(solution)/shard_map/all_to_all | solution.py:1213
  459.2 61.3 %collective-permute-start.3 = (f32[28,1280]{1,0:T(8,128)}, f32[28,1280]{1,0:T(8,128)S(1)}, u32[]{:S(2)}, u32[]{:S(2)}) collective-permute-start(f32[28,1280]{1,0:T(8,128)} %slice_select_fusion), channel_id=1, source_target_pairs={{0,16},{16,0},{1,17},{17,1},{2,18},{18,2},{3,19},{19,3},{4,20},{20... | collective-permute-start | bytes 430088 | tf_op jit(solution)/shard_map/ppermute | solution.py:1040
  461.0 83.9 %collective-permute-start.4 = (bf16[640,1792]{1,0:T(8,128)(2,1)}, bf16[640,1792]{1,0:T(8,128)(2,1)}, u32[]{:S(2)}, u32[]{:S(2)}) collective-permute-start(bf16[640,1792]{1,0:T(8,128)(2,1)} %get-tuple-element.49), channel_id=1, source_target_pairs={{0,16},{16,0},{1,17},{17,1},{2,18},{18,2},{3,19},{19,3},{4,20},{20... | collective-permute-start | bytes 6881288 | tf_op jit(solution)/shard_map/ppermute | solution.py:1040
  461.2 80.8 %collective-permute-start.5 = (bf16[448,1280]{1,0:T(8,128)(2,1)}, bf16[448,1280]{1,0:T(8,128)(2,1)}, u32[]{:S(2)}, u32[]{:S(2)}) collective-permute-start(bf16[448,1280]{1,0:T(8,128)(2,1)} %get-tuple-element.51), channel_id=1, source_target_pairs={{0,16},{16,0},{1,17},{17,1},{2,18},{18,2},{3,19},{19,3},{4,20},{20... | collective-permute-start | bytes 3440648 | tf_op jit(solution)/shard_map/ppermute | solution.py:1040
  487.4 12.3 %slice-start.2 = ((s8[13434880]{0:T(1024)(128)(4,1)}), s8[4194304]{0:T(1024)(128)(4,1)S(1)}, s32[]{:S(2)}) async-start(s8[13434880]{0:T(1024)(128)(4,1)} %bitcast.148), calls=%async_computation.7 | async-start | bytes 8388608
  487.4 12.3 %slice-start.3 = ((s8[13434880]{0:T(1024)(128)(4,1)}), s8[4194304]{0:T(1024)(128)(4,1)S(1)}, s32[]{:S(2)}) async-start(s8[13434880]{0:T(1024)(128)(4,1)} %bitcast.148), calls=%async_computation.8 | async-start | bytes 8388608
  488.6 11.1 %slice-start.4 = ((s8[13434880]{0:T(1024)(128)(4,1)}), s8[4194304]{0:T(1024)(128)(4,1)S(1)}, s32[]{:S(2)}) async-start(s8[13434880]{0:T(1024)(128)(4,1)} %bitcast.148), calls=%async_computation.9 | async-start | bytes 8388608
  491.2 8.5 %slice-start.5 = ((s8[13434880]{0:T(1024)(128)(4,1)}), s8[851968]{0:T(1024)(128)(4,1)S(1)}, s32[]{:S(2)}) async-start(s8[13434880]{0:T(1024)(128)(4,1)} %bitcast.148), calls=%async_computation.10 | async-start | bytes 1703936
  499.7 8.6 %copy-start.10 = (f32[384,1280]{1,0:T(8,128)S(1)}, f32[384,1280]{1,0:T(8,128)}, u32[]{:S(2)}) copy-start(f32[384,1280]{1,0:T(8,128)} %copy-done.9) | copy-start | bytes 5898244
  533.9 10.9 %copy-start.5 = (bf16[640,1792]{1,0:T(8,128)(2,1)S(1)}, bf16[640,1792]{1,0:T(8,128)(2,1)}, u32[]{:S(2)}) copy-start(bf16[640,1792]{1,0:T(8,128)(2,1)} %get-tuple-element.48) | copy-start | bytes 6881284
  550.2 117.9 %copy-start.38 = (f32[2,40]{0,1:T(8,128)S(1)}, f32[2,40]{0,1:T(8,128)}, u32[]{:S(2)}) copy-start(f32[2,40]{0,1:T(8,128)} %copy.231) | copy-start | bytes 964
  550.2 117.9 %copy-start.39 = (f32[2,40]{0,1:T(8,128)S(1)}, f32[2,40]{0,1:T(8,128)}, u32[]{:S(2)}) copy-start(f32[2,40]{0,1:T(8,128)} %copy.230) | copy-start | bytes 964
  550.2 118.9 %copy-start.56 = (f32[2,40]{1,0:T(2,128)S(1)}, f32[2,40]{1,0:T(2,128)}, u32[]{:S(2)}) copy-start(f32[2,40]{1,0:T(2,128)} %param.32) | copy-start | bytes 964
  550.2 119.0 %copy-start.40 = (f32[2,40]{0,1:T(8,128)S(1)}, f32[2,40]{0,1:T(8,128)}, u32[]{:S(2)}) copy-start(f32[2,40]{0,1:T(8,128)} %copy.234) | copy-start | bytes 964
  678.2 10.5 %slice-start = ((s8[4587520]{0:T(1024)(128)(4,1)}), s8[4194304]{0:T(1024)(128)(4,1)S(1)}, s32[]{:S(2)}) async-start(s8[4587520]{0:T(1024)(128)(4,1)} %bitcast.139), calls=%async_computation.5 | async-start | bytes 8388608
  678.2 10.5 %slice-start.8 = ((s8[4587520]{0:T(1024)(128)(4,1)}), s8[4194304]{0:T(1024)(128)(4,1)S(1)}, s32[]{:S(2)}) async-start(s8[4587520]{0:T(1024)(128)(4,1)} %bitcast.158), calls=%async_computation.13 | async-start | bytes 8388608
  681.6 7.1 %copy-start.6 = (bf16[640,1792]{1,0:T(8,128)(2,1)S(1)}, bf16[640,1792]{1,0:T(8,128)(2,1)}, u32[]{:S(2)}) copy-start(bf16[640,1792]{1,0:T(8,128)(2,1)} %get-tuple-element.48) | copy-start | bytes 6881284
  681.6 7.1 %slice-start.9 = ((s8[4587520]{0:T(1024)(128)(4,1)}), s8[393216]{0:T(1024)(128)(4,1)S(1)}, s32[]{:S(2)}) async-start(s8[4587520]{0:T(1024)(128)(4,1)} %bitcast.158), calls=%async_computation.14 | async-start | bytes 786432
  (50 other events, 180.4 us)
Sparse Core Ops, SparseCore 0:
  10.3 149.3 all-gather.2
  445.7 159.2 reduce-scatter.1

commit v5 on v4

--- a/solution.py
+++ b/solution.py
@@ -14,6 +14,7 @@
 FF = 896
 TOP = 6
 ADAM_STEP = 5
+MIXED_FIRST = 896
 GIVEN = 1280
 
 
@@ -50,34 +51,6 @@
     return (cosine, sine_table, allowed)
 
 
-def rotate(vectors, cosine, sine_table):
-    half_width = vectors.shape[-1] // 2
-    turned = jnp.concatenate([-vectors[..., half_width:], vectors[..., :half_width]], axis=-1)
-    return vectors * cosine[:, None, :] + turned * sine_table[:, None, :]
-
-
-def rotate_back(gradient, cosine, sine_table):
-    half_width = gradient.shape[-1] // 2
-    scaled_sine = gradient * sine_table[:, None, :]
-    turned = jnp.concatenate(
-        [scaled_sine[..., half_width:], -scaled_sine[..., :half_width]], axis=-1
-    )
-    return gradient * cosine[:, None, :] + turned
-
-
-def silu_slope(gate_vals):
-    logistic = jax.nn.sigmoid(gate_vals)
-    return logistic * (1.0 + gate_vals * (1.0 - logistic))
-
-
-def swiglu_back(act_grad, gate_up):
-    gate_part = gate_up[:, :FF]
-    up_part = gate_up[:, FF:]
-    return jnp.concatenate(
-        [act_grad * up_part * silu_slope(gate_part), act_grad * jax.nn.silu(gate_part)], axis=1
-    ).astype(jnp.bfloat16)
-
-
 def adam_update(weight, first_moment, second_moment, gradient, factor, step_rate, decay_rate):
     clipped = gradient * factor
     first_new = BETA_ONE * first_moment + (1.0 - BETA_ONE) * clipped
@@ -91,6 +64,11 @@
 
 
 MESH = pl.DeviceIdType.MESH
+
+
+PIECE = 64
+CHUNK = 64
+SHARE_BACK = 6
 
 
 class Place:
@@ -174,7 +152,7 @@
     return events
 
 
-def gather_body(place, orders, slices, own_ref, out_ref, block_of, send_sem, recv_sem):
+def gather_body(place, orders, slices, own_ref, out_ref, block_of, send_sem, recv_sem, fill=()):
     size = place.size
     sends = []
     count = [0]
@@ -198,7 +176,12 @@
         under(conds, lambda: copy().start())
         sends.append((conds, copy))
 
-    for _, part, offs in plan_gather(size, orders):
+    fill = list(fill)
+    plan = plan_gather(size, orders)
+    every = max(1, len(plan) // (len(fill) + 1))
+    for number, (_, part, offs) in enumerate(plan):
+        if fill and number % every == every - 1:
+            fill.pop(0)()
         order = orders[part]
         steps = dict(zip(order, offs))
         last = max([i for i, o in enumerate(offs) if o], default=-1)
@@ -229,6 +212,8 @@
             elif i > last:
                 for t in range(1, size[axis]):
                     send(conds, part, block, src, lambda axis=axis, t=t: place.moved(**{axis: t}))
+    for run in fill:
+        run()
     for conds, copy in sends:
         under(conds, lambda copy=copy: copy().wait_send())
 
@@ -252,17 +237,29 @@
     return {"A": na, "B": rest // na, "C": 2, "Y": n_dp}
 
 
-def gather_kernel(n_dp, n_exp, orders, slices, dense, x_ref, out_ref, send_sem, recv_sem, local_sem):
+def gather_kernel(n_dp, n_exp, orders, slices, dense, x_ref, pass_ref, out_ref, passed_ref, send_sem, recv_sem,
+                  local_sem, pass_send, pass_recv):
     place = Place(n_dp, n_exp)
+
+    def piece(n):
+        rows = pl.ds(n * PIECE, PIECE)
+        return pltpu.make_async_remote_copy(
+            src_ref=pass_ref.at[rows], dst_ref=passed_ref.at[rows], send_sem=pass_send.at[n], recv_sem=pass_recv.at[n],
+            device_id=place.device(place.moved(Y=1)), device_id_type=MESH)
+
+    pieces = pass_ref.shape[0] // PIECE if n_dp == 2 else 0
     block_of = place.flat if dense else place.expert
     place.greet(orders[0], False)
     own = pltpu.make_async_copy(x_ref, out_ref.at[block_of(place.pos)], local_sem)
     own.start()
-    gather_body(place, orders, slices, x_ref, out_ref, block_of, send_sem, recv_sem)
+    gather_body(place, orders, slices, x_ref, out_ref, block_of, send_sem, recv_sem,
+                [lambda n=n: piece(n).start() for n in range(pieces)])
     own.wait()
-
-
-def gather(x, n_dp, n_exp, dense, cid, parts=None):
+    for n in range(pieces):
+        piece(n).wait()
+
+
+def gather(x, passed, n_dp, n_exp, dense, cid, parts=None):
     size = sizes(n_dp, n_exp)
     rows, cols = x.shape
     if dense:
@@ -276,17 +273,20 @@
     blocks = n_exp * (n_dp if dense else 1)
     return pl.pallas_call(
         functools.partial(gather_kernel, n_dp, n_exp, orders, slices, dense),
-        out_shape=jax.ShapeDtypeStruct((blocks, rows, cols), x.dtype),
-        in_specs=[pl.BlockSpec(memory_space=pl.ANY)],
-        out_specs=pl.BlockSpec(memory_space=pl.ANY),
+        out_shape=[
+            jax.ShapeDtypeStruct((blocks, rows, cols), x.dtype), jax.ShapeDtypeStruct(passed.shape, passed.dtype)],
+        in_specs=[pl.BlockSpec(memory_space=pl.ANY)] * 2,
+        out_specs=[pl.BlockSpec(memory_space=pl.ANY)] * 2,
         scratch_shapes=[
             pltpu.SemaphoreType.DMA((count_gather(size, orders),)),
             pltpu.SemaphoreType.DMA((len(orders), blocks)),
             pltpu.SemaphoreType.DMA(()),
+            pltpu.SemaphoreType.DMA((max(1, passed.shape[0] // PIECE),)),
+            pltpu.SemaphoreType.DMA((max(1, passed.shape[0] // PIECE),)),
         ],
         compiler_params=pltpu.CompilerParams(collective_id=cid, has_side_effects=True),
         name="gather_dense" if dense else "gather_group",
-    )(x)
+    )(x, passed)
 
 
 def line_order(n):
@@ -448,10 +448,10 @@
         value_ref[...] = total
 
 
-def reduce_kernel(n_dp, n_exp, orders, slices, dense, arrays, sq_ref, *refs):
+def reduce_kernel(n_dp, n_exp, orders, slices, dense, arrays, *refs):
     g_refs, out_refs, scratch = refs[:arrays], refs[arrays:2 * arrays], refs[2 * arrays + 1:]
     norm_ref = refs[2 * arrays]
-    land, (send_sem, recv_sem, norm_land, norm_send, norm_recv) = scratch[:-5], scratch[-5:]
+    land, (send_sem, recv_sem) = scratch[:-2], scratch[-2:]
     place = Place(n_dp, n_exp)
     place.greet(orders[0], True)
     base = [0]
@@ -463,42 +463,37 @@
         out_refs[which][:, lo:lo + w] = total
 
     reduce_body(place, orders, slices, g_refs, place.flat if dense else place.expert, land, base, send_sem, recv_sem, finish)
-    total = sq_ref[...]
+    total = jnp.zeros((8, 128), jnp.float32)
     for out in out_refs:
         total = total + jnp.sum(out[...] * out[...])
     norm_ref[...] = total
-    norm_exchange(place, norm_ref, norm_land, norm_send, norm_recv)
-
-
-def reduce_dense(arrays, squares, n_dp, n_exp, cid):
+
+
+def reduce_dense(arrays, n_dp, n_exp, cid):
     size = sizes(n_dp, n_exp)
     blocks, rows = arrays[0].shape[:2]
     orders, slices = [], []
     for which, g in enumerate(arrays):
         cols = g.shape[2]
-        half = cols // 256 * 128
+        half = cols // 128 * SHARE_BACK // 16 * 128
         for order, lo, w in (("CBYA", 0, half), ("CYBA", half, cols - half)):
             if w:
                 orders.append(order)
                 slices.append((which, lo, w))
     slots = [len(stage_slots(size, order)) for order in orders]
-    top = max(size.values())
     return pl.pallas_call(
         functools.partial(reduce_kernel, n_dp, n_exp, orders, slices, True, len(arrays)),
         out_shape=[jax.ShapeDtypeStruct((rows, g.shape[2]), jnp.float32) for g in arrays] + [
             jax.ShapeDtypeStruct((8, 128), jnp.float32)],
-        in_specs=[pl.BlockSpec(memory_space=pltpu.VMEM)] * (len(arrays) + 1),
+        in_specs=[pl.BlockSpec(memory_space=pltpu.VMEM)] * len(arrays),
         out_specs=[pl.BlockSpec(memory_space=pltpu.VMEM)] * (len(arrays) + 1),
         scratch_shapes=[pltpu.VMEM((k, rows, s[2]), g.dtype) for k, s in zip(slots, slices)] + [
             pltpu.SemaphoreType.DMA((count_reduce(size, orders),)),
             pltpu.SemaphoreType.DMA((sum(slots),)),
-            pltpu.VMEM((4, top, 8, 128), jnp.float32),
-            pltpu.SemaphoreType.DMA((4, top)),
-            pltpu.SemaphoreType.DMA((4, top)),
         ],
         compiler_params=pltpu.CompilerParams(collective_id=cid, has_side_effects=True, vmem_limit_bytes=60 * 1024 * 1024),
         name="reduce_dense",
-    )(jnp.full((8, 128), squares, jnp.float32), *arrays)
+    )(*arrays)
 
 
 def mm(a, b):
@@ -545,18 +540,18 @@
 
 def fused_kernel(n_dp, n_exp, experts, cap, halves, x_ref, cot_ref, rank_own, *refs):
     win_h, wdown_h, refs = refs[:halves], refs[halves:2 * halves], refs[2 * halves:]
-    wrt_h, wshin_h, wshdown_h, xall, mixed, total_out, gg_out, refs = *refs[:7], refs[7:]
+    wrt_h, wshin_h, wshdown_h, xall, mixed_a, mixed_b, total_out, gg_out, refs = *refs[:8], refs[8:]
     gin_out, gdown_out, refs = refs[:halves], refs[halves:2 * halves], refs[2 * halves:]
     fused_body(n_dp, n_exp, experts, cap, x_ref, cot_ref, rank_own, win_h, wdown_h, wrt_h, wshin_h, wshdown_h,
-               xall, mixed, total_out, gg_out, gin_out, gdown_out, *refs)
+               xall, mixed_a, mixed_b, total_out, gg_out, gin_out, gdown_out, *refs)
 
 
 def fused_body(n_dp, n_exp, experts, cap, x_ref, cot_ref, rank_own, win_h, wdown_h, wrt_h, wshin_h, wshdown_h,
-                 xall, mixed, total_out, gg_out, gin_out, gdown_out, gshin, gshdown, core_land, b_land, a_land,
+                 xall, mixed_a, mixed_b, total_out, gg_out, gin_out, gdown_out, gshin, gshdown, core_land, b_land, a_land,
                  win, wdown, wrt, wshin, wshdown, rank_ref, xv, cv, xr_s, act_s, gr_s, dgu_s, back_s, mixed_s, held, bsrc, stage,
                  gg_s, gin_acc, gdown_acc,
                  w_sem, x_sem, c_sem, m_sem, s_sem, ag_send, ag_recv, core_send, core_recv, b_send, b_recv,
-                 a_send, a_recv, g_send, g_recv, r_send, r_recv):
+                 a_send, a_recv, g_send, g_recv, r_send, r_recv, y_send, y_recv):
     low, wide = jnp.bfloat16, jnp.float32
     place = Place(n_dp, n_exp)
     na, nb = place.size["A"], place.size["B"]
@@ -578,7 +573,9 @@
     barrier = pltpu.get_barrier_semaphore()
     for s in range(1, n_exp):
         pl.semaphore_signal(barrier, inc=1, device_id=(pos["Y"], lax.rem(me + s, n_exp)), device_id_type=MESH)
-    pl.semaphore_wait(barrier, n_exp - 1)
+    if len(win_h) == 2:
+        pl.semaphore_signal(barrier, inc=1, device_id=place.device(place.moved(Y=1)), device_id_type=MESH)
+    pl.semaphore_wait(barrier, n_exp - 1 + (len(win_h) == 2))
 
     def rank_copy(s):
         j = lax.rem(me + s, n_exp)
@@ -784,8 +781,12 @@
             src_ref=gg_s.at[k, n], dst_ref=gg_out.at[me], send_sem=g_send.at[k, n], recv_sem=g_recv.at[me],
             device_id=(pos["Y"], to), device_id_type=MESH)
 
-    def mixed_copy(slot, n, j):
-        return pltpu.make_async_copy(mixed_s.at[slot, n], mixed.at[j], m_sem.at[slot, n])
+    cut = mixed_a.shape[2]
+
+    def mixed_copies(slot, n, j):
+        return [
+            pltpu.make_async_copy(mixed_s.at[slot, n, :, pl.ds(0, cut)], mixed_a.at[j], m_sem.at[slot, n, 0]),
+            pltpu.make_async_copy(mixed_s.at[slot, n, :, pl.ds(cut, d - cut)], mixed_b.at[j], m_sem.at[slot, n, 1])]
 
     def step(k, carry):
         slot = lax.rem(k, 2)
@@ -856,7 +857,8 @@
         @pl.when(k >= 2)
         def _():
             for n, j in enumerate((one, two)):
-                mixed_copy(slot, n, j).wait()
+                for copy in mixed_copies(slot, n, j):
+                    copy.wait()
 
         for n in range(2):
             x = xv[n]
@@ -877,7 +879,8 @@
             gshdown[...] += mm_tn(sact, ct)
             gshin[...] += mm_tn(x, dsh)
         for n, j in enumerate((one, two)):
-            mixed_copy(slot, n, j).start()
+            for copy in mixed_copies(slot, n, j):
+                copy.start()
         at(k, {q: [lambda q=q: core_copy(q).start()] for q in range(steps)})
 
         @pl.when(k > 0)
@@ -906,17 +909,20 @@
 
     lax.fori_loop(0, steps, step, 0)
     gg_out[me] = gg_s[0, 0]
-    win[...] = gin_acc[...].astype(low)
-    wdown[...] = gdown_acc[...].astype(low)
     outs = []
-    for pieces, whole in ((gin_out, win), (gdown_out, wdown)):
+    for pieces, whole, acc in ((gin_out, win, gin_acc), (gdown_out, wdown, gdown_acc)):
+        whole[...] = acc[...].astype(low)
         for n, piece in enumerate(pieces):
             rows = piece.shape[0]
             start = lax.rem(pos["Y"] + n, len(pieces)) * rows
-            outs.append(pltpu.make_async_copy(
-                whole.at[pl.ds(pl.multiple_of(start, 16), rows)], piece, w_sem.at[len(outs)]))
-    for out in outs:
-        out.start()
+            part = whole.at[pl.ds(pl.multiple_of(start, 16), rows)]
+            if n and whole is win:
+                outs.append(pltpu.make_async_remote_copy(
+                    src_ref=part, dst_ref=piece, send_sem=y_send, recv_sem=y_recv,
+                    device_id=place.device(place.moved(Y=1)), device_id_type=MESH))
+            else:
+                outs.append(pltpu.make_async_copy(part, piece, w_sem.at[len(outs)]))
+            outs[-1].start()
     for run in late:
         run()
     total = held[0].astype(wide)
@@ -940,7 +946,8 @@
     for k in (steps - 2, steps - 1):
         one, two = pair_index(k)
         for n, j in enumerate((one, two)):
-            mixed_copy(k % 2, n, j).wait()
+            for copy in mixed_copies(k % 2, n, j):
+                copy.wait()
 
     def gg_done(k, carry):
         one, two = pair_index(k)
@@ -987,7 +994,8 @@
         in_specs=[hbm, hbm, vmem] + [hbm] * (2 * len(win) + 3),
         out_shape=[
             jax.ShapeDtypeStruct((n_exp,) + x.shape, low),
-            jax.ShapeDtypeStruct((n_exp,) + block, low),
+            jax.ShapeDtypeStruct((n_exp, toks, MIXED_FIRST), low),
+            jax.ShapeDtypeStruct((n_exp, toks, d - MIXED_FIRST), low),
             jax.ShapeDtypeStruct(block, wide),
             jax.ShapeDtypeStruct((n_exp, 1, toks), wide),
             *[jax.ShapeDtypeStruct(w.shape, low) for w in (*win, *wdown)],
@@ -997,7 +1005,7 @@
             jax.ShapeDtypeStruct((na * max(nb - 1, 1),) + block, low),
             jax.ShapeDtypeStruct((na,) + block, low),
         ],
-        out_specs=[hbm, hbm, hbm, vmem] + [hbm] * (2 * len(win)) + [vmem, vmem, hbm, hbm, hbm],
+        out_specs=[hbm, hbm, hbm, hbm, vmem] + [hbm] * (2 * len(win)) + [vmem, vmem, hbm, hbm, hbm],
         scratch_shapes=[
             pltpu.VMEM((d, 2 * FF), low), pltpu.VMEM((FF, d), low), pltpu.VMEM(wrt.shape, low),
             pltpu.VMEM(wshin.shape, low), pltpu.VMEM(wshdown.shape, low), pltpu.VMEM((n_exp, 1, toks), wide),
@@ -1007,17 +1015,308 @@
             pltpu.VMEM((2, 2) + block, low), pltpu.VMEM((2, 2) + block, low), pltpu.VMEM((na,) + block, low),
             pltpu.VMEM((2,) + block, low), pltpu.VMEM((nb,) + block, low),
             pltpu.VMEM((steps, 2, 1, toks), wide), pltpu.VMEM((d, 2 * FF), wide), pltpu.VMEM((FF, d), wide),
-            dma((3 + 2 * len(win),)), dma((2, 2)), dma((2, 2)), dma((2, 2)), dma((nb,)),
+            dma((3 + 2 * len(win),)), dma((2, 2)), dma((2, 2)), dma((2, 2, 2)), dma((nb,)),
             dma((ag_count,)), dma((n_exp,)), dma((steps,)), dma((steps,)),
             dma((na * max(nb - 1, 1),)), dma((na * max(nb - 1, 1),)), dma((na,)), dma((na,)),
-            dma((steps, 2)), dma((n_exp,)), dma((n_exp,)), dma((n_exp,)),
+            dma((steps, 2)), dma((n_exp,)), dma((n_exp,)), dma((n_exp,)), dma(()), dma(()),
         ],
         compiler_params=pltpu.CompilerParams(collective_id=cid, has_side_effects=True, vmem_limit_bytes=63 * 1024 * 1024),
         cost_estimate=pl.CostEstimate(flops=flops, bytes_accessed=100 * 1024 * 1024, transcendentals=0),
         name="experts_fused",
     )(x, cot_all, rank, *win, *wdown, wrt, wshin, wshdown)
     n = len(win)
-    return out[1], out[2], out[3], out[4:4 + n], out[4 + n:4 + 2 * n], out[4 + 2 * n], out[5 + 2 * n]
+    return out[1], out[2], out[3], out[4], out[5:5 + n], out[5 + n:5 + 2 * n], out[5 + 2 * n], out[6 + 2 * n]
+
+
+def attend_kernel(heads_n, experts, tok_ref, gains_ref, full_ref, router_ref, cos_ref, sin_ref, bias_ref,
+                  q_ref, k_ref, v_ref, heads_ref, resid_ref, mlp_ref, probs_ref, attn_ref):
+    low, wide = jnp.bfloat16, jnp.float32
+    width = heads_n * HD
+    d = mlp_ref.shape[1]
+    scale = HD ** (-0.5)
+    inputs = tok_ref[...].astype(wide)
+    attn_ref[...] = (inputs * rms_scale(inputs) * gains_ref[0:1, :]).astype(low)
+    lane = lax.broadcasted_iota(jnp.int32, (1, HD), 1)
+    sign = jnp.where(lane < HD // 2, -1.0, 1.0)
+
+    def turn(g):
+        return g * cos_ref[...] + pltpu.roll(g, HD // 2, 1) * sign * sin_ref[...]
+
+    pair = 2 * HD
+
+    def project(j, carry):
+        for part, out in ((0, q_ref), (1, k_ref), (2, v_ref)):
+            y = mm(attn_ref[...], full_ref[:, pl.ds(pl.multiple_of(part * width + j * pair, HD), pair)])
+            for n in range(2):
+                one = y[:, n * HD : (n + 1) * HD]
+                at = pl.ds(pl.multiple_of(j * pair + n * HD, HD), HD)
+                out[:, at] = (turn(one) if part < 2 else one).astype(low)
+        return carry
+
+    lax.fori_loop(0, heads_n // 2, project, 0)
+
+    def head(h, carry):
+        at = pl.ds(pl.multiple_of(h * HD, HD), HD)
+        s = jnp.where(bias_ref[...] > 0.0, mm_nt(q_ref[:, at], k_ref[:, at]) * scale, NEGATIVE)
+        e = jnp.exp(s - jnp.max(s, axis=-1, keepdims=True))
+        p = e / jnp.sum(e, axis=-1, keepdims=True)
+        heads_ref[:, at] = mm(p.astype(low), v_ref[:, at]).astype(low)
+        return carry
+
+    lax.fori_loop(0, heads_n, head, 0)
+    residual = inputs + mm(heads_ref[...], full_ref[:, 3 * width : 3 * width + d])
+    resid_ref[...] = residual
+    mlp_ref[...] = (residual * rms_scale(residual) * gains_ref[1:2, :]).astype(low)
+    logits = mm_nt(router_ref[...], mlp_ref[...])
+    e = jnp.exp(logits - jnp.max(logits, axis=0, keepdims=True))
+    probs_ref[...] = e / jnp.sum(e, axis=0, keepdims=True)
+
+
+def attend(experts, tokens, *args):
+    toks, d = tokens.shape
+    low, wide = jnp.bfloat16, jnp.float32
+    width = H * HD
+    shape = jax.ShapeDtypeStruct
+    vmem = pl.BlockSpec(memory_space=pltpu.VMEM)
+    return pl.pallas_call(
+        functools.partial(attend_kernel, H, experts),
+        in_specs=[vmem] * (len(args) + 1),
+        out_specs=[vmem] * 8,
+        out_shape=[shape((toks, width), low)] * 4 + [
+            shape((toks, d), wide), shape((toks, d), low), shape((experts, toks), wide), shape((toks, d), low)],
+        compiler_params=pltpu.CompilerParams(vmem_limit_bytes=60 * 1024 * 1024),
+        cost_estimate=pl.CostEstimate(flops=7 * 10**9, bytes_accessed=24 * 1024 * 1024, transcendentals=0),
+        name="attend",
+    )(tokens, *args)
+
+
+def attend_back_kernel(
+    heads_n, experts, back_ref, gg_ref, probs_ref, router_ref, mlp_ref, resid_ref, cot_ref, tok_ref, gains_ref, full_ref,
+    heads_ref, q_ref, k_ref, v_ref, attn_ref, cos_ref, sin_ref, bias_ref,
+    gqkv_ref, gout_ref, gin_ref, small_ref, pg_ref, hg_ref, rl_ref
+):
+    low, wide = jnp.bfloat16, jnp.float32
+    width = heads_n * HD
+    d = mlp_ref.shape[1]
+    scale = HD ** (-0.5)
+    gg = gg_ref[...]
+    rp = probs_ref[...]
+    logit = (rp * (gg - jnp.sum(gg * rp, axis=0, keepdims=True))).astype(low)
+    residual = resid_ref[...]
+    r2 = rms_scale(residual)
+    n2 = residual * r2
+    mg = back_ref[...] + mm_tn(logit, router_ref[...])
+    small_ref[...] = jnp.zeros_like(small_ref)
+    small_ref[0:experts, :] = mm(logit, mlp_ref[...])
+    small_ref[experts + 8 : experts + 9, :] = jnp.sum(mg * n2, axis=0, keepdims=True)
+    u = mg * gains_ref[1:2, :]
+    resid_grad = cot_ref[...].astype(wide) + r2 * (u - n2 * jnp.mean(u * n2, axis=-1, keepdims=True))
+    gin_ref[...] = resid_grad
+    rl_ref[...] = resid_grad.astype(low)
+    gout_ref[...] = mm_tn(heads_ref[...], rl_ref[...]).astype(low)
+    hg_ref[...] = mm_nt(rl_ref[...], full_ref[:, 3 * width : 3 * width + d]).astype(low)
+    lane = lax.broadcasted_iota(jnp.int32, (1, HD), 1)
+    sign = jnp.where(lane < HD // 2, 1.0, -1.0)
+
+    def turn_back(g):
+        return g * cos_ref[...] + pltpu.roll(g * sin_ref[...], HD // 2, 1) * sign
+
+    def head(h, carry):
+        at = pl.ds(pl.multiple_of(h * HD, HD), HD)
+        q, k, v, hg = q_ref[:, at], k_ref[:, at], v_ref[:, at], hg_ref[:, at]
+        s = jnp.where(bias_ref[...] > 0.0, mm_nt(q, k) * scale, NEGATIVE)
+        e = jnp.exp(s - jnp.max(s, axis=-1, keepdims=True))
+        p = e / jnp.sum(e, axis=-1, keepdims=True)
+        dp = mm_nt(hg, v)
+        sg = (p * (dp - jnp.sum(dp * p, axis=-1, keepdims=True))).astype(low)
+        pg_ref[:, at] = turn_back(mm(sg, k) * scale).astype(low)
+        pg_ref[:, pl.ds(pl.multiple_of(width + h * HD, HD), HD)] = turn_back(mm_tn(sg, q) * scale).astype(low)
+        pg_ref[:, pl.ds(pl.multiple_of(2 * width + h * HD, HD), HD)] = mm_tn(p.astype(low), hg).astype(low)
+        return carry
+
+    lax.fori_loop(0, heads_n, head, 0)
+    wide_cols = 640
+
+    def columns(j, carry):
+        at = pl.ds(pl.multiple_of(j * wide_cols, 128), wide_cols)
+        gqkv_ref[:, at] = mm_tn(attn_ref[...], pg_ref[:, at]).astype(low)
+        return carry
+
+    lax.fori_loop(0, 3 * width // wide_cols, columns, 0)
+    ag = mm_nt(pg_ref[...], full_ref[:, : 3 * width])
+    inputs = tok_ref[...].astype(wide)
+    r1 = rms_scale(inputs)
+    n1 = inputs * r1
+    small_ref[experts : experts + 1, :] = jnp.sum(ag * n1, axis=0, keepdims=True)
+    u1 = ag * gains_ref[0:1, :]
+    gin_ref[...] += r1 * (u1 - n1 * jnp.mean(u1 * n1, axis=-1, keepdims=True))
+
+
+def attend_back(experts, *args):
+    toks, d = args[4].shape
+    low, wide = jnp.bfloat16, jnp.float32
+    width = H * HD
+    return pl.pallas_call(
+        functools.partial(attend_back_kernel, H, experts),
+        in_specs=[pl.BlockSpec(memory_space=pltpu.VMEM)] * len(args),
+        out_specs=[pl.BlockSpec(memory_space=pltpu.VMEM)] * 4,
+        out_shape=[
+            jax.ShapeDtypeStruct((d, 3 * width), low),
+            jax.ShapeDtypeStruct((width, d), low),
+            jax.ShapeDtypeStruct((toks, d), wide),
+            jax.ShapeDtypeStruct((experts + 16, d), wide),
+        ],
+        scratch_shapes=[pltpu.VMEM((toks, 3 * width), low), pltpu.VMEM((toks, width), low), pltpu.VMEM((toks, d), low)],
+        compiler_params=pltpu.CompilerParams(vmem_limit_bytes=62 * 1024 * 1024),
+        cost_estimate=pl.CostEstimate(flops=14 * 10**9, bytes_accessed=45 * 1024 * 1024, transcendentals=0),
+        name="attend_back",
+    )(*args)
+
+
+def norm_kernel(n_dp, n_exp, counts, sq_ref, *refs):
+    groups, refs = refs[: sum(counts)], refs[sum(counts) :]
+    norm_ref, land, send_sem, recv_sem = refs
+    place = Place(n_dp, n_exp)
+    place.greet("CBYA", True)
+    total = sq_ref[...]
+    at = 0
+    for count in counts:
+        pieces = groups[at : at + count]
+        at += count
+        rows, cols = pieces[0].shape
+        step = 32 if rows % 32 == 0 else rows
+
+        def add(i, acc, pieces=pieces, step=step):
+            part = pl.ds(pl.multiple_of(i * step, step), step)
+            g = pieces[0][part, :].astype(jnp.float32)
+            for piece in pieces[1:]:
+                g = g + piece[part, :].astype(jnp.float32)
+            return acc + jnp.sum(g * g, axis=0, keepdims=True)
+
+        sums = lax.fori_loop(0, rows // step, add, jnp.zeros((1, cols), jnp.float32))
+        total = total + jnp.sum(sums)
+    norm_ref[...] = total
+    norm_exchange(place, norm_ref, land, send_sem, recv_sem)
+
+
+def sum_squares(groups, dense_squares, n_dp, n_exp, cid):
+    top = max(sizes(n_dp, n_exp).values())
+    flat = [g for group in groups for g in group]
+    vmem = pl.BlockSpec(memory_space=pltpu.VMEM)
+    return pl.pallas_call(
+        functools.partial(norm_kernel, n_dp, n_exp, [len(group) for group in groups]),
+        out_shape=jax.ShapeDtypeStruct((8, 128), jnp.float32),
+        in_specs=[vmem] * (1 + len(flat)),
+        out_specs=vmem,
+        scratch_shapes=[
+            pltpu.VMEM((4, top, 8, 128), jnp.float32),
+            pltpu.SemaphoreType.DMA((4, top)),
+            pltpu.SemaphoreType.DMA((4, top)),
+        ],
+        compiler_params=pltpu.CompilerParams(collective_id=cid, has_side_effects=True, vmem_limit_bytes=40 * 1024 * 1024),
+        name="sum_squares",
+    )(dense_squares, *flat)
+
+
+def adam_kernel(rates, decays, big, counts, norm_ref, *refs):
+    n = len(rates)
+    states, grads, at = [], [], 0
+    for i in range(n):
+        states.append(refs[at : at + 3])
+        at += 3
+    for i in range(n):
+        grads.append(refs[at : at + counts[i]])
+        at += counts[i]
+    outs = [refs[at + 3 * i : at + 3 * i + 3] for i in range(n)]
+    at += 3 * n
+    held = []
+    for i in range(big):
+        held.append((refs[at : at + 3], refs[at + 3 : at + 3 + counts[i]], refs[at + 3 + counts[i]], refs[at + 4 + counts[i]]))
+        at += 5 + counts[i]
+
+    def copies(i, j):
+        state_v, grad_v, in_sem, out_sem = held[i]
+        step = CHUNK if state_v[0].shape[0] % CHUNK == 0 else CHUNK // 2
+        part = pl.ds(pl.multiple_of(j * step, step), step)
+        pairs = list(zip(states[i] + grads[i], state_v + grad_v))
+        ins = [pltpu.make_async_copy(a.at[part], b.at[part], in_sem.at[j, q]) for q, (a, b) in enumerate(pairs)]
+        back = [pltpu.make_async_copy(a.at[part], b.at[part], out_sem.at[j, q]) for q, (a, b) in enumerate(zip(state_v, outs[i]))]
+        return part, ins, back
+
+    def chunks(i):
+        rows = held[i][0][0].shape[0]
+        return rows // (CHUNK if rows % CHUNK == 0 else CHUNK // 2)
+
+    for i in range(big):
+
+        def load(j, carry, i=i):
+            for copy in copies(i, j)[1]:
+                copy.start()
+            return carry
+
+        lax.fori_loop(0, chunks(i), load, 0)
+    factor = jnp.minimum(1.0, CLIP / jnp.sqrt(norm_ref[0:1, 0:1]))
+
+    def total(pieces, part):
+        g = pieces[0][part].astype(jnp.float32)
+        for piece in pieces[1:]:
+            g = g + piece[part].astype(jnp.float32)
+        return g
+
+    for i in range(big, n):
+        w, m, v = states[i]
+        new = adam_update(w[...], m[...], v[...], total(grads[i], Ellipsis), factor, rates[i], decays[i])
+        for out, value in zip(outs[i], new):
+            out[...] = value
+    for i in range(big):
+
+        def work(j, carry, i=i):
+            part, ins, back = copies(i, j)
+            for copy in ins:
+                copy.wait()
+            state_v, grad_v = held[i][0], held[i][1]
+            new = adam_update(
+                state_v[0][part, :], state_v[1][part, :], state_v[2][part, :], total(grad_v, part), factor, rates[i], decays[i]
+            )
+            for ref, value in zip(state_v, new):
+                ref[part, :] = value
+            for copy in back:
+                copy.start()
+            return carry
+
+        lax.fori_loop(0, chunks(i), work, 0)
+    for i in range(big):
+
+        def finish(j, carry, i=i):
+            for copy in copies(i, j)[2]:
+                copy.wait()
+            return carry
+
+        lax.fori_loop(0, chunks(i), finish, 0)
+
+
+def adam(norm, states, grads, rates, decays, big):
+    hbm = pl.BlockSpec(memory_space=pl.ANY)
+    vmem = pl.BlockSpec(memory_space=pltpu.VMEM)
+    counts = [len(g) for g in grads]
+    flat = [a for s in states for a in s] + [a for g in grads for a in g]
+    specs = [hbm if i < big else vmem for i in range(len(states)) for _ in range(3)]
+    scratch = []
+    for i in range(big):
+        rows = states[i][0].shape[0]
+        pieces = rows // (CHUNK if rows % CHUNK == 0 else CHUNK // 2)
+        scratch += [pltpu.VMEM(a.shape, a.dtype) for a in (*states[i], *grads[i])]
+        scratch += [pltpu.SemaphoreType.DMA((pieces, 3 + counts[i])), pltpu.SemaphoreType.DMA((pieces, 3))]
+    out = pl.pallas_call(
+        functools.partial(adam_kernel, rates, decays, big, counts),
+        in_specs=[vmem] + specs + [hbm if i < big else vmem for i in range(len(grads)) for _ in range(counts[i])],
+        out_specs=specs,
+        out_shape=[jax.ShapeDtypeStruct(a.shape, a.dtype) for s in states for a in s],
+        scratch_shapes=scratch,
+        compiler_params=pltpu.CompilerParams(vmem_limit_bytes=60 * 1024 * 1024),
+        name="adam",
+    )(norm, *flat)
+    return [tuple(out[3 * i : 3 * i + 3]) for i in range(len(states))]
 
 
 def swap_rows(x, n_dp):
@@ -1032,13 +1331,6 @@
     first = lax.axis_index("dp") == 0
     x, other = pieces
     return jnp.concatenate([jnp.where(first, x, other), jnp.where(first, other, x)], axis=0)
-
-
-def halve_rows(pieces, n_dp):
-    if n_dp != 2:
-        return lax.psum_scatter(pieces[0], "dp", scatter_dimension=0, tiled=True).astype(jnp.float32)
-    other = lax.ppermute(pieces[1], "dp", [(0, 1), (1, 0)])
-    return pieces[0].astype(jnp.float32) + other.astype(jnp.float32)
 
 
 def split_rows(x, n_dp):
@@ -1089,23 +1381,22 @@
     n_exp = lax.axis_size("expert")
     n_all = n_dp * n_exp
     capacity = min(row_count, (5 * row_count * TOP // (4 * expert_count) + 7) // 8 * 8)
-    score_scale = HD ** (-0.5)
     rows_w = w_qkv.shape[0]
     unit = w_shared_down.shape[0]
 
     pad = jnp.zeros((rows_w, 128 - expert_count - 2), wide)
     packed = jnp.concatenate([w_qkv, w_out, w_router, norm_gains.T, pad], axis=1).astype(low)
-    full = gather(packed, n_dp, n_exp, True, 1).reshape(D, -1)
+    edown_low = w_expert_down[0].astype(low)
+    full, edown_other = gather(packed, edown_low, n_dp, n_exp, True, 1)
+    full = full.reshape(D, -1)
+    expert_down_full = [edown_low, edown_other] if n_dp == 2 else swap_rows(edown_low, n_dp)
     full, ein_low = lax.optimization_barrier((full, w_expert_in[0].astype(low)))
     expert_in_full = swap_rows(ein_low, n_dp)
-    qkv_full = full[:, : 3 * H * HD]
-    out_full = full[:, 3 * H * HD : 3 * H * HD + D]
     small_full = full[:, 3 * H * HD + D :]
     router_full = small_full[:, :expert_count]
     gain_one = small_full[:, expert_count].astype(wide)
     gain_two = small_full[:, expert_count + 1].astype(wide)
     cot_all = lax.all_gather(cotangent[:, :GIVEN], "expert", axis=0, tiled=False)
-    expert_down_full = swap_rows(w_expert_down[0].astype(low), n_dp)
     shin_send = (
         w_shared_in.astype(low)
         .reshape(rows_w, 2, n_dp, n_exp, unit)
@@ -1117,33 +1408,13 @@
     shdown_mine = in_order(swap_rows(w_shared_down.astype(low), n_dp))
     half = n_dp * unit
 
-    inputs = tokens.astype(wide)
+    gain_rows = jnp.stack([gain_one, gain_two])
+    router_rows = router_full.T
     cosine, sine_table, allowed = rotary_tables(lengths[0], row_count, HD)
-    scale_one = rms_scale(inputs)
-    normed_one = inputs * scale_one
-    attn_in = (normed_one * gain_one).astype(low)
-    projected = jnp.dot(attn_in, qkv_full, preferred_element_type=wide).reshape(
-        row_count, 3, H, HD
-    )
-    queries = rotate(projected[:, 0], cosine, sine_table).astype(low)
-    keys_rot = rotate(projected[:, 1], cosine, sine_table).astype(low)
-    values_low = projected[:, 2].astype(low)
-    raw_scores = (
-        jnp.einsum("qhd,khd->hqk", queries, keys_rot, preferred_element_type=wide) * score_scale
-    )
-    scores = jnp.where(allowed[None], raw_scores, NEGATIVE)
-    row_max = jnp.max(scores, axis=-1, keepdims=True)
-    exped = jnp.exp(scores - row_max)
-    probs_attn = exped / jnp.sum(exped, axis=-1, keepdims=True)
-    probs_low = probs_attn.astype(low)
-    mixed_heads = jnp.einsum("hqk,khd->qhd", probs_low, values_low, preferred_element_type=wide)
-    heads_low = mixed_heads.astype(low).reshape(row_count, H * HD)
-    residual = inputs + jnp.dot(heads_low, out_full, preferred_element_type=wide)
-    scale_two = rms_scale(residual)
-    normed_two = residual * scale_two
-    mlp_in = (normed_two * gain_two).astype(low)
-    logits = jnp.dot(mlp_in, router_full, preferred_element_type=wide)
-    router_probs = jax.nn.softmax(logits, axis=-1)
+    allowed = allowed.astype(wide)
+    queries, keys_rot, values_low, heads_low, residual, mlp_in, probs_rows, attn_in = attend(
+        expert_count, tokens, gain_rows, full, router_rows, cosine, sine_table, allowed
+    )
 
     routed = jnp.any(routes[:, :, None] == jnp.arange(expert_count, dtype=jnp.int32), axis=1)
     rank = jnp.where(routed, jnp.cumsum(routed.astype(jnp.int32), axis=0) - 1, -1).astype(wide).T
@@ -1153,92 +1424,63 @@
     gap = jnp.zeros((D, hid - half), low)
     wshin = jnp.concatenate([shin_mine[:, :half], gap, shin_mine[:, half:], gap], axis=1)
     wshdown = jnp.concatenate([shdown_mine, jnp.zeros((hid - half, D), low)], axis=0)
-    mixed_part, back_sum, gate_grad, grad_ein, grad_edown, shin_wide, shdown_wide = fused(
+    mixed_a, mixed_b, back_sum, gate_grad, grad_ein, grad_edown, shin_wide, shdown_wide = fused(
         jnp.concatenate([mlp_in, cotangent[:, GIVEN:]], axis=1), cot_all, rank[:, None, :], expert_in_full, expert_down_full, wrt, wshin, wshdown, n_dp, n_exp, expert_count, cap, 2
     )
-    mixed_sum = lax.psum_scatter(mixed_part, "expert", scatter_dimension=0, tiled=False)
+    mixed_a = lax.psum_scatter(mixed_a, "expert", scatter_dimension=0, tiled=False)
     grad_shin = jnp.concatenate([shin_wide[:, :half], shin_wide[:, hid : hid + half]], axis=1)
     grad_shdown = shdown_wide[:half]
-    prob_grad = gate_grad[:, 0, :].T
-    logit_grad = (
-        router_probs * (prob_grad - jnp.sum(prob_grad * router_probs, axis=-1, keepdims=True))
-    ).astype(low)
-    grad_router = jnp.einsum("td,te->de", mlp_in, logit_grad, preferred_element_type=wide)
-    mlp_in_grad = back_sum + jnp.einsum(
-        "te,de->td", logit_grad, router_full, preferred_element_type=wide
-    )
-    out_grad = cotangent.astype(wide)
-    grad_gain_two = jnp.sum(mlp_in_grad * normed_two, axis=0)
-    scaled_two = mlp_in_grad * gain_two
-    resid_grad = out_grad + scale_two * (
-        scaled_two - normed_two * jnp.mean(scaled_two * normed_two, axis=-1, keepdims=True)
-    )
-    resid_low = resid_grad.astype(low)
-    grad_out = jnp.einsum("ti,td->id", heads_low, resid_low, preferred_element_type=wide)
-    heads_grad = jnp.einsum("td,id->ti", resid_low, out_full, preferred_element_type=wide)
-    heads_grad = heads_grad.astype(low).reshape(row_count, H, HD)
-    attn_prob_grad = jnp.einsum("qhd,khd->hqk", heads_grad, values_low, preferred_element_type=wide)
-    value_grad = jnp.einsum("hqk,qhd->khd", probs_low, heads_grad, preferred_element_type=wide)
-    score_grad = probs_attn * (
-        attn_prob_grad - jnp.sum(attn_prob_grad * probs_attn, axis=-1, keepdims=True)
-    )
-    score_grad = score_grad.astype(low)
-    query_grad = (
-        jnp.einsum("hqk,khd->qhd", score_grad, keys_rot, preferred_element_type=wide) * score_scale
-    )
-    key_grad = (
-        jnp.einsum("hqk,qhd->khd", score_grad, queries, preferred_element_type=wide) * score_scale
-    )
-    projected_grad = jnp.stack(
-        [
-            rotate_back(query_grad, cosine, sine_table),
-            rotate_back(key_grad, cosine, sine_table),
-            value_grad,
-        ],
-        axis=1,
-    )
-    projected_grad = projected_grad.reshape(row_count, 3 * H * HD).astype(low)
-    grad_qkv = jnp.einsum("td,tk->dk", attn_in, projected_grad, preferred_element_type=wide)
-    attn_grad = jnp.einsum("tk,dk->td", projected_grad, qkv_full, preferred_element_type=wide)
-    grad_gain_one = jnp.sum(attn_grad * normed_one, axis=0)
-    scaled_one = attn_grad * gain_one
-    input_grad = resid_grad + scale_one * (
-        scaled_one - normed_one * jnp.mean(scaled_one * normed_one, axis=-1, keepdims=True)
-    )
-
-    small_grad = jnp.concatenate(
-        [grad_router, grad_gain_one[:, None], grad_gain_two[:, None], jnp.zeros((D, 128 - expert_count - 2), wide)],
-        axis=1,
-    )
+    grad_qkv, grad_out, input_grad, small_rows = attend_back(
+        expert_count,
+        back_sum,
+        gate_grad[:, 0, :],
+        probs_rows,
+        router_rows,
+        mlp_in,
+        residual,
+        cotangent,
+        tokens,
+        gain_rows,
+        full,
+        heads_low,
+        queries,
+        keys_rot,
+        values_low,
+        attn_in,
+        cosine,
+        sine_table,
+        allowed,
+    )
+
     shin_back = lax.all_to_all(
         grad_shin.astype(low).reshape(n_all, rows_w, 2 * half), both, 0, 0, tiled=True
     )
+    shdown_halves = split_rows(grad_shdown, n_dp)
+    if n_dp == 2:
+        swap = [(0, 1), (1, 0)]
+        came = (lax.ppermute(shdown_halves[1], "dp", swap), lax.ppermute(grad_edown[1], "dp", swap))
+        grad_qkv, shin_back, came = lax.optimization_barrier((grad_qkv, shin_back, came))
+        shdown_own = [shdown_halves[0], came[0]]
+        edown_own = [grad_edown[0], came[1]]
+        ein_own = list(grad_ein)
+    else:
+        shdown_own, edown_own, ein_own = (
+            [lax.psum_scatter(g[0], "dp", scatter_dimension=0, tiled=True)] for g in (shdown_halves, grad_edown, grad_ein)
+        )
+    small_grad = jnp.concatenate(
+        [small_rows.astype(low).T, jnp.zeros((D, 128 - expert_count - 16), low)], axis=1
+    )
     shin_own = jnp.sum(
         shin_back.reshape(n_dp, n_exp, rows_w, 2, n_dp, unit).astype(wide), axis=0
     )
     shin_own = shin_own.transpose(1, 2, 3, 0, 4).reshape(rows_w, 2 * FF)
-    shdown_own = halve_rows(split_rows(grad_shdown, n_dp), n_dp)
-    ein_own = halve_rows(grad_ein, n_dp)
-    edown_own = halve_rows(grad_edown, n_dp)
-    squares = sum(jnp.sum(g * g) for g in (shin_own, shdown_own, ein_own, edown_own))
-    qkv_own, out_own, small_own, norm = reduce_dense(
-        [g.astype(low).reshape(n_all, rows_w, -1) for g in (grad_qkv, grad_out, small_grad)], squares, n_dp, n_exp, 5
-    )
-    qkv_own, mixed_sum = lax.optimization_barrier((qkv_own, mixed_sum))
-    mixed = (residual + mixed_sum.astype(wide)).astype(low)
-    owned_grads = (
-        small_own[:, expert_count : expert_count + 2].T,
-        qkv_own,
-        out_own,
-        shin_own,
-        shdown_own,
-        small_own[:, :expert_count],
-        ein_own[None],
-        edown_own[None],
-    )
-    total_squares = norm[0, 0]
-    grad_norm = jnp.sqrt(total_squares)
-    factor = jnp.minimum(1.0, CLIP / grad_norm)
+    qkv_own, out_own, small_own, dense_squares = reduce_dense(
+        [g.reshape(n_all, rows_w, -1) for g in (grad_qkv, grad_out, small_grad)], n_dp, n_exp, 5
+    )
+    qkv_own, mixed_a, mixed_b = lax.optimization_barrier((qkv_own, mixed_a, mixed_b))
+    mixed_b = lax.psum_scatter(mixed_b, "expert", scatter_dimension=0, tiled=False)
+    norm = sum_squares([[shin_own], shdown_own, ein_own, edown_own], dense_squares, n_dp, n_exp, 6)
+    grad_norm = jnp.sqrt(norm[0, 0])
     weights = (
         norm_gains,
         w_qkv,
@@ -1280,15 +1522,25 @@
         (FF // 64) ** (-0.5),
     )
     decays = (0.0, DECAY, DECAY, DECAY, DECAY, DECAY, DECAY, DECAY)
-    updated = []
-    for weight, first_moment, second_moment, gradient, step_rate, decay_rate in zip(
-        weights, firsts, seconds, owned_grads, rates, decays
-    ):
-        updated.extend(
-            adam_update(
-                weight, first_moment, second_moment, gradient, factor, step_rate, decay_rate
-            )
-        )
+    owned = (
+        [small_own[:, expert_count : expert_count + 16 : 8].T],
+        [qkv_own],
+        [out_own],
+        [shin_own],
+        shdown_own,
+        [small_own[:, :expert_count]],
+        ein_own,
+        edown_own,
+    )
+    order = (6, 7, 0, 1, 2, 3, 4, 5)
+    states = [
+        tuple(a.reshape(a.shape[-2:]) for a in (weights[i], firsts[i], seconds[i])) for i in order
+    ]
+    fresh = adam(norm, states, [owned[i] for i in order], [rates[i] for i in order], [decays[i] for i in order], 2)
+    new = dict(zip(order, fresh))
+    updated = [a.reshape(b.shape) for i in range(8) for a, b in zip(new[i], (weights[i], firsts[i], seconds[i]))]
+    mixed_b, *updated = lax.optimization_barrier((mixed_b, *updated))
+    mixed = (residual + jnp.concatenate([mixed_a, mixed_b], axis=1).astype(wide)).astype(low)
     return (
         mixed,
         input_grad,

time: 715 us -> 695 us (0.972)
  Pallas kernels: 459 us -> 572 us
  matrix products: 60.5 us -> 0 us
  other arithmetic: 75.3 us -> 24.7 us
  waiting for transfers between devices: 43.2 us -> 32.5 us
    pallas_call x0 -> x4, Pallas kernels: none -> 106 us  [the longest x1 38.3 us: attend_back(): pl.pallas_call(functools.partial(attend_back_kernel, H, experts), in_spec...]
    dot_general x14 -> x0, matrix products: 54.7 us -> none  [the longest x1 8.63 us: local(): jnp.einsum('tk,dk->td', projected_grad, qkv_full, preferred_element_type=...]
    sub x8 -> x0, other arithmetic: 22.8 us -> none  [adam_update(): weight - step_rate * (first_hat / (jnp.sqrt(second_hat) + ADAM_EPS) + dec...]
    ppermute x3 -> x2, waiting for transfers between devices: 34.4 us -> 17.6 us  [swap_rows(): return [x, lax.ppermute(x, 'dp', [(0, 1), (1, 0)])]]
    reduce_scatter x1 -> x2, waiting for transfers between devices: 0.02 us -> 14.1 us  [the longest x1 14.1 us: local(): lax.psum_scatter(mixed_b, 'expert', scatter_dimension=0, tiled=False)]
    reduce_sum x7 -> x0, other arithmetic: 10.9 us -> none  [the longest x4 10.6 us: local(): jnp.sum(g * g)]
    ppermute x3 -> x2, waiting for transfers between devices: 8.05 us -> 0.01 us  [the longest x1 0.01 us: local(): lax.ppermute(shdown_halves[1], 'dp', swap)]
    unnamed x154 -> x58, local copies, waits for them, and re-layouts: 16.4 us -> 14.2 us
  transfers between devices with their start and end apart: 10 -> 9, of which waited for: 2 -> 2; matrix products, arithmetic and copies ran while one was open for 22% -> 6% of each run, Pallas kernels for 30% -> 46%
where the time goes in v5:
time: 695 us; the launch traced here: 690 us
  Pallas kernels  572 us (82%)
  local copies, waits for them, and re-layouts  33.6 us (5%)
  waiting for transfers between devices  32.5 us (5%)
  other arithmetic  24.7 us (4%)
  between operations  16.5 us (2%)
  starting transfers between devices  10.9 us (2%)
    pallas_call x1, Pallas kernels, fused(): pl.pallas_call(functools.partial(fused_kernel, n_dp, n_exp, experts, cap,...  251 us
    pallas_call x1, Pallas kernels, reduce_dense(): pl.pallas_call(functools.partial(reduce_kernel, n_dp, n_exp, orders, slic...  117 us
    pallas_call x1, Pallas kernels, gather(): pl.pallas_call(functools.partial(gather_kernel, n_dp, n_exp, orders, slic...  97 us
    pallas_call x1, Pallas kernels, attend_back(): pl.pallas_call(functools.partial(attend_back_kernel, H, experts), in_spec...  38.3 us
    pallas_call x1, Pallas kernels, sum_squares(): pl.pallas_call(functools.partial(norm_kernel, n_dp, n_exp, [len(group) fo...  24.3 us
    pallas_call x1, Pallas kernels, adam(): pl.pallas_call(functools.partial(adam_kernel, rates, decays, big, counts)...  22.4 us
    pallas_call x1, Pallas kernels, attend(): pl.pallas_call(functools.partial(attend_kernel, H, experts), in_specs=[vm...  20.7 us
    ppermute x2, waiting for transfers between devices, swap_rows(): return [x, lax.ppermute(x, 'dp', [(0, 1), (1, 0)])]  17.6 us
  transfers between devices with their start and end apart: 9, of which 2 were waited for; matrix products, arithmetic and copies ran while one was open for 6% of the time, Pallas kernels for 46%

profile of v5, /device:TPU:0, one launch (start us, length us, event | category | flops | bytes accessed | tf_op | source)
XLA Modules:
  0.0 689.6 jit_solution(10407573373893251872)
XLA Ops:
  7.9 1.1 convert.30
  9.1 0.9 convert.31
  12.4 1.1 bitcast_convert_fusion.1.pass_ref.refs_2_
  13.6 97.0 %gather_dense.1 = (bf16[32,40,5248]{2,1,0:T(8,128)(2,1)}, bf16[448,1280]{1,0:T(8,128)(2,1)}) custom-call(bf16[40,5248]{1,0:T(8,128)(2,1)} %concatenate.37.x_ref, bf16[448,1280]{1,0:T(8,128)(2,1)} %bitcast_convert_fusion.1.pass_ref.refs_2_), custom_call_target="tpu_custom_call" | custom-call | tf_op jit(solution)/shard_map/gather_dense/pallas_call | solution.py:274
  110.6 4.0 bitcast_convert_fusion.refs_0_
  114.6 1.6 collective-permute-start
  116.7 1.7 reshape.187
  120.0 3.6 all-to-all-start
  123.8 1.6 slice_reduce_fusion.1
  125.5 1.1 fusion.5
  132.2 20.7 %attend.1 = (bf16[384,1280]{1,0:T(8,128)(2,1)}, bf16[384,1280]{1,0:T(8,128)(2,1)}, bf16[384,1280]{1,0:T(8,128)(2,1)}, bf16[384,1280]{1,0:T(8,128)(2,1)}, f32[384...) custom-call(bf16[384,1280]{1,0:T(8,128)(2,1)} %tok_ref.3, ...), custom_call_target="tpu_custom_call" | custom-call | flops 7000000000 | bytes 25165824 | tf_op jit(solution)/shard_map/attend/pallas_call | solution.py:1081
  154.5 17.6 %collective-permute-done.1 = bf16[28,1280]{1,0:T(8,128)(2,1)S(1)} collective-permute-done((bf16[28,1280]{1,0:T(8,128)(2,1)S(1)}, bf16[28,1280]{1,0:T(8,128)(2,1)S(1)}, u32[]{:S(2)}, u32[]{:S(2)}) %collective-permute-start.1) | collective-permute-done | bytes 71712 | tf_op jit(solution)/shard_map/ppermute | solution.py:1325
  173.1 1.3 pad_maximum_fusion.refs_5_
  174.4 251.5 %experts_fused.1 = (bf16[16,384,1280]{2,1,0:T(8,128)(2,1)}, bf16[16,384,896]{2,1,0:T(8,128)(2,1)}, bf16[16,384,384]{2,1,0:T(8,128)(2,1)}, f32[384,1280]{1,0:T(8,...) custom-call(bf16[384,1280]{1,0:T(8,128)(2,1)} %get-tuple-element.116, ...), custom_call_target="tpu_custom_call" | custom-call | flops 93616865280 | bytes 104857600 | tf_op jit(solution)/shard_map/experts_fused/pallas_call | solution.py:992
  428.3 2.9 all-to-all-start.1
  431.9 1.8 collective-permute-start.2
  433.9 38.3 %attend_back.1 = (bf16[1280,3840]{1,0:T(8,128)(2,1)}, bf16[1280,1280]{1,0:T(8,128)(2,1)}, f32[384,1280]{1,0:T(8,128)}, f32[32,1280]{1,0:T(8,128)}) custom-call(f32[384,1280]{1,0:T(8,128)} %get-tuple-element.119.back_ref, f32[16,384]{1,0:T(8,128)} %bitcast.86, f32[16,384]{1,0:T(8,128)} %get-tuple-element.121.probs_ref, bf16[16,1280]{1,0:T(8,128)(2,1)} %copy.122.router_ref, ...), custom_call_target="tpu_custom_call" | custom-call | flops 14000000000 | bytes 47185920 | tf_op jit(solution)/shard_map/attend_back/pallas_call | solution.py:1159
  474.2 117.3 %reduce_dense.1 = (f32[40,3840]{1,0:T(8,128)}, f32[40,1280]{1,0:T(8,128)}, f32[40,128]{1,0:T(8,128)}, f32[8,128]{1,0:T(8,128)}) custom-call(bf16[32,40,3840]{2,1,0:T(8,128)(2,1)} %bitcast.65, bf16[32,40,1280]{2,1,0:T(8,128)(2,1)} %bitcast.70, bf16[32,40,128]{2,1,0:T(8,128)(2,1)} %bitcast.75), custom_call_target="tpu_custom_call" | custom-call | tf_op jit(solution)/shard_map/reduce_dense/pallas_call | solution.py:484
  594.3 2.1 reshape.205
  596.5 4.0 reduce_sum.29
  600.5 3.3 copy.128
  603.7 2.9 reshape.193.refs_0_.refs_31_
  607.3 1.8 copy-done.1
  609.1 1.3 copy-done.4
  610.4 1.0 copy-done.5
  613.3 24.3 %sum_squares.1.norm_ref = f32[8,128]{1,0:T(8,128)S(1)} custom-call(f32[8,128]{1,0:T(8,128)S(1)} %copy-done.10, f32[40,1792]{1,0:T(8,128)S(1)} %copy-done.5, f32[28,1280]{1,0:T(8,128)S(1)} %copy-done.6, f32[28,1280]{1,0:T(8,128)S(1)} %copy-done.8, bf16[640,1792]{1,0:T(8,128)(2,1)S(1)} %copy-done, bf16[640,1792]{1,0:T(8,128)(2,1)S(1)} %copy-done.1, ...), custom_call_target="tpu_custom_call" | custom-call | tf_op jit(solution)/shard_map/sum_squares/pallas_call | solution.py:1206
  638.9 22.4 %adam.1 = (f32[640,1792]{1,0:T(8,128)}, f32[640,1792]{1,0:T(8,128)}, f32[640,1792]{1,0:T(8,128)}, f32[448,1280]{1,0:T(8,128)}, f32[448,1280]{1,0:T(8,128)}, /*in...) custom-call(f32[8,128]{1,0:T(8,128)} %copy-done.9, ...), custom_call_target="tpu_custom_call" | custom-call | tf_op jit(solution)/shard_map/adam/pallas_call | solution.py:1310
  661.3 14.1 %reduce-scatter.5.cloned.1.call-done = bf16[1,384,384]{2,1,0:T(8,128)(2,1)} async-done(((bf16[16,384,384]{2,1,0:T(8,128)(2,1)}), bf16[1,384,384]{2,1,0:T(8,128)(2,1)}) %reduce-scatter.5.cloned.1.call-update) | async-done | bytes 294928 | tf_op jit(solution)/shard_map/reduce_scatter | solution.py:1481
  675.4 1.4 copy.133
  676.8 1.4 copy.134
  678.2 1.4 copy.135
  679.6 2.1 add_convert_fusion
  (114 shorter events, 24.6 us)
Async XLA Ops:
  7.2 5.2 copy-start.11
  7.2 167.2 %all-gather.3.cloned.1.call-start = ((), (), s32[]{:S(2)}) async-start(), calls=%async_computation.6 | async-start | bytes 16711680 | tf_op jit(solution)/shard_map/all_gather | solution.py:1399
  110.6 5.6 copy-start.13
  110.6 6.1 copy-start.15
  114.6 59.8 %collective-permute-start = (bf16[640,1792]{1,0:T(8,128)(2,1)}, bf16[640,1792]{1,0:T(8,128)(2,1)}, u32[]{:S(2)}, u32[]{:S(2)}) collective-permute-start(bf16[640,1792]{1,0:T(8,128)(2,1)} %bitcast_convert_fusion.refs_0_), channel_id=1, source_target_pairs={{0,16},{16,0},{1,17},{17,1},{2,18},{18,2},{3,19},{19,3},{4,20},{20... | collective-permute-start | bytes 6881288 | tf_op jit(solution)/shard_map/ppermute | solution.py:1325
  116.2 55.9 %collective-permute-start.1 = (bf16[28,1280]{1,0:T(8,128)(2,1)S(1)}, bf16[28,1280]{1,0:T(8,128)(2,1)S(1)}, u32[]{:S(2)}, u32[]{:S(2)}) collective-permute-start(bf16[28,1280]{1,0:T(8,128)(2,1)S(1)} %convert_element_type.80), channel_id=1, source_target_pairs={{0,16},{16,0},{1,17},{17,1},{2,18},{18,2},{3,19},{19,3},{4,20},{20... | collective-permute-start | bytes 215048 | tf_op jit(solution)/shard_map/ppermute | solution.py:1325
  118.9 8.5 %copy-start.24 = (s32[1,4]{1,0:T(1,128)S(1)}, s32[1,4]{1,0:T(1,128)}, u32[]{:S(2)}) copy-start(s32[1,4]{1,0:T(1,128)} %param.29) | copy-start | bytes 52
  118.9 8.7 %copy-start.21 = (s32[384,6]{0,1:T(8,128)S(1)}, s32[384,6]{0,1:T(8,128)}, u32[]{:S(2)}) copy-start(s32[384,6]{0,1:T(8,128)} %param.30) | copy-start | bytes 27652
  120.0 52.9 %all-to-all-start = ((bf16[32,40,112]{2,1,0:T(8,128)(2,1)}), bf16[32,40,112]{2,1,0:T(8,128)(2,1)S(1)}, u32[]{:S(2)}, u32[]{:S(2)}) async-start(bf16[32,40,112]{2,1,0:T(8,128)(2,1)} %pad_maximum_fusion.1), calls=%async_computation | async-start | bytes 655360 | tf_op jit(solution)/shard_map/all_to_all | solution.py:1407
  123.6 468.0 %reduce-scatter.3.cloned.1.call-start = ((), (), s32[]{:S(2)}) async-start(), calls=%async_computation.4 | async-start | bytes 11698176 | tf_op jit(solution)/shard_map/reduce_scatter | solution.py:1430
  425.9 1.3 copy-start.14
  427.2 4.0 copy-start.17
  428.3 45.9 %all-to-all-start.1 = ((bf16[32,40,112]{2,1,0:T(8,128)(2,1)}), bf16[32,40,112]{2,1,0:T(8,128)(2,1)S(1)}, u32[]{:S(2)}, u32[]{:S(2)}) async-start(bf16[32,40,112]{2,1,0:T(8,128)(2,1)} %pad_maximum_fusion.2), calls=%async_computation.1 | async-start | bytes 655360 | tf_op jit(solution)/shard_map/all_to_all | solution.py:1455
  431.2 244.3 %reduce-scatter.5.cloned.1.call-start = ((), (), s32[]{:S(2)}) async-start(), calls=%async_computation.5 | async-start | bytes 5013504 | tf_op jit(solution)/shard_map/reduce_scatter | solution.py:1481
  431.9 42.3 %collective-permute-start.2 = (f32[28,1280]{1,0:T(8,128)S(1)}, f32[28,1280]{1,0:T(8,128)S(1)}, u32[]{:S(2)}, u32[]{:S(2)}) collective-permute-start(f32[28,1280]{1,0:T(8,128)S(1)} %get-tuple-element.339), channel_id=1, source_target_pairs={{0,16},{16,0},{1,17},{17,1},{2,18},{18,2},{3,19},{19,3},{4,20},{20... | collective-permute-start | bytes 430088 | tf_op jit(solution)/shard_map/ppermute | solution.py:1461
  433.7 40.5 %collective-permute-start.3 = (bf16[448,1280]{1,0:T(8,128)(2,1)}, bf16[448,1280]{1,0:T(8,128)(2,1)S(1)}, u32[]{:S(2)}, u32[]{:S(2)}) collective-permute-start(bf16[448,1280]{1,0:T(8,128)(2,1)} %get-tuple-element.130), channel_id=1, source_target_pairs={{0,16},{16,0},{1,17},{17,1},{2,18},{18,2},{3,19},{19,3},{4,20},{20... | collective-permute-start | bytes 3440648 | tf_op jit(solution)/shard_map/ppermute | solution.py:1461
  474.2 117.3 %copy-start.7 = (f32[28,1280]{1,0:T(8,128)}, f32[28,1280]{1,0:T(8,128)S(1)}, u32[]{:S(2)}) copy-start(f32[28,1280]{1,0:T(8,128)S(1)} %collective-permute-done.2.refs_2_.refs_33_) | copy-start | bytes 430084
  474.2 117.3 %copy-start.3 = (bf16[448,1280]{1,0:T(8,128)(2,1)}, bf16[448,1280]{1,0:T(8,128)(2,1)S(1)}, u32[]{:S(2)}) copy-start(bf16[448,1280]{1,0:T(8,128)(2,1)S(1)} %collective-permute-done.3.refs_6_.refs_27_) | copy-start | bytes 3440644
  591.6 1.4 copy-start.22
  591.6 2.0 copy-start.23
  600.4 6.2 copy-start.18
  600.4 6.9 copy-start
  600.5 6.9 copy-start.2
  600.5 6.9 copy-start.10
  607.3 1.8 copy-start.1
  609.1 1.3 copy-start.4
  610.4 1.0 copy-start.5
  611.4 0.9 copy-start.6
  612.3 1.0 copy-start.8
  637.6 1.2 copy-start.9
  638.8 40.8 %copy-start.12 = (f32[384,1280]{1,0:T(8,128)S(1)}, f32[384,1280]{1,0:T(8,128)}, u32[]{:S(2)}) copy-start(f32[384,1280]{1,0:T(8,128)} %get-tuple-element.115.resid_ref) | copy-start | bytes 5898244
  638.8 40.8 %copy-start.16 = (bf16[1,384,896]{2,1,0:T(8,128)(2,1)S(1)}, bf16[1,384,896]{2,1,0:T(8,128)(2,1)}, u32[]{:S(2)}) copy-start(bf16[1,384,896]{2,1,0:T(8,128)(2,1)} %reduce-scatter.3.cloned.1.call-done) | copy-start | bytes 2064388
  (2 other events, 1.4 us)
Sparse Core Ops, SparseCore 0:
  10.3 150.4 all-gather.2
  426.0 164.5 reduce-scatter.2
  595.0 80.4 reduce-scatter.4

commit v6 on v5

--- a/solution.py
+++ b/solution.py
@@ -14,6 +14,7 @@
 FF = 896
 TOP = 6
 ADAM_STEP = 5
+HEAD = 192
 MIXED_FIRST = 896
 GIVEN = 1280
 
@@ -237,25 +238,27 @@
     return {"A": na, "B": rest // na, "C": 2, "Y": n_dp}
 
 
-def gather_kernel(n_dp, n_exp, orders, slices, dense, x_ref, pass_ref, out_ref, passed_ref, send_sem, recv_sem,
-                  local_sem, pass_send, pass_recv):
+def gather_kernel(n_dp, n_exp, orders, slices, dense, n_pass, x_ref, *refs):
+    pass_refs, out_ref, passed_refs = refs[:n_pass], refs[n_pass], refs[n_pass + 1:2 * n_pass + 1]
+    send_sem, recv_sem, local_sem, pass_send, pass_recv = refs[2 * n_pass + 1:]
     place = Place(n_dp, n_exp)
+    pieces = [(q, r) for q in range(n_pass) for r in range(pass_refs[q].shape[0] // PIECE)] if n_dp == 2 else []
 
     def piece(n):
-        rows = pl.ds(n * PIECE, PIECE)
+        q, r = pieces[n]
+        rows = pl.ds(r * PIECE, PIECE)
         return pltpu.make_async_remote_copy(
-            src_ref=pass_ref.at[rows], dst_ref=passed_ref.at[rows], send_sem=pass_send.at[n], recv_sem=pass_recv.at[n],
+            src_ref=pass_refs[q].at[rows], dst_ref=passed_refs[q].at[rows], send_sem=pass_send.at[n], recv_sem=pass_recv.at[n],
             device_id=place.device(place.moved(Y=1)), device_id_type=MESH)
 
-    pieces = pass_ref.shape[0] // PIECE if n_dp == 2 else 0
     block_of = place.flat if dense else place.expert
     place.greet(orders[0], False)
     own = pltpu.make_async_copy(x_ref, out_ref.at[block_of(place.pos)], local_sem)
     own.start()
     gather_body(place, orders, slices, x_ref, out_ref, block_of, send_sem, recv_sem,
-                [lambda n=n: piece(n).start() for n in range(pieces)])
+                [lambda n=n: piece(n).start() for n in range(len(pieces))])
     own.wait()
-    for n in range(pieces):
+    for n in range(len(pieces)):
         piece(n).wait()
 
 
@@ -272,21 +275,21 @@
         slices = tuple((i * w, w) for i in range(len(orders)))
     blocks = n_exp * (n_dp if dense else 1)
     return pl.pallas_call(
-        functools.partial(gather_kernel, n_dp, n_exp, orders, slices, dense),
-        out_shape=[
-            jax.ShapeDtypeStruct((blocks, rows, cols), x.dtype), jax.ShapeDtypeStruct(passed.shape, passed.dtype)],
-        in_specs=[pl.BlockSpec(memory_space=pl.ANY)] * 2,
-        out_specs=[pl.BlockSpec(memory_space=pl.ANY)] * 2,
+        functools.partial(gather_kernel, n_dp, n_exp, orders, slices, dense, len(passed)),
+        out_shape=[jax.ShapeDtypeStruct((blocks, rows, cols), x.dtype)] + [
+            jax.ShapeDtypeStruct(p.shape, p.dtype) for p in passed],
+        in_specs=[pl.BlockSpec(memory_space=pl.ANY)] * (1 + len(passed)),
+        out_specs=[pl.BlockSpec(memory_space=pl.ANY)] * (1 + len(passed)),
         scratch_shapes=[
             pltpu.SemaphoreType.DMA((count_gather(size, orders),)),
             pltpu.SemaphoreType.DMA((len(orders), blocks)),
             pltpu.SemaphoreType.DMA(()),
-            pltpu.SemaphoreType.DMA((max(1, passed.shape[0] // PIECE),)),
-            pltpu.SemaphoreType.DMA((max(1, passed.shape[0] // PIECE),)),
+            pltpu.SemaphoreType.DMA((max(1, sum(p.shape[0] // PIECE for p in passed)),)),
+            pltpu.SemaphoreType.DMA((max(1, sum(p.shape[0] // PIECE for p in passed)),)),
         ],
         compiler_params=pltpu.CompilerParams(collective_id=cid, has_side_effects=True),
         name="gather_dense" if dense else "gather_group",
-    )(x, passed)
+    )(x, *passed)
 
 
 def line_order(n):
@@ -538,8 +541,8 @@
     return out
 
 
-def fused_kernel(n_dp, n_exp, experts, cap, halves, x_ref, cot_ref, rank_own, *refs):
-    win_h, wdown_h, refs = refs[:halves], refs[halves:2 * halves], refs[2 * halves:]
+def fused_kernel(n_dp, n_exp, experts, cap, n_in, halves, x_ref, cot_ref, rank_own, *refs):
+    win_h, wdown_h, refs = refs[:n_in], refs[n_in:n_in + halves], refs[n_in + halves:]
     wrt_h, wshin_h, wshdown_h, xall, mixed_a, mixed_b, total_out, gg_out, refs = *refs[:8], refs[8:]
     gin_out, gdown_out, refs = refs[:halves], refs[halves:2 * halves], refs[2 * halves:]
     fused_body(n_dp, n_exp, experts, cap, x_ref, cot_ref, rank_own, win_h, wdown_h, wrt_h, wshin_h, wshdown_h,
@@ -573,9 +576,9 @@
     barrier = pltpu.get_barrier_semaphore()
     for s in range(1, n_exp):
         pl.semaphore_signal(barrier, inc=1, device_id=(pos["Y"], lax.rem(me + s, n_exp)), device_id_type=MESH)
-    if len(win_h) == 2:
+    if len(wdown_h) == 2:
         pl.semaphore_signal(barrier, inc=1, device_id=place.device(place.moved(Y=1)), device_id_type=MESH)
-    pl.semaphore_wait(barrier, n_exp - 1 + (len(win_h) == 2))
+    pl.semaphore_wait(barrier, n_exp - 1 + (len(wdown_h) == 2))
 
     def rank_copy(s):
         j = lax.rem(me + s, n_exp)
@@ -656,10 +659,13 @@
 
     moves = [(wrt_h, wrt), (wshin_h, wshin), (wshdown_h, wshdown)]
     for pieces, whole in ((win_h, win), (wdown_h, wdown)):
-        for n, piece in enumerate(pieces):
-            rows = piece.shape[0]
-            start = lax.rem(pos["Y"] + n, len(pieces)) * rows
-            moves.append((piece, whole.at[pl.ds(pl.multiple_of(start, 16), rows)]))
+        here = max(len(pieces) // 2, 1)
+        base = sum(piece.shape[0] for piece in pieces[:here])
+        for first in range(0, len(pieces), here):
+            start = lax.rem(pos["Y"] + first // here, len(pieces) // here) * base
+            for piece in pieces[first:first + here]:
+                moves.append((piece, whole.at[pl.ds(pl.multiple_of(start, 16), piece.shape[0])]))
+                start = start + piece.shape[0]
     wloads = [pltpu.make_async_copy(h, v, w_sem.at[i]) for i, (h, v) in enumerate(moves)]
     for load in wloads:
         load.start()
@@ -990,22 +996,23 @@
     ag_count = 2 + (nb - 1) + 1 + (na - 1) * (2 + nb) + na * (nb - 1)
     flops = 2 * n_exp * (cap * d * FF * 9 + toks * cap * d * 4 + toks * d * hid * 9)
     out = pl.pallas_call(
-        functools.partial(fused_kernel, n_dp, n_exp, experts, cap, len(win)),
-        in_specs=[hbm, hbm, vmem] + [hbm] * (2 * len(win) + 3),
+        functools.partial(fused_kernel, n_dp, n_exp, experts, cap, len(win), len(wdown)),
+        in_specs=[hbm, hbm, vmem] + [hbm] * (len(win) + len(wdown) + 3),
         out_shape=[
             jax.ShapeDtypeStruct((n_exp,) + x.shape, low),
             jax.ShapeDtypeStruct((n_exp, toks, MIXED_FIRST), low),
             jax.ShapeDtypeStruct((n_exp, toks, d - MIXED_FIRST), low),
             jax.ShapeDtypeStruct(block, wide),
             jax.ShapeDtypeStruct((n_exp, 1, toks), wide),
-            *[jax.ShapeDtypeStruct(w.shape, low) for w in (*win, *wdown)],
+            *[jax.ShapeDtypeStruct((d // len(wdown), 2 * FF), low) for _ in wdown],
+            *[jax.ShapeDtypeStruct(w.shape, low) for w in wdown],
             jax.ShapeDtypeStruct((d, 2 * hid), wide),
             jax.ShapeDtypeStruct((hid, d), wide),
             jax.ShapeDtypeStruct((steps,) + block, low),
             jax.ShapeDtypeStruct((na * max(nb - 1, 1),) + block, low),
             jax.ShapeDtypeStruct((na,) + block, low),
         ],
-        out_specs=[hbm, hbm, hbm, hbm, vmem] + [hbm] * (2 * len(win)) + [vmem, vmem, hbm, hbm, hbm],
+        out_specs=[hbm, hbm, hbm, hbm, vmem] + [hbm] * (2 * len(wdown)) + [vmem, vmem, hbm, hbm, hbm],
         scratch_shapes=[
             pltpu.VMEM((d, 2 * FF), low), pltpu.VMEM((FF, d), low), pltpu.VMEM(wrt.shape, low),
             pltpu.VMEM(wshin.shape, low), pltpu.VMEM(wshdown.shape, low), pltpu.VMEM((n_exp, 1, toks), wide),
@@ -1015,7 +1022,7 @@
             pltpu.VMEM((2, 2) + block, low), pltpu.VMEM((2, 2) + block, low), pltpu.VMEM((na,) + block, low),
             pltpu.VMEM((2,) + block, low), pltpu.VMEM((nb,) + block, low),
             pltpu.VMEM((steps, 2, 1, toks), wide), pltpu.VMEM((d, 2 * FF), wide), pltpu.VMEM((FF, d), wide),
-            dma((3 + 2 * len(win),)), dma((2, 2)), dma((2, 2)), dma((2, 2, 2)), dma((nb,)),
+            dma((3 + len(win) + len(wdown),)), dma((2, 2)), dma((2, 2)), dma((2, 2, 2)), dma((nb,)),
             dma((ag_count,)), dma((n_exp,)), dma((steps,)), dma((steps,)),
             dma((na * max(nb - 1, 1),)), dma((na * max(nb - 1, 1),)), dma((na,)), dma((na,)),
             dma((steps, 2)), dma((n_exp,)), dma((n_exp,)), dma((n_exp,)), dma(()), dma(()),
@@ -1024,7 +1031,7 @@
         cost_estimate=pl.CostEstimate(flops=flops, bytes_accessed=100 * 1024 * 1024, transcendentals=0),
         name="experts_fused",
     )(x, cot_all, rank, *win, *wdown, wrt, wshin, wshdown)
-    n = len(win)
+    n = len(wdown)
     return out[1], out[2], out[3], out[4], out[5:5 + n], out[5 + n:5 + 2 * n], out[5 + 2 * n], out[6 + 2 * n]
 
 
@@ -1387,25 +1394,36 @@
     pad = jnp.zeros((rows_w, 128 - expert_count - 2), wide)
     packed = jnp.concatenate([w_qkv, w_out, w_router, norm_gains.T, pad], axis=1).astype(low)
     edown_low = w_expert_down[0].astype(low)
-    full, edown_other = gather(packed, edown_low, n_dp, n_exp, True, 1)
+    passed = [edown_low]
+    early = HEAD if n_dp == 2 else 0
+    if n_dp == 2:
+        passed.append(w_expert_in[0, :early].astype(low))
+    packed, passed, cot_late = lax.optimization_barrier((packed, passed, cotangent))
+    full, *others = gather(packed, passed, n_dp, n_exp, True, 1)
     full = full.reshape(D, -1)
-    expert_down_full = [edown_low, edown_other] if n_dp == 2 else swap_rows(edown_low, n_dp)
-    full, ein_low = lax.optimization_barrier((full, w_expert_in[0].astype(low)))
-    expert_in_full = swap_rows(ein_low, n_dp)
+    full, ein_rest, shin_low, shdown_low = lax.optimization_barrier(
+        (full, w_expert_in[0, early:].astype(low), w_shared_in.astype(low), w_shared_down.astype(low))
+    )
+    if n_dp == 2:
+        rest_other = lax.ppermute(ein_rest, "dp", [(0, 1), (1, 0)])
+        expert_in_full = [passed[1], ein_rest, others[1], rest_other]
+        expert_down_full = [passed[0], others[0]]
+    else:
+        expert_in_full, expert_down_full = swap_rows(ein_rest, n_dp), swap_rows(passed[0], n_dp)
     small_full = full[:, 3 * H * HD + D :]
     router_full = small_full[:, :expert_count]
     gain_one = small_full[:, expert_count].astype(wide)
     gain_two = small_full[:, expert_count + 1].astype(wide)
-    cot_all = lax.all_gather(cotangent[:, :GIVEN], "expert", axis=0, tiled=False)
+    cot_all = lax.all_gather(cot_late[:, :GIVEN], "expert", axis=0, tiled=False)
     shin_send = (
-        w_shared_in.astype(low)
+        shin_low
         .reshape(rows_w, 2, n_dp, n_exp, unit)
         .transpose(3, 0, 1, 2, 4)
         .reshape(n_exp, rows_w, 2 * n_dp * unit)
     )
     shin_send = jnp.concatenate([shin_send] * n_dp, axis=0)
     shin_mine = lax.all_to_all(shin_send, both, 0, 0, tiled=True).reshape(D, 2 * n_dp * unit)
-    shdown_mine = in_order(swap_rows(w_shared_down.astype(low), n_dp))
+    shdown_mine = in_order(swap_rows(shdown_low, n_dp))
     half = n_dp * unit
 
     gain_rows = jnp.stack([gain_one, gain_two])
@@ -1455,11 +1473,15 @@
     shin_back = lax.all_to_all(
         grad_shin.astype(low).reshape(n_all, rows_w, 2 * half), both, 0, 0, tiled=True
     )
+    shin_own = jnp.sum(
+        shin_back.reshape(n_dp, n_exp, rows_w, 2, n_dp, unit).astype(wide), axis=0
+    )
+    shin_own = shin_own.transpose(1, 2, 3, 0, 4).reshape(rows_w, 2 * FF)
     shdown_halves = split_rows(grad_shdown, n_dp)
     if n_dp == 2:
         swap = [(0, 1), (1, 0)]
         came = (lax.ppermute(shdown_halves[1], "dp", swap), lax.ppermute(grad_edown[1], "dp", swap))
-        grad_qkv, shin_back, came = lax.optimization_barrier((grad_qkv, shin_back, came))
+        grad_qkv, shin_own, came = lax.optimization_barrier((grad_qkv, shin_own, came))
         shdown_own = [shdown_halves[0], came[0]]
         edown_own = [grad_edown[0], came[1]]
         ein_own = list(grad_ein)
@@ -1470,10 +1492,6 @@
     small_grad = jnp.concatenate(
         [small_rows.astype(low).T, jnp.zeros((D, 128 - expert_count - 16), low)], axis=1
     )
-    shin_own = jnp.sum(
-        shin_back.reshape(n_dp, n_exp, rows_w, 2, n_dp, unit).astype(wide), axis=0
-    )
-    shin_own = shin_own.transpose(1, 2, 3, 0, 4).reshape(rows_w, 2 * FF)
     qkv_own, out_own, small_own, dense_squares = reduce_dense(
         [g.reshape(n_all, rows_w, -1) for g in (grad_qkv, grad_out, small_grad)], n_dp, n_exp, 5
     )
@@ -1528,17 +1546,17 @@
         [out_own],
         [shin_own],
         shdown_own,
-        [small_own[:, :expert_count]],
+        [small_own[:, :expert_count].T],
         ein_own,
         edown_own,
     )
     order = (6, 7, 0, 1, 2, 3, 4, 5)
     states = [
-        tuple(a.reshape(a.shape[-2:]) for a in (weights[i], firsts[i], seconds[i])) for i in order
+        tuple(a.T if i == 5 else a.reshape(a.shape[-2:]) for a in (weights[i], firsts[i], seconds[i])) for i in order
     ]
     fresh = adam(norm, states, [owned[i] for i in order], [rates[i] for i in order], [decays[i] for i in order], 2)
     new = dict(zip(order, fresh))
-    updated = [a.reshape(b.shape) for i in range(8) for a, b in zip(new[i], (weights[i], firsts[i], seconds[i]))]
+    updated = [a.T if i == 5 else a.reshape(b.shape) for i in range(8) for a, b in zip(new[i], (weights[i], firsts[i], seconds[i]))]
     mixed_b, *updated = lax.optimization_barrier((mixed_b, *updated))
     mixed = (residual + jnp.concatenate([mixed_a, mixed_b], axis=1).astype(wide)).astype(low)
     return (

time: 695 us -> 686 us (0.987)
  Pallas kernels: 572 us -> 565 us
    ppermute x2 -> x1, waiting for transfers between devices: 17.6 us -> 0.01 us  [swap_rows(): return [x, lax.ppermute(x, 'dp', [(0, 1), (1, 0)])]]
    pallas_call x1, Pallas kernels: 117 us -> 104 us  [reduce_dense(): pl.pallas_call(functools.partial(reduce_kernel, n_dp, n_exp, orders, slic...]
    reduce_scatter x1, waiting for transfers between devices: 14.1 us -> 26.5 us  [local(): lax.psum_scatter(mixed_b, 'expert', scatter_dimension=0, tiled=False)]
    unnamed x58 -> x48, local copies, waits for them, and re-layouts: 14.2 us -> 9.17 us
  transfers between devices with their start and end apart: 9 -> 9, of which waited for: 2 -> 2; matrix products, arithmetic and copies ran while one was open for 6% -> 5% of each run, Pallas kernels for 46% -> 46%
where the time goes in v6:
time: 686 us; the launch traced here: 681 us
  Pallas kernels  565 us (82%)
  waiting for transfers between devices  31.7 us (5%)
  local copies, waits for them, and re-layouts  31.3 us (5%)
  other arithmetic  23.3 us (3%)
  between operations  16.2 us (2%)
  starting transfers between devices  14.1 us (2%)
    pallas_call x1, Pallas kernels, fused(): pl.pallas_call(functools.partial(fused_kernel, n_dp, n_exp, experts, cap,...  252 us
    pallas_call x1, Pallas kernels, reduce_dense(): pl.pallas_call(functools.partial(reduce_kernel, n_dp, n_exp, orders, slic...  104 us
    pallas_call x1, Pallas kernels, gather(): pl.pallas_call(functools.partial(gather_kernel, n_dp, n_exp, orders, slic...  103 us
    pallas_call x1, Pallas kernels, attend_back(): pl.pallas_call(functools.partial(attend_back_kernel, H, experts), in_spec...  38.3 us
    reduce_scatter x1, waiting for transfers between devices, local(): lax.psum_scatter(mixed_b, 'expert', scatter_dimension=0, tiled=False)  26.5 us
    pallas_call x1, Pallas kernels, adam(): pl.pallas_call(functools.partial(adam_kernel, rates, decays, big, counts)...  23 us
    pallas_call x1, Pallas kernels, sum_squares(): pl.pallas_call(functools.partial(norm_kernel, n_dp, n_exp, [len(group) fo...  22.3 us
    pallas_call x1, Pallas kernels, attend(): pl.pallas_call(functools.partial(attend_kernel, H, experts), in_specs=[vm...  21.5 us
  transfers between devices with their start and end apart: 9, of which 2 were waited for; matrix products, arithmetic and copies ran while one was open for 5% of the time, Pallas kernels for 46%

profile of v6, /device:TPU:0, one launch (start us, length us, event | category | flops | bytes accessed | tf_op | source)
XLA Modules:
  0.0 681.1 jit_solution(3033566957455538076)
XLA Ops:
  8.8 1.1 convert.35
  9.9 1.4 convert.34
  11.3 2.8 bitcast_convert_fusion.refs_0_.refs_4_
  16.2 102.6 %gather_dense.1 = (bf16[32,40,5248]{2,1,0:T(8,128)(2,1)}, bf16[448,1280]{1,0:T(8,128)(2,1)}, bf16[192,1792]{1,0:T(8,128)(2,1)}) custom-call(bf16[40,5248]{1,0:T(8,128)(2,1)} %concatenate.37.x_ref, bf16[448,1280]{1,0:T(8,128)(2,1)} %bitcast_convert_fusion.refs_0_.refs_4_, bf16[192,1792]{1,0:T(8,128)(2,1)} %slice_bitcast_fusion.1.refs_1_.refs_0_), custom_call_target="tpu_custom_call" | custom-call | tf_op jit(solution)/shard_map/gather_dense/pallas_call | solution.py:277
  118.8 1.3 slice_bitcast_fusion.refs_1_
  120.5 1.7 reshape.191
  123.8 5.6 all-to-all-start
  129.7 1.8 collective-permute-start
  132.9 1.7 slice_reduce_fusion.1
  134.6 1.1 fusion.5
  138.9 0.9 fusion.1.bias_ref
  139.8 21.5 %attend.1 = (bf16[384,1280]{1,0:T(8,128)(2,1)}, bf16[384,1280]{1,0:T(8,128)(2,1)}, bf16[384,1280]{1,0:T(8,128)(2,1)}, bf16[384,1280]{1,0:T(8,128)(2,1)}, f32[384...) custom-call(bf16[384,1280]{1,0:T(8,128)(2,1)} %tok_ref.3, ...), custom_call_target="tpu_custom_call" | custom-call | flops 7000000000 | bytes 25165824 | tf_op jit(solution)/shard_map/attend/pallas_call | solution.py:1088
  164.0 1.3 pad_maximum_fusion.refs_7_
  165.3 5.1 collective-permute-done.refs_3_
  170.4 252.5 %experts_fused.1 = (bf16[16,384,1280]{2,1,0:T(8,128)(2,1)}, bf16[16,384,896]{2,1,0:T(8,128)(2,1)}, bf16[16,384,384]{2,1,0:T(8,128)(2,1)}, f32[384,1280]{1,0:T(8,...) custom-call(bf16[384,1280]{1,0:T(8,128)(2,1)} %get-tuple-element.126, ...), custom_call_target="tpu_custom_call" | custom-call | flops 93616865280 | bytes 104857600 | tf_op jit(solution)/shard_map/experts_fused/pallas_call | solution.py:998
  424.9 1.5 collective-permute-start.2
  427.5 2.6 all-to-all-start.1
  430.1 1.7 collective-permute-start.3
  431.8 38.3 %attend_back.1 = (bf16[1280,3840]{1,0:T(8,128)(2,1)}, bf16[1280,1280]{1,0:T(8,128)(2,1)}, f32[384,1280]{1,0:T(8,128)}, f32[32,1280]{1,0:T(8,128)}) custom-call(f32[384,1280]{1,0:T(8,128)} %get-tuple-element.133.back_ref, f32[16,384]{1,0:T(8,128)} %bitcast.96, f32[16,384]{1,0:T(8,128)} %get-tuple-element.135.probs_ref, bf16[16,1280]{1,0:T(8,128)(2,1)} %copy.102.router_ref, ...), custom_call_target="tpu_custom_call" | custom-call | flops 14000000000 | bytes 47185920 | tf_op jit(solution)/shard_map/attend_back/pallas_call | solution.py:1166
  472.1 3.6 reshape.210
  475.7 4.2 reduce_sum.29
  479.9 1.8 copy.107
  481.8 2.9 reshape.194.refs_0_.refs_31_
  484.7 104.4 %reduce_dense.1 = (f32[40,3840]{1,0:T(8,128)}, f32[40,1280]{1,0:T(8,128)}, f32[40,128]{1,0:T(8,128)}, f32[8,128]{1,0:T(8,128)}) custom-call(bf16[32,40,3840]{2,1,0:T(8,128)(2,1)} %bitcast.75, bf16[32,40,1280]{2,1,0:T(8,128)(2,1)} %bitcast.80, bf16[32,40,128]{2,1,0:T(8,128)(2,1)} %bitcast.85), custom_call_target="tpu_custom_call" | custom-call | tf_op jit(solution)/shard_map/reduce_dense/pallas_call | solution.py:487
  589.1 1.6 copy-done
  591.0 1.6 copy-done.1
  592.7 1.3 copy-done.4
  593.9 1.0 copy-done.5
  596.7 22.3 %sum_squares.1.norm_ref = f32[8,128]{1,0:T(8,128)S(1)} custom-call(f32[8,128]{1,0:T(8,128)S(1)} %copy-done.10, f32[40,1792]{1,0:T(8,128)S(1)} %copy-done.5, f32[28,1280]{1,0:T(8,128)S(1)} %copy-done.6, f32[28,1280]{1,0:T(8,128)S(1)} %copy-done.8, bf16[640,1792]{1,0:T(8,128)(2,1)S(1)} %copy-done, bf16[640,1792]{1,0:T(8,128)(2,1)S(1)} %copy-done.1, ...), custom_call_target="tpu_custom_call" | custom-call | tf_op jit(solution)/shard_map/sum_squares/pallas_call | solution.py:1213
  621.6 23.0 %adam.1 = (f32[640,1792]{1,0:T(8,128)}, f32[640,1792]{1,0:T(8,128)}, f32[640,1792]{1,0:T(8,128)}, f32[448,1280]{1,0:T(8,128)}, f32[448,1280]{1,0:T(8,128)}, /*in...) custom-call(f32[8,128]{1,0:T(8,128)} %copy-done.9, ...), custom_call_target="tpu_custom_call" | custom-call | tf_op jit(solution)/shard_map/adam/pallas_call | solution.py:1317
  644.6 26.5 %reduce-scatter.5.cloned.1.call-done = bf16[1,384,384]{2,1,0:T(8,128)(2,1)} async-done(((bf16[16,384,384]{2,1,0:T(8,128)(2,1)}), bf16[1,384,384]{2,1,0:T(8,128)(2,1)}) %reduce-scatter.5.cloned.1.call-update) | async-done | bytes 294928 | tf_op jit(solution)/shard_map/reduce_scatter | solution.py:1499
  671.1 2.1 add_convert_fusion
  (107 shorter events, 22.3 us)
Async XLA Ops:
  7.2 163.2 %all-gather.3.cloned.1.call-start = ((), (), s32[]{:S(2)}) async-start(), calls=%async_computation.6 | async-start | bytes 16711680 | tf_op jit(solution)/shard_map/all_gather | solution.py:1417
  8.8 5.2 copy-start.11
  14.3 1.8 copy-start.17
  14.3 1.8 copy-start.15
  120.0 9.7 %copy-start.13 = (bf16[448,1792]{1,0:T(8,128)(2,1)S(1)}, bf16[448,1792]{1,0:T(8,128)(2,1)}, u32[]{:S(2)}) copy-start(bf16[448,1792]{1,0:T(8,128)(2,1)} %slice_bitcast_fusion.refs_1_) | copy-start | bytes 4816900
  120.0 11.5 %copy-start.22 = (s32[1,4]{1,0:T(1,128)S(1)}, s32[1,4]{1,0:T(1,128)}, u32[]{:S(2)}) copy-start(s32[1,4]{1,0:T(1,128)} %param.29) | copy-start | bytes 52
  120.0 11.7 %copy-start.21 = (s32[384,6]{0,1:T(8,128)S(1)}, s32[384,6]{0,1:T(8,128)}, u32[]{:S(2)}) copy-start(s32[384,6]{0,1:T(8,128)} %param.30) | copy-start | bytes 27652
  120.0 42.9 %collective-permute-start.1 = (bf16[28,1280]{1,0:T(8,128)(2,1)S(1)}, bf16[28,1280]{1,0:T(8,128)(2,1)S(1)}, u32[]{:S(2)}, u32[]{:S(2)}) collective-permute-start(bf16[28,1280]{1,0:T(8,128)(2,1)S(1)} %convert_element_type.80), channel_id=1, source_target_pairs={{0,16},{16,0},{1,17},{17,1},{2,18},{18,2},{3,19},{19,3},{4,20},{20... | collective-permute-start | bytes 215048 | tf_op jit(solution)/shard_map/ppermute | solution.py:1332
  123.8 40.0 %all-to-all-start = ((bf16[32,40,112]{2,1,0:T(8,128)(2,1)}), bf16[32,40,112]{2,1,0:T(8,128)(2,1)S(1)}, u32[]{:S(2)}, u32[]{:S(2)}) async-start(bf16[32,40,112]{2,1,0:T(8,128)(2,1)} %pad_maximum_fusion.1), calls=%async_computation | async-start | bytes 655360 | tf_op jit(solution)/shard_map/all_to_all | solution.py:1425
  129.4 459.6 %reduce-scatter.3.cloned.1.call-start = ((), (), s32[]{:S(2)}) async-start(), calls=%async_computation.4 | async-start | bytes 11698176 | tf_op jit(solution)/shard_map/reduce_scatter | solution.py:1448
  129.7 40.7 %collective-permute-start = (bf16[448,1792]{1,0:T(8,128)(2,1)S(1)}, bf16[448,1792]{1,0:T(8,128)(2,1)}, u32[]{:S(2)}, u32[]{:S(2)}) collective-permute-start(bf16[448,1792]{1,0:T(8,128)(2,1)S(1)} %copy-done.13), channel_id=1, source_target_pairs={{0,16},{16,0},{1,17},{17,1},{2,18},{18,2},{3,19},{19,3},{4,20},{20... | collective-permute-start | bytes 4816904 | tf_op jit(solution)/shard_map/ppermute | solution.py:1408
  422.9 0.7 copy-start.19
  422.9 1.3 copy-start.18
  422.9 3.5 copy-start.14
  424.9 59.7 %collective-permute-start.2 = (f32[28,1280]{1,0:T(8,128)S(1)}, f32[28,1280]{1,0:T(8,128)S(1)}, u32[]{:S(2)}, u32[]{:S(2)}) collective-permute-start(f32[28,1280]{1,0:T(8,128)S(1)} %get-tuple-element.218), channel_id=1, source_target_pairs={{0,16},{16,0},{1,17},{17,1},{2,18},{18,2},{3,19},{19,3},{4,20},{20... | collective-permute-start | bytes 430088 | tf_op jit(solution)/shard_map/ppermute | solution.py:1483
  427.5 44.6 %all-to-all-start.1 = ((bf16[32,40,112]{2,1,0:T(8,128)(2,1)}), bf16[32,40,112]{2,1,0:T(8,128)(2,1)S(1)}, u32[]{:S(2)}, u32[]{:S(2)}) async-start(bf16[32,40,112]{2,1,0:T(8,128)(2,1)} %pad_maximum_fusion.2), calls=%async_computation.1 | async-start | bytes 655360 | tf_op jit(solution)/shard_map/all_to_all | solution.py:1473
  430.1 241.0 %reduce-scatter.5.cloned.1.call-start = ((), (), s32[]{:S(2)}) async-start(), calls=%async_computation.5 | async-start | bytes 5013504 | tf_op jit(solution)/shard_map/reduce_scatter | solution.py:1499
  430.1 54.5 %collective-permute-start.3 = (bf16[448,1280]{1,0:T(8,128)(2,1)}, bf16[448,1280]{1,0:T(8,128)(2,1)S(1)}, u32[]{:S(2)}, u32[]{:S(2)}) collective-permute-start(bf16[448,1280]{1,0:T(8,128)(2,1)} %get-tuple-element.144), channel_id=1, source_target_pairs={{0,16},{16,0},{1,17},{17,1},{2,18},{18,2},{3,19},{19,3},{4,20},{20... | collective-permute-start | bytes 3440648 | tf_op jit(solution)/shard_map/ppermute | solution.py:1483
  484.6 104.4 %copy-start.7 = (f32[28,1280]{1,0:T(8,128)}, f32[28,1280]{1,0:T(8,128)S(1)}, u32[]{:S(2)}) copy-start(f32[28,1280]{1,0:T(8,128)S(1)} %collective-permute-done.2.refs_2_.refs_33_) | copy-start | bytes 430084
  484.6 104.4 %copy-start.3 = (bf16[448,1280]{1,0:T(8,128)(2,1)}, bf16[448,1280]{1,0:T(8,128)(2,1)S(1)}, u32[]{:S(2)}) copy-start(bf16[448,1280]{1,0:T(8,128)(2,1)S(1)} %collective-permute-done.3.refs_6_.refs_27_) | copy-start | bytes 3440644
  589.1 1.6 copy-start
  589.1 1.9 copy-start.2
  589.1 1.9 copy-start.10
  591.0 1.6 copy-start.1
  592.7 1.3 copy-start.4
  593.9 1.0 copy-start.5
  594.9 0.9 copy-start.6
  595.8 0.9 copy-start.8
  596.7 23.6 %copy-start.20 = (f32[40,128]{1,0:T(8,128)S(1)}, f32[40,128]{1,0:T(8,128)}, u32[]{:S(2)}) copy-start(f32[40,128]{1,0:T(8,128)} %get-tuple-element.160) | copy-start | bytes 61444
  619.1 2.5 copy-start.9
  621.6 49.5 %copy-start.12 = (f32[384,1280]{1,0:T(8,128)S(1)}, f32[384,1280]{1,0:T(8,128)}, u32[]{:S(2)}) copy-start(f32[384,1280]{1,0:T(8,128)} %get-tuple-element.125.resid_ref) | copy-start | bytes 5898244
  621.6 49.5 %copy-start.16 = (bf16[1,384,896]{2,1,0:T(8,128)(2,1)S(1)}, bf16[1,384,896]{2,1,0:T(8,128)(2,1)}, u32[]{:S(2)}) copy-start(bf16[1,384,896]{2,1,0:T(8,128)(2,1)} %reduce-scatter.3.cloned.1.call-done) | copy-start | bytes 2064388
Sparse Core Ops, SparseCore 0:
  16.2 146.0 all-gather.2
  423.1 157.5 reduce-scatter.2
  589.2 81.7 reduce-scatter.4
